TPU v7x, 32 devices: a whole 2x2x4 slice. The times are simulated.
32 devices in a mesh: grp: 2 (over x), dom: 16 (over z, y, core).
Axes of the slice: x: 2, y: 2, z: 4, core: 2. Of those that a mesh axis runs over, the one named last changes fastest.
Arguments:
- e_field: float32 [131072], P(('grp', 'dom')), may hold values from -6 to 6
- b_field: float32 [229376], P(('grp', 'dom')), may hold values from -6 to 6
- face_edges: int32 [3, 229376], P(None, ('grp', 'dom')), may hold values from 0 to 5119
- face_signs: int32 [3, 229376], P(None, ('grp', 'dom')), may hold values from -1 to 1, as said below
- send_prev: int32 [16384], P(('grp', 'dom')), may hold values from 0 to 4095
- send_next: int32 [16384], P(('grp', 'dom')), may hold values from 0 to 4095
- eps_inv: float32 [131072], P(('grp', 'dom')), may hold values from 0.5 to 2
- mu_inv: float32 [229376], P(('grp', 'dom')), may hold values from 0.5 to 2
- huy_face: int32 [4096], P(('grp', 'dom')), may hold values from 0 to 7167
- huy_edge: int32 [4096], P(('grp', 'dom')), may hold values from 0 to 4095
- huy_live: int32 [4096], P(('grp', 'dom')), may hold values from 0 to 1, as said below
- huy_geom: float32 [9, 4096], P(None, ('grp', 'dom')), may hold values from -4 to 4
- huy_acc: float32 [16, 4096], P(None, ('grp', 'dom')), may hold values from -6 to 6
- wavenum: float32 [4], replicated, may hold values from 1 to 4
- angles: float32 [2, 4096], P(None, 'grp'), may hold values from -3.140625 to 3.140625
Outputs:
- e_next: float32 [131072], P(('grp', 'dom'))
- b_next: float32 [229376], P(('grp', 'dom'))
- power: float32 [4, 4096], P(None, 'grp')
Inputs may be any that keep to these rules, and one draw needn't show every extreme that they name: `face_signs`: each entry is -1 or 1. `huy_live`: within each part the live slots come first, and in some part all 128 slots are live. `face_edges`: slots of the part's extended edge values: own edges, then the halo from part p-1, then that from part p+1.
All inputs are finite; a program needn't handle non-finite values.
Results may differ from a plain program's by a relative error of at most 0.0031.
Values sent between devices are 32-bit elements; how exact they have to be, the bound alone decides.
No kernel may reach another device: no remote copies, remote signals or barrier semaphores. Data moves between devices by JAX's collectives and lax.ppermute only.
A program may use at most 64 MiB of HBM per device.

v0:
```python
import jax
import jax.numpy as jnp
from jax import lax
from jax.sharding import PartitionSpec as P

STEPS = 2
FREQ = 4


time_step = 0.25


def from_behind(shard, axis, by):
    peers = lax.axis_size(axis)
    pairs = [(i, i + by) for i in range(peers) if 0 <= i + by < peers]
    return lax.ppermute(shard, axis, pairs)


def cross_rows(left, right):
    return jnp.stack(
        [
            left[1] * right[2] - left[2] * right[1],
            left[2] * right[0] - left[0] * right[2],
            left[0] * right[1] - left[1] * right[0],
        ]
    )


def unit_dirs(angles):
    polar = angles[0]
    azimuth = angles[1]
    return jnp.stack(
        [jnp.sin(polar) * jnp.cos(azimuth), jnp.sin(polar) * jnp.sin(azimuth), jnp.cos(polar)]
    )


def make_currents(acc_live, geometry):
    normal = geometry[0:3]
    tangent = geometry[3:6]
    blocks = []
    for freq_index in range(FREQ):
        offset = 2 * FREQ
        blocks.append(
            jnp.concatenate(
                [
                    normal * acc_live[2 * freq_index],
                    normal * acc_live[2 * freq_index + 1],
                    tangent * acc_live[offset + 2 * freq_index],
                    tangent * acc_live[offset + 2 * freq_index + 1],
                ],
                0,
            )
        )
    return jnp.stack(blocks).astype(jnp.bfloat16)


def radiate(currents, centres, dirs, wavenum):
    proj = (
        centres[0][:, None] * dirs[0][None, :]
        + centres[1][:, None] * dirs[1][None, :]
        + centres[2][:, None] * dirs[2][None, :]
    )
    rows = []
    for freq_index in range(FREQ):
        theta = wavenum[freq_index] * proj
        cosines = jnp.cos(theta).astype(jnp.bfloat16)
        sines = jnp.sin(theta).astype(jnp.bfloat16)
        p_sum = jnp.dot(currents[freq_index], cosines, preferred_element_type=jnp.float32)
        q_sum = jnp.dot(currents[freq_index], sines, preferred_element_type=jnp.float32)
        rows.append(
            jnp.concatenate(
                [
                    p_sum[0:3] - q_sum[3:6],
                    q_sum[0:3] + p_sum[3:6],
                    p_sum[6:9] - q_sum[9:12],
                    q_sum[6:9] + p_sum[9:12],
                ],
                0,
            )
        )
    return jnp.concatenate(rows, 0)


def intensity(field, dirs, scale):
    rows = []
    for freq_index in range(FREQ):
        base = 12 * freq_index
        real_part = cross_rows(dirs, cross_rows(dirs, field[base : base + 3])) - cross_rows(
            dirs, field[base + 6 : base + 9]
        )
        imag_part = cross_rows(dirs, cross_rows(dirs, field[base + 3 : base + 6])) - cross_rows(
            dirs, field[base + 9 : base + 12]
        )
        rows.append(jnp.sum(real_part * real_part + imag_part * imag_part, axis=0) * scale)
    return jnp.stack(rows)


def per_device(
    e_field,
    b_field,
    face_edges,
    face_signs,
    send_prev,
    send_next,
    eps_inv,
    mu_inv,
    huy_face,
    huy_edge,
    huy_live,
    huy_geom,
    huy_acc,
    wavenum,
    angles,
):
    edges_own = e_field.shape[0]
    halo_len = send_prev.shape[0]
    signs = face_signs.astype(jnp.float32)
    flat_index = face_edges.reshape(-1)
    back_index = jnp.concatenate([send_next, send_prev])
    edge_vals = e_field
    face_vals = b_field
    acc = huy_acc
    for step_index in range(STEPS):
        to_next = edge_vals[send_next]
        to_prev = edge_vals[send_prev]
        from_prev = from_behind(to_next, ("grp", "dom"), 1)
        from_next = from_behind(to_prev, ("grp", "dom"), -1)
        extended = jnp.concatenate([edge_vals, from_prev, from_next])
        curl = signs[0] * extended[face_edges[0]]
        curl = curl + signs[1] * extended[face_edges[1]]
        curl = curl + signs[2] * extended[face_edges[2]]
        face_vals = face_vals - time_step * curl
        scaled = mu_inv * face_vals
        contrib = jax.ops.segment_sum(
            (signs * scaled[None, :]).reshape(-1), flat_index, num_segments=edges_own + 2 * halo_len
        )
        back_from_next = from_behind(contrib[edges_own : edges_own + halo_len], ("grp", "dom"), -1)
        back_from_prev = from_behind(contrib[edges_own + halo_len :], ("grp", "dom"), 1)
        total = contrib[:edges_own] + jax.ops.segment_sum(
            jnp.concatenate([back_from_next, back_from_prev]), back_index, num_segments=edges_own
        )
        edge_vals = edge_vals + time_step * eps_inv * total
        moment = (step_index + 1) * time_step
        coef = jnp.stack([jnp.cos(wavenum * moment), -jnp.sin(wavenum * moment)], 1).reshape(-1)
        acc = acc + jnp.concatenate(
            [
                coef[:, None] * face_vals[huy_face][None, :],
                coef[:, None] * edge_vals[huy_edge][None, :],
            ],
            0,
        )
    acc_live = acc * huy_live.astype(jnp.float32)[None, :]
    local_dirs = unit_dirs(angles)
    scale = 1.0 / (huy_acc.shape[1] * lax.axis_size(("grp", "dom")))
    all_angles = lax.all_gather(angles, "grp", axis=1, tiled=True)
    own_field = radiate(
        make_currents(acc_live, huy_geom), huy_geom[6:9], unit_dirs(all_angles), wavenum
    )
    field = lax.psum_scatter(own_field, "grp", scatter_dimension=1, tiled=True)
    total_field = lax.psum(field, "dom")
    power = intensity(total_field, local_dirs, scale)
    return (edge_vals, face_vals, power)


def solution(mesh):
    return jax.shard_map(
        per_device,
        mesh=mesh,
        in_specs=(
            P(("grp", "dom")),
            P(("grp", "dom")),
            P(None, ("grp", "dom")),
            P(None, ("grp", "dom")),
            P(("grp", "dom")),
            P(("grp", "dom")),
            P(("grp", "dom")),
            P(("grp", "dom")),
            P(("grp", "dom")),
            P(("grp", "dom")),
            P(("grp", "dom")),
            P(None, ("grp", "dom")),
            P(None, ("grp", "dom")),
            P(),
            P(None, "grp"),
        ),
        out_specs=(P(("grp", "dom")), P(("grp", "dom")), P(None, "grp")),
        check_vma=False,
    )
```

profile of v0, /device:TPU:0, one launch (start us, length us, event | category | flops | bytes accessed | tf_op | source)
XLA Modules:
  0.0 761.3 jit_solution(1907246883477973626)
XLA Ops:
  8.6 3.1 gather_fusion
  18.8 10.8 %all_gather.3 = f32[2,4096]{1,0:T(2,128)S(1)} all-gather(f32[2,2048]{1,0:T(2,128)S(1)} %copy-done.5), channel_id=1, replica_groups=mesh['grp'=2,'dom'=16] {'grp'}, dimensions={1}, use_global_device_ids=true | all-gather | bytes 49152 | tf_op jit(solution)/shard_map/all_gather | solution.py:155
  31.6 39.9 %gather_fusion.3 = f32[7168]{0:T(1024)S(1)} fusion(f32[5120]{0:T(1024)S(1)} %constant_dynamic-update-slice_fusion, s32[7168]{0:T(1024)S(1)} %broadcast_clamp_fusion.1), kind=kCustom, calls=%fused_computation.3 | custom fusion | bytes 86016 | tf_op jit(solution)/shard_map/gather | solution.py:130
  71.6 39.9 %gather_fusion.4 = f32[7168]{0:T(1024)S(1)} fusion(f32[5120]{0:T(1024)S(1)} %constant_dynamic-update-slice_fusion, s32[7168]{0:T(1024)S(1)} %broadcast_clamp_fusion), kind=kCustom, calls=%fused_computation.4 | custom fusion | bytes 86016 | tf_op jit(solution)/shard_map/gather | solution.py:131
  111.5 39.9 %gather_fusion.2 = f32[7168]{0:T(1024)S(1)} fusion(f32[5120]{0:T(1024)S(1)} %constant_dynamic-update-slice_fusion, s32[7168]{0:T(1024)S(1)} %broadcast_clamp_fusion.2), kind=kCustom, calls=%fused_computation.2 | custom fusion | bytes 86016 | tf_op jit(solution)/shard_map/gather | solution.py:129
  151.6 112.4 %scatter_custom_fusion = f32[5120]{0:T(1024)S(1)} fusion(s32[21504]{0:T(1024)S(1)} %reshape.264, f32[21504]{0:T(1024)S(1)} %reshape.266, f32[]{:T(128)} %constant.9.clone.1), kind=kCustom, calls=%fused_computation.97 | custom fusion | flops 21504 | bytes 20484 | tf_op jit(solution)/shard_map/scatter-add | solution.py:134
  269.1 6.1 scatter_fusion
  288.2 39.9 %gather_fusion.9 = f32[7168]{0:T(1024)S(1)} fusion(f32[5120]{0:T(1024)S(1)} %pad_maximum_fusion.1, s32[7168]{0:T(1024)S(1)} %broadcast_clamp_fusion), kind=kCustom, calls=%fused_computation.9 | custom fusion | bytes 86016 | tf_op jit(solution)/shard_map/gather | solution.py:131
  328.1 39.9 %gather_fusion.8 = f32[7168]{0:T(1024)S(1)} fusion(f32[5120]{0:T(1024)S(1)} %pad_maximum_fusion.1, s32[7168]{0:T(1024)S(1)} %broadcast_clamp_fusion.1), kind=kCustom, calls=%fused_computation.8 | custom fusion | bytes 86016 | tf_op jit(solution)/shard_map/gather | solution.py:130
  368.1 39.9 %gather_fusion.7 = f32[7168]{0:T(1024)S(1)} fusion(f32[5120]{0:T(1024)S(1)} %pad_maximum_fusion.1, s32[7168]{0:T(1024)S(1)} %broadcast_clamp_fusion.2), kind=kCustom, calls=%fused_computation.7 | custom fusion | bytes 86016 | tf_op jit(solution)/shard_map/gather | solution.py:129
  408.1 112.4 %scatter_custom_fusion.2 = f32[5120]{0:T(1024)S(1)} fusion(s32[21504]{0:T(1024)S(1)} %reshape.264, f32[21504]{0:T(1024)S(1)} %reshape.282, f32[]{:T(128)} %constant.9.clone.1), kind=kCustom, calls=%fused_computation.95 | custom fusion | flops 21504 | bytes 20484 | tf_op jit(solution)/shard_map/scatter-add | solution.py:134
  521.9 4.9 collective-permute-start.7
  528.0 6.1 scatter_fusion.1
  535.6 7.9 %fusion.11 = f32[12,4096]{1,0:T(8,128)S(1)} fusion(f32[]{:T(128)} %bitcast.38, f32[4096]{0:T(1024)S(1)} %bitcast.98, f32[128]{0:T(128)S(1)} %get-tuple-element.121, f32[4096]{0:T(1024)S(1)} %bitcast.90, f32[128]{0:T(128)S(1)} %get-tuple-element.122, f32[4096]{0:T(1024)S(1)} %bitcast.82, f32[128]{0:T(128)S(1)} %get-tuple-element.120, ...), kind=kOutput, calls=%fused_computation.38 | convolution fusion | flops 16265216 | bytes 250372 | tf_op jit(solution)/shard_map/dot_general | solution.py:69
  543.5 8.1 %fusion.10 = f32[12,4096]{1,0:T(8,128)S(1)} fusion(f32[]{:T(128)} %bitcast.38, f32[4096]{0:T(1024)S(1)} %bitcast.99, f32[128]{0:T(128)S(1)} %get-tuple-element.121, f32[4096]{0:T(1024)S(1)} %bitcast.91, f32[128]{0:T(128)S(1)} %get-tuple-element.122, f32[4096]{0:T(1024)S(1)} %bitcast.83, f32[128]{0:T(128)S(1)} %get-tuple-element.120, ...), kind=kOutput, calls=%fused_computation.37 | convolution fusion | flops 16265216 | bytes 250372 | tf_op jit(solution)/shard_map/dot_general | solution.py:68
  551.6 7.9 %fusion.7 = f32[12,4096]{1,0:T(8,128)S(1)} fusion(f32[]{:T(128)} %bitcast.28, f32[4096]{0:T(1024)S(1)} %bitcast.100, f32[128]{0:T(128)S(1)} %get-tuple-element.121, f32[4096]{0:T(1024)S(1)} %bitcast.92, f32[128]{0:T(128)S(1)} %get-tuple-element.122, f32[4096]{0:T(1024)S(1)} %bitcast.84, f32[128]{0:T(128)S(1)} %get-tuple-element.120, ...), kind=kOutput, calls=%fused_computation.34 | convolution fusion | flops 16265216 | bytes 250372 | tf_op jit(solution)/shard_map/dot_general | solution.py:69
  559.5 8.2 %fusion.6 = f32[12,4096]{1,0:T(8,128)S(1)} fusion(f32[]{:T(128)} %bitcast.28, f32[4096]{0:T(1024)S(1)} %bitcast.101, f32[128]{0:T(128)S(1)} %get-tuple-element.121, f32[4096]{0:T(1024)S(1)} %bitcast.93, f32[128]{0:T(128)S(1)} %get-tuple-element.122, f32[4096]{0:T(1024)S(1)} %bitcast.85, f32[128]{0:T(128)S(1)} %get-tuple-element.120, ...), kind=kOutput, calls=%fused_computation.33 | convolution fusion | flops 16265216 | bytes 250372 | tf_op jit(solution)/shard_map/dot_general | solution.py:68
  567.7 8.1 %fusion.9 = f32[12,4096]{1,0:T(8,128)S(1)} fusion(f32[]{:T(128)} %bitcast.33, f32[4096]{0:T(1024)S(1)} %bitcast.102, f32[128]{0:T(128)S(1)} %get-tuple-element.121, f32[4096]{0:T(1024)S(1)} %bitcast.94, f32[128]{0:T(128)S(1)} %get-tuple-element.122, f32[4096]{0:T(1024)S(1)} %bitcast.86, f32[128]{0:T(128)S(1)} %get-tuple-element.120, ...), kind=kOutput, calls=%fused_computation.36 | convolution fusion | flops 16265216 | bytes 250372 | tf_op jit(solution)/shard_map/dot_general | solution.py:69
  575.8 7.9 %fusion.8 = f32[12,4096]{1,0:T(8,128)S(1)} fusion(f32[]{:T(128)} %bitcast.33, f32[4096]{0:T(1024)S(1)} %bitcast.103, f32[128]{0:T(128)S(1)} %get-tuple-element.121, f32[4096]{0:T(1024)S(1)} %bitcast.95, f32[128]{0:T(128)S(1)} %get-tuple-element.122, f32[4096]{0:T(1024)S(1)} %bitcast.87, f32[128]{0:T(128)S(1)} %get-tuple-element.120, ...), kind=kOutput, calls=%fused_computation.35 | convolution fusion | flops 16265216 | bytes 250372 | tf_op jit(solution)/shard_map/dot_general | solution.py:68
  583.7 8.2 %fusion.5 = f32[12,4096]{1,0:T(8,128)S(1)} fusion(f32[4096]{0:T(1024)S(1)} %bitcast.104, f32[128]{0:T(128)S(1)} %get-tuple-element.121, f32[4096]{0:T(1024)S(1)} %bitcast.96, f32[128]{0:T(128)S(1)} %get-tuple-element.122, f32[4096]{0:T(1024)S(1)} %bitcast.88, f32[128]{0:T(128)S(1)} %get-tuple-element.120, f32[]{:T(128)} %bitcast.17, ...), kind=kOutput, calls=%fused_computation.32 | convolution fusion | flops 16265216 | bytes 250372 | tf_op jit(solution)/shard_map/dot_general | solution.py:69
  591.9 7.9 %fusion.4 = f32[12,4096]{1,0:T(8,128)S(1)} fusion(f32[4096]{0:T(1024)S(1)} %bitcast.105, f32[128]{0:T(128)S(1)} %get-tuple-element.121, f32[4096]{0:T(1024)S(1)} %bitcast.97, f32[128]{0:T(128)S(1)} %get-tuple-element.122, f32[4096]{0:T(1024)S(1)} %bitcast.89, f32[128]{0:T(128)S(1)} %get-tuple-element.120, f32[]{:T(128)} %bitcast.17, ...), kind=kOutput, calls=%fused_computation.31 | convolution fusion | flops 16265216 | bytes 250372 | tf_op jit(solution)/shard_map/dot_general | solution.py:68
  600.4 14.5 %concatenate.51 = f32[48,4096]{1,0:T(8,128)} concatenate(f32[3,4096]{1,0:T(4,128)S(1)} %get-tuple-element.26, f32[3,4096]{1,0:T(4,128)S(1)} %get-tuple-element.25, f32[3,4096]{1,0:T(4,128)S(1)} %get-tuple-element.24, f32[3,4096]{1,0:T(4,128)S(1)} %get-tuple-element.23, f32[3,4096]{1,0:T(4,128)S(1)} %get-tuple-element.22, f32[3,4096]{1,0:T(4,128)S(1)} %get-tuple-element.21, ...), dimensions={0} | concatenate | bytes 1572864 | tf_op jit(solution)/shard_map/concatenate | solution.py:81
  614.9 32.7 %reduce-scatter.2.cloned.1.call-done = f32[48,2048]{1,0:T(8,128)} async-done(((f32[48,4096]{1,0:T(8,128)}), f32[48,2048]{1,0:T(8,128)}) %reduce-scatter.2.cloned.1.call-update) | async-done | bytes 393232 | tf_op jit(solution)/shard_map/reduce_scatter | solution.py:159
  647.6 94.1 %all-reduce.2.cloned.1.call-done = f32[48,2048]{1,0:T(8,128)} async-done(((f32[48,2048]{1,0:T(8,128)}), f32[48,2048]{1,0:T(8,128)}) %all-reduce.2.cloned.1.call-update) | async-done | bytes 393232 | tf_op jit(solution)/shard_map/psum | solution.py:160
  (130 shorter events, 45.3 us)
Async XLA Ops:
  7.2 640.4 %reduce-scatter.2.cloned.1.call-start = ((), (), s32[]{:S(2)}) async-start(), calls=%async_computation.1 | async-start | bytes 1179648 | tf_op jit(solution)/shard_map/reduce_scatter | solution.py:159
  11.8 19.8 %collective-permute-start = (f32[512]{0:T(512)S(1)}, f32[512]{0:T(512)S(1)}, u32[]{:S(2)}, u32[]{:S(2)}) collective-permute-start(f32[512]{0:T(512)S(1)} %gather_fusion), channel_id=1, source_target_pairs={{0,1},{1,2},{2,3},{3,4},{4,5},{5,6},{6,7},{7,8},{8,9},{9,10},{10,1... | collective-permute-start | bytes 6152 | tf_op jit(solution)/shard_map/ppermute | solution.py:16
  14.2 4.6 copy-start.14
  14.2 4.6 copy-start.11
  14.2 4.6 copy-start.10
  14.2 4.6 copy-start.5
  14.2 16.4 %copy-start.6 = (s32[3,7168]{1,0:T(4,128)S(1)}, s32[3,7168]{1,0:T(4,128)}, u32[]{:S(2)}) copy-start(s32[3,7168]{1,0:T(4,128)} %param.17) | copy-start | bytes 258052
  14.2 16.6 %copy-start.4 = (s32[3,7168]{1,0:T(4,128)S(1)}, s32[3,7168]{1,0:T(4,128)}, u32[]{:S(2)}) copy-start(s32[3,7168]{1,0:T(4,128)} %param.18) | copy-start | bytes 258052
  17.4 14.2 %collective-permute-start.1 = (f32[512]{0:T(512)S(1)}, f32[512]{0:T(512)S(1)}, u32[]{:S(2)}, u32[]{:S(2)}) collective-permute-start(f32[512]{0:T(512)S(1)} %gather_fusion.1), channel_id=1, source_target_pairs={{1,0},{2,1},{3,2},{4,3},{5,4},{6,5},{7,6},{8,7},{9,8},{10,9},{11,1... | collective-permute-start | bytes 6152 | tf_op jit(solution)/shard_map/ppermute | solution.py:16
  111.5 39.9 %copy-start.7 = (f32[7168]{0:T(1024)S(1)}, f32[7168]{0:T(1024)}, u32[]{:S(2)}) copy-start(f32[7168]{0:T(1024)} %param.22) | copy-start | bytes 86020
  111.5 39.9 %copy-start.9 = (f32[7168]{0:T(1024)S(1)}, f32[7168]{0:T(1024)}, u32[]{:S(2)}) copy-start(f32[7168]{0:T(1024)} %param.16) | copy-start | bytes 86020
  264.0 4.4 collective-permute-start.2
  265.3 3.8 collective-permute-start.3
  269.1 6.1 copy-start.8
  278.4 6.7 copy-start.15
  281.6 6.3 collective-permute-start.4
  283.8 4.4 collective-permute-start.5
  408.0 126.1 %copy-start.2 = (f32[7168]{0:T(1024)}, f32[7168]{0:T(1024)S(1)}, u32[]{:S(2)}) copy-start(f32[7168]{0:T(1024)S(1)} %get-tuple-element.8) | copy-start | bytes 86020
  520.6 7.4 collective-permute-start.6
  521.9 6.1 collective-permute-start.7
  528.0 7.5 copy-start.12
  534.1 9.4 %copy-start.1 = (f32[4096]{0:T(1024)}, f32[4096]{0:T(1024)S(1)}, u32[]{:S(2)}) copy-start(f32[4096]{0:T(1024)S(1)} %multiply_add_fusion.1) | copy-start | bytes 49156
  614.9 126.8 %all-reduce.2.cloned.1.call-start = ((), (), s32[]{:S(2)}) async-start(), calls=%async_computation.2 | async-start | bytes 786432 | tf_op jit(solution)/shard_map/psum | solution.py:160
  741.7 10.0 %copy-start.3 = (f32[48,2048]{1,0:T(8,128)S(1)}, f32[48,2048]{1,0:T(8,128)}, u32[]{:S(2)}) copy-start(f32[48,2048]{1,0:T(8,128)} %all-reduce.2.cloned.1.call-done) | copy-start | bytes 1179652
  (2 other events, 6.0 us)
Sparse Core Ops, SparseCore 0:
  615.0 32.5 reduce-scatter.1
  651.3 90.3 all-reduce.1
where the time goes:
time: 771 us; the launch traced here: 761 us
  local copies, waits for them, and re-layouts  273 us (35%)
  other arithmetic  253 us (33%)
  waiting for transfers between devices  128 us (17%)
  matrix products  64.2 us (8%)
  starting transfers between devices  17.8 us (2%)
  between operations  15.3 us (2%)
  blocking collectives  10.8 us (1%)
    scatter-add x2, other arithmetic, per_device(): jax.ops.segment_sum((signs * scaled[None, :]).reshape(-1), flat_index, nu...  225 us
    psum x1, waiting for transfers between devices, per_device(): total_field = lax.psum(field, 'dom')  94.1 us
    gather x2, local copies, waits for them, and re-layouts, per_device(): curl = signs[0] * extended[face_edges[0]]  79.8 us
    gather x2, local copies, waits for them, and re-layouts, per_device(): curl = curl + signs[1] * extended[face_edges[1]]  79.8 us
    gather x2, local copies, waits for them, and re-layouts, per_device(): curl = curl + signs[2] * extended[face_edges[2]]  79.8 us
    reduce_scatter x1, waiting for transfers between devices, per_device(): field = lax.psum_scatter(own_field, 'grp', scatter_dimension=1, tiled=True)  32.7 us
    dot_general x4, matrix products, radiate(): jnp.dot(currents[freq_index], sines, preferred_element_type=jnp.float32)  32.1 us
    dot_general x4, matrix products, radiate(): jnp.dot(currents[freq_index], cosines, preferred_element_type=jnp.float32)  32.1 us
  transfers between devices with their start and end apart: 10, of which 4 were waited for; matrix products, arithmetic and copies ran while one was open for 1% of the time, Pallas kernels for 0%

commit v1 on v0

v1 whole, which is shorter than its diff:
```python
import functools
import math

import jax
import jax.numpy as jnp
from jax import lax
from jax.experimental import pallas as pl
from jax.experimental.pallas import tpu as pltpu
from jax.sharding import PartitionSpec as P

STEPS = 2
FREQ = 4
LANES = 128
AXES = ("grp", "dom")

time_step = 0.25

SIN_TERMS = (
    6.28318281855342,
    -41.34142139883725,
    81.59618387543962,
    -76.58010053965613,
    41.20539488778604,
    -12.271262339293433,
)
COS_TERMS = (
    0.999999221631531,
    -19.738982521135544,
    64.92872672354663,
    -85.27239794967592,
    58.794042407527144,
    -21.076787389280092,
)

PARAMS = pltpu.CompilerParams(vmem_limit_bytes=48 * 1024 * 1024)


def lookup(table_ref, rows, index):
    asked = index.shape[0]
    if asked < 8:
        index = jnp.broadcast_to(index, (8, LANES)) if asked == 1 else jnp.concatenate([index] * (8 // asked), 0)
    row_of = lax.shift_right_logical(index, 7)
    lane_of = lax.bitwise_and(index, LANES - 1)
    found = jnp.zeros(index.shape, jnp.float32)
    for row in range(rows):
        line = jnp.broadcast_to(table_ref[row : row + 1, :], index.shape)
        found = jnp.where(row_of == row, jnp.take_along_axis(line, lane_of, axis=1), found)
    return found[:asked]


def spread(index, values, rows):
    row_of = lax.shift_right_logical(index, 7)
    lane_of = lax.bitwise_and(index, LANES - 1)
    high = values.astype(jnp.bfloat16).astype(jnp.float32)
    low = values - high
    row_iota = lax.broadcasted_iota(jnp.int32, (rows, LANES), 0)
    lane_iota = lax.broadcasted_iota(jnp.int32, (LANES, LANES), 0)
    lefts = []
    rights = []
    for at in range(index.shape[0]):
        hit = row_iota == row_of[at : at + 1, :]
        left = [
            jnp.where(hit, high[at : at + 1, :], 0.0),
            jnp.where(hit, low[at : at + 1, :], 0.0),
        ]
        lefts.append(jnp.concatenate(left, 0).astype(jnp.bfloat16))
        rights.append(
            jnp.where(lane_iota == lane_of[at : at + 1, :], 1.0, 0.0).astype(jnp.bfloat16)
        )
    both = lax.dot_general(
        jnp.concatenate(lefts, 1),
        jnp.concatenate(rights, 1),
        (((1,), (1,)), ((), ())),
        preferred_element_type=jnp.float32,
    )
    return both[:rows] + both[rows:]


def gather_sends(even, table_ref, rows, send_next, send_prev, send_a_ref, send_b_ref):
    found = lookup(table_ref, rows, jnp.concatenate([send_next, send_prev], 0))
    half = send_next.shape[0]
    send_a_ref[...] = jnp.where(even, found[:half], found[half:])
    send_b_ref[...] = jnp.where(even, found[half:], found[:half])


def first_sends_kernel(even_ref, e_ref, send_next_ref, send_prev_ref, send_a_ref, send_b_ref):
    gather_sends(
        even_ref[0] == 1,
        e_ref,
        e_ref.shape[0],
        send_next_ref[...],
        send_prev_ref[...],
        send_a_ref,
        send_b_ref,
    )


def faces_kernel(
    even_ref,
    e_ref,
    got_a_ref,
    got_b_ref,
    edges_ref,
    signs_ref,
    b_ref,
    mu_ref,
    huy_face_ref,
    b_out_ref,
    own_ref,
    send_a_ref,
    send_b_ref,
    sample_ref,
    table_ref,
    index_ref,
    value_ref,
):
    even = even_ref[0] == 1
    own_rows = e_ref.shape[0]
    halo_rows = got_a_ref.shape[0]
    face_rows = b_ref.shape[0]
    rows = own_rows + 2 * halo_rows
    got_a = got_a_ref[...]
    got_b = got_b_ref[...]
    table_ref[0:own_rows, :] = e_ref[...]
    table_ref[own_rows : own_rows + halo_rows, :] = jnp.where(even, got_b, got_a)
    table_ref[own_rows + halo_rows : rows, :] = jnp.where(even, got_a, got_b)
    for k in range(3):
        for at in range(face_rows):
            lanes = slice(at * LANES, (at + 1) * LANES)
            to = k * face_rows + at
            index_ref[to : to + 1, :] = edges_ref[k : k + 1, lanes]
            value_ref[to : to + 1, :] = signs_ref[k : k + 1, lanes].astype(jnp.float32)
    curl = None
    for k in range(3):
        span = slice(k * face_rows, (k + 1) * face_rows)
        term = value_ref[span, :] * lookup(table_ref, rows, index_ref[span, :])
        curl = term if curl is None else curl + term
    b_new = b_ref[...] - time_step * curl
    b_out_ref[...] = b_new
    scaled = mu_ref[...] * b_new
    for k in range(3):
        span = slice(k * face_rows, (k + 1) * face_rows)
        value_ref[span, :] = value_ref[span, :] * scaled

    def body(at, total):
        span = pl.ds(pl.multiple_of(at * 8, 8), 8)
        return total + spread(index_ref[span, :], value_ref[span, :], rows)

    total = lax.fori_loop(
        0, 3 * face_rows // 8, body, jnp.zeros((rows, LANES), jnp.float32)
    )
    own_ref[...] = total[:own_rows]
    to_prev = total[own_rows : own_rows + halo_rows]
    to_next = total[own_rows + halo_rows :]
    send_a_ref[...] = jnp.where(even, to_next, to_prev)
    send_b_ref[...] = jnp.where(even, to_prev, to_next)
    sample_ref[...] = lookup(b_out_ref, face_rows, huy_face_ref[...])


def edges_update(even, e_ref, eps_ref, own_ref, got_a_ref, got_b_ref, send_next, send_prev, e_out_ref):
    rows = e_ref.shape[0]
    got_a = got_a_ref[...]
    got_b = got_b_ref[...]
    from_next = jnp.where(even, got_a, got_b)
    from_prev = jnp.where(even, got_b, got_a)
    back = spread(
        jnp.concatenate([send_next, send_prev], 0),
        jnp.concatenate([from_next, from_prev], 0),
        rows,
    )
    e_out_ref[...] = e_ref[...] + time_step * eps_ref[...] * (own_ref[...] + back)


def edges_kernel(
    even_ref,
    e_ref,
    eps_ref,
    own_ref,
    got_a_ref,
    got_b_ref,
    send_next_ref,
    send_prev_ref,
    huy_edge_ref,
    e_out_ref,
    send_a_ref,
    send_b_ref,
    sample_ref,
):
    even = even_ref[0] == 1
    rows = e_ref.shape[0]
    send_next = send_next_ref[...]
    send_prev = send_prev_ref[...]
    edges_update(
        even, e_ref, eps_ref, own_ref, got_a_ref, got_b_ref, send_next, send_prev, e_out_ref
    )
    gather_sends(even, e_out_ref, rows, send_next, send_prev, send_a_ref, send_b_ref)
    sample_ref[...] = lookup(e_out_ref, rows, huy_edge_ref[...])


def last_edges_kernel(
    even_ref,
    wave_ref,
    e_ref,
    eps_ref,
    own_ref,
    got_a_ref,
    got_b_ref,
    send_next_ref,
    send_prev_ref,
    huy_edge_ref,
    b_first_ref,
    b_last_ref,
    e_first_ref,
    live_ref,
    geom_ref,
    acc_ref,
    e_out_ref,
    share_ref,
):
    even = even_ref[0] == 1
    rows = e_ref.shape[0]
    edges_update(
        even,
        e_ref,
        eps_ref,
        own_ref,
        got_a_ref,
        got_b_ref,
        send_next_ref[...],
        send_prev_ref[...],
        e_out_ref,
    )
    e_last = lookup(e_out_ref, rows, huy_edge_ref[...])
    live = live_ref[...].astype(jnp.float32)
    geom = geom_ref[...]
    normal = geom[0:3]
    tangent = geom[3:6]
    samples = ((b_first_ref[...], b_last_ref[...]), (e_first_ref[...], e_last))
    blocks = []
    for q in range(FREQ):
        pieces = []
        for kind, shape in ((0, normal), (1, tangent)):
            for part in range(2):
                row = 2 * FREQ * kind + 2 * q + part
                value = acc_ref[row : row + 1, :]
                for step in range(STEPS):
                    value = value + wave_ref[step, 2 * q + part] * samples[kind][step]
                pieces.append(shape * (value * live))
        pieces.append(geom[6:9])
        pieces.append(jnp.zeros((1, LANES), jnp.float32))
        blocks.append(jnp.concatenate(pieces, 0))
    for q in range(FREQ):
        share_ref[q] = blocks[q]


def far_kernel(wave_ref, share_ref, angles_ref, power_ref, scale):
    sources = share_ref.shape[0]
    width = angles_ref.shape[1]
    polar = angles_ref[0:1, :]
    azimuth = angles_ref[1:2, :]
    dirs = [
        jnp.sin(polar) * jnp.cos(azimuth),
        jnp.sin(polar) * jnp.sin(azimuth),
        jnp.cos(polar),
    ]
    turns = wave_ref[0]
    scaled = jnp.concatenate(
        [jnp.zeros((4, width), jnp.float32)]
        + [one * turns for one in dirs]
        + [jnp.zeros((1, width), jnp.float32)],
        0,
    )
    t1 = scaled.astype(jnp.bfloat16).astype(jnp.float32)
    t2 = (scaled - t1).astype(jnp.bfloat16).astype(jnp.float32)
    t3 = scaled - t1 - t2
    right = jnp.concatenate([t1, t2, t3, t1, t2, t1], 0).astype(jnp.bfloat16)
    group = 2

    def body(at, sums):
        p_sum, q_sum = sums
        lefts = []
        currents = []
        for one in range(group):
            piece = share_ref[at * group + one]
            centre = piece[8:16]
            u1 = centre.astype(jnp.bfloat16).astype(jnp.float32)
            u2 = (centre - u1).astype(jnp.bfloat16).astype(jnp.float32)
            u3 = centre - u1 - u2
            lefts.append(jnp.concatenate([u1, u1, u1, u2, u2, u3], 0).astype(jnp.bfloat16))
            currents.append(piece.astype(jnp.bfloat16))
        left = jnp.concatenate(lefts, 1)
        current = jnp.concatenate(currents, 1)
        theta = lax.dot_general(
            left, right, (((0,), (0,)), ((), ())), preferred_element_type=jnp.float32
        )
        f = theta - jnp.round(theta)
        s = f * f
        sine = SIN_TERMS[-1] * s + SIN_TERMS[-2]
        for term in SIN_TERMS[-3::-1]:
            sine = sine * s + term
        sine = sine * f
        cosine = COS_TERMS[-1] * s + COS_TERMS[-2]
        for term in COS_TERMS[-3::-1]:
            cosine = cosine * s + term
        p_sum = p_sum + jnp.dot(
            current, cosine.astype(jnp.bfloat16), preferred_element_type=jnp.float32
        )
        q_sum = q_sum + jnp.dot(
            current, sine.astype(jnp.bfloat16), preferred_element_type=jnp.float32
        )
        return p_sum, q_sum

    zeros = jnp.zeros((16, width), jnp.float32)
    p_sum, q_sum = lax.fori_loop(0, sources // group, body, (zeros, zeros))

    def row(table, at):
        return table[at : at + 1, :]

    def cross(left, right):
        return [
            left[1] * right[2] - left[2] * right[1],
            left[2] * right[0] - left[0] * right[2],
            left[0] * right[1] - left[1] * right[0],
        ]

    n_real = [row(p_sum, i) - row(q_sum, 3 + i) for i in range(3)]
    n_imag = [row(q_sum, i) + row(p_sum, 3 + i) for i in range(3)]
    l_real = [row(p_sum, 6 + i) - row(q_sum, 9 + i) for i in range(3)]
    l_imag = [row(q_sum, 6 + i) + row(p_sum, 9 + i) for i in range(3)]
    power = jnp.zeros((1, width), jnp.float32)
    for n_part, l_part in ((n_real, l_real), (n_imag, l_imag)):
        outer = cross(dirs, cross(dirs, n_part))
        inner = cross(dirs, l_part)
        for i in range(3):
            gap = outer[i] - inner[i]
            power = power + gap * gap
    power_ref[...] = power * scale


VMEM_SPEC = pl.BlockSpec(memory_space=pltpu.VMEM)
SMEM_SPEC = pl.BlockSpec(memory_space=pltpu.SMEM)


def call(kernel, scalars, arrays, outs, scratch=(), name=None):
    return pl.pallas_call(
        kernel,
        out_shape=[jax.ShapeDtypeStruct(shape, jnp.float32) for shape in outs],
        in_specs=[SMEM_SPEC] * len(scalars) + [VMEM_SPEC] * len(arrays),
        out_specs=[VMEM_SPEC] * len(outs),
        scratch_shapes=list(scratch),
        compiler_params=PARAMS,
        name=name,
    )(*scalars, *arrays)


def per_device(
    e_field,
    b_field,
    face_edges,
    face_signs,
    send_prev,
    send_next,
    eps_inv,
    mu_inv,
    huy_face,
    huy_edge,
    huy_live,
    huy_geom,
    huy_acc,
    wavenum,
    angles,
):
    grp_size = lax.axis_size("grp")
    dom_size = lax.axis_size("dom")
    parts = grp_size * dom_size
    me = lax.axis_index(AXES)
    even = (1 - me % 2).astype(jnp.int32).reshape(1)
    pairs_a = [(i, i ^ 1) for i in range(parts)]
    pairs_b = [(i, i + 1) for i in range(1, parts - 1, 2)]
    pairs_b = pairs_b + [(j, i) for i, j in pairs_b]

    def swap(send_a, send_b):
        return lax.ppermute(send_a, AXES, pairs_a), lax.ppermute(send_b, AXES, pairs_b)

    def table(array):
        return array.reshape(-1, LANES)

    e_table, b_table = table(e_field), table(b_field)
    eps_table, mu_table = table(eps_inv), table(mu_inv)
    next_table, prev_table = table(send_next), table(send_prev)
    face_table, edge_table, live_table = table(huy_face), table(huy_edge), table(huy_live)
    own = e_table.shape
    halo = next_table.shape
    faces = b_table.shape
    sample = face_table.shape
    rows = own[0] + 2 * halo[0]

    moments = time_step * jnp.arange(1, STEPS + 1, dtype=jnp.float32)
    phase = moments[:, None] * wavenum[None, :]
    coef = jnp.stack([jnp.cos(phase), -jnp.sin(phase)], 2).reshape(STEPS, 2 * FREQ)

    send = call(
        first_sends_kernel, [even], [e_table, next_table, prev_table], [halo, halo], name="first_sends"
    )
    b_samples = []
    e_samples = []
    for step in range(STEPS):
        got = swap(*send)
        b_table, own_sum, back_a, back_b, b_sample = call(
            faces_kernel,
            [even],
            [e_table, *got, face_edges, face_signs, b_table, mu_table, face_table],
            [faces, own, halo, halo, sample],
            [
                pltpu.VMEM((rows, LANES), jnp.float32),
                pltpu.VMEM((3 * faces[0], LANES), jnp.int32),
                pltpu.VMEM((3 * faces[0], LANES), jnp.float32),
            ],
            name="faces",
        )
        b_samples.append(b_sample)
        got = swap(back_a, back_b)
        common = [e_table, eps_table, own_sum, *got, next_table, prev_table, edge_table]
        if step < STEPS - 1:
            e_table, *send, e_sample = call(
                edges_kernel, [even], common, [own, halo, halo, sample], name="edges"
            )
            e_samples.append(e_sample)
        else:
            e_table, share = call(
                last_edges_kernel,
                [even, coef],
                common + [*b_samples, *e_samples, live_table, huy_geom, huy_acc],
                [own, (FREQ, 16, LANES)],
                name="last_edges",
            )
    blocks = dom_size // FREQ
    width = angles.shape[1] // blocks
    shares = jnp.broadcast_to(
        share[None, :, None], (grp_size, FREQ, blocks, 16, LANES)
    ).reshape(parts, 16, LANES)
    shares = lax.all_to_all(shares, AXES, 0, 0, tiled=True)
    place = lax.axis_index("dom")
    own_freq = place // blocks
    own_angles = lax.dynamic_slice_in_dim(angles, (place % blocks) * width, width, axis=1)
    turns = lax.dynamic_slice_in_dim(wavenum, own_freq, 1) * (0.5 / math.pi)
    scale = 1.0 / (LANES * parts)
    (power,) = call(
        functools.partial(far_kernel, scale=scale),
        [turns],
        [shares, own_angles],
        [(1, width)],
        name="far",
    )
    power = lax.all_to_all(
        jnp.broadcast_to(power, (dom_size, width)), "dom", 0, 0, tiled=True
    ).reshape(FREQ, blocks * width)
    return (e_table.reshape(-1), b_table.reshape(-1), power)


def solution(mesh):
    return jax.shard_map(
        per_device,
        mesh=mesh,
        in_specs=(
            P(("grp", "dom")),
            P(("grp", "dom")),
            P(None, ("grp", "dom")),
            P(None, ("grp", "dom")),
            P(("grp", "dom")),
            P(("grp", "dom")),
            P(("grp", "dom")),
            P(("grp", "dom")),
            P(("grp", "dom")),
            P(("grp", "dom")),
            P(("grp", "dom")),
            P(None, ("grp", "dom")),
            P(None, ("grp", "dom")),
            P(),
            P(None, "grp"),
        ),
        out_specs=(P(("grp", "dom")), P(("grp", "dom")), P(None, "grp")),
        check_vma=False,
    )
```

time: 771 us -> 100 us (0.13); the launches traced: 761 us -> 99.8 us
  local copies, waits for them, and re-layouts: 273 us -> 8.03 us
  other arithmetic: 253 us -> 0.2 us
  waiting for transfers between devices: 128 us -> 9.36 us
  matrix products: 64.2 us -> 0 us
  Pallas kernels: 0 us -> 30.8 us
  starting transfers between devices: 17.8 us -> 39.9 us
  between operations: 15.3 us -> 1.53 us
    gather x14 -> x0, local copies, waits for them, and re-layouts: 257 us -> none  [the longest x2 79.8 us: per_device(): curl = signs[0] * extended[face_edges[0]]]
    scatter-add x4 -> x0, other arithmetic: 237 us -> none  [the longest x2 225 us: per_device(): jax.ops.segment_sum((signs * scaled[None, :]).reshape(-1), flat_index, nu...]
    psum x1 -> x0, waiting for transfers between devices: 94.1 us -> none  [per_device(): total_field = lax.psum(field, 'dom')]
    dot_general x8 -> x0, matrix products: 64.2 us -> none  [the longest x4 32.1 us: radiate(): jnp.dot(currents[freq_index], sines, preferred_element_type=jnp.float32)]
    reduce_scatter x1 -> x0, waiting for transfers between devices: 32.7 us -> none  [per_device(): field = lax.psum_scatter(own_field, 'grp', scatter_dimension=1, tiled=True)]
    pallas_call x0 -> x6, Pallas kernels: none -> 30.8 us  [call(): pl.pallas_call(kernel, out_shape=[jax.ShapeDtypeStruct(shape, jnp.float32...]
    all_to_all x0 -> x1, starting transfers between devices: none -> 21.3 us  [per_device(): shares = lax.all_to_all(shares, AXES, 0, 0, tiled=True)]
    concatenate x2 -> x0, local copies, waits for them, and re-layouts: 14.5 us -> none  [the longest x1 14.5 us: radiate(): return jnp.concatenate(rows, 0)]
  transfers between devices with their start and end apart: 10 -> 9, of which waited for: 4 -> 3; matrix products, arithmetic and copies ran while one was open for 1% -> 1% of each run, Pallas kernels for 0% -> 0%
where the time goes in v1:
time: 100 us; the launch traced here: 99.8 us
  starting transfers between devices  39.9 us (40%)
  Pallas kernels  30.8 us (31%)
  blocking collectives  9.99 us (10%)
  waiting for transfers between devices  9.36 us (9%)
  local copies, waits for them, and re-layouts  8.03 us (8%)
  between operations  1.53 us (2%)
    pallas_call x6, Pallas kernels, call(): pl.pallas_call(kernel, out_shape=[jax.ShapeDtypeStruct(shape, jnp.float32...  30.8 us
    all_to_all x1, starting transfers between devices, per_device(): shares = lax.all_to_all(shares, AXES, 0, 0, tiled=True)  21.3 us
    ppermute x4, starting transfers between devices, swap(): lax.ppermute(send_a, AXES, pairs_a)  16.1 us
    all_to_all x1, blocking collectives, per_device(): lax.all_to_all(jnp.broadcast_to(power, (dom_size, width)), 'dom', 0, 0, t...  9.99 us
    all_to_all x1, waiting for transfers between devices, per_device(): shares = lax.all_to_all(shares, AXES, 0, 0, tiled=True)  8.99 us
    unnamed x38, local copies, waits for them, and re-layouts  5.88 us
    ppermute x4, starting transfers between devices, swap(): lax.ppermute(send_b, AXES, pairs_b)  2.6 us
  transfers between devices with their start and end apart: 9, of which 3 were waited for; matrix products, arithmetic and copies ran while one was open for 1% of the time, Pallas kernels for 0%

profile of v1, /device:TPU:0, one launch (start us, length us, event | category | flops | bytes accessed | tf_op | source)
XLA Modules:
  0.0 99.8 jit_solution(12849855324354963166)
XLA Ops:
  0.7 0.7 copy-done.5
  1.4 0.7 copy-done.9
  2.1 0.7 copy-done.11
  3.4 0.6 collective-permute-start.1
  4.2 0.6 copy-done.15
  4.9 0.9 copy-done.1
  5.8 0.9 copy-done.3
  6.7 8.0 %faces.2 = (f32[56,128]{1,0:T(8,128)S(1)}, f32[32,128]{1,0:T(8,128)S(1)}, f32[4,128]{1,0:T(4,128)S(1)}, f32[4,128]{1,0:T(4,128)S(1)}, f32[1,128]{1,0:T(1,128)S(1)}) custom-call(s32[1]{0:T(128)} %bitcast.even_ref, f32[32,128]{1,0:T(8,128)S(1)} %bitcast.15, f32[4,128]{1,0:T(4,128)S(1)} %collective-permute-done.got_a_ref, ...), custom_call_target="tpu_custom_call" | custom-call | tf_op jit(solution)/shard_map/faces/pallas_call | solution.py:345
  14.7 5.1 %collective-permute-start.2 = (f32[4,128]{1,0:T(4,128)S(1)}, f32[4,128]{1,0:T(4,128)S(1)}, u32[]{:S(2)}, u32[]{:S(2)}) collective-permute-start(f32[4,128]{1,0:T(4,128)S(1)} %get-tuple-element.24), channel_id=1, source_target_pairs={{0,1},{1,0},{2,3},{3,2},{4,5},{5,4},{6,7},{7,6},{8,9},{9,8},{10,11... | collective-permute-start | bytes 6152 | tf_op jit(solution)/shard_map/ppermute | solution.py:383
  19.8 0.6 collective-permute-start.3
  20.6 0.7 copy-done.12
  21.7 5.5 %collective-permute-start.4 = (f32[4,128]{1,0:T(4,128)S(1)}, f32[4,128]{1,0:T(4,128)S(1)}, u32[]{:S(2)}, u32[]{:S(2)}) collective-permute-start(f32[4,128]{1,0:T(4,128)S(1)} %get-tuple-element.27), channel_id=1, source_target_pairs={{0,1},{1,0},{2,3},{3,2},{4,5},{5,4},{6,7},{7,6},{8,9},{9,8},{10,11... | collective-permute-start | bytes 6152 | tf_op jit(solution)/shard_map/ppermute | solution.py:383
  27.2 0.6 collective-permute-start.5
  28.0 8.5 %faces.3 = (f32[56,128]{1,0:T(8,128)}, f32[32,128]{1,0:T(8,128)S(1)}, f32[4,128]{1,0:T(4,128)S(1)}, f32[4,128]{1,0:T(4,128)S(1)}, f32[1,128]{1,0:T(1,128)S(1)}) custom-call(s32[1]{0:T(128)} %bitcast.even_ref, f32[32,128]{1,0:T(8,128)S(1)} %get-tuple-element.26.e_ref, f32[4,128]{1,0:T(4,128)S(1)} %collective-permute-done.4.got_a_ref, ...), custom_call_target="tpu_custom_call" | custom-call | tf_op jit(solution)/shard_map/faces/pallas_call | solution.py:345
  36.6 5.0 %collective-permute-start.6 = (f32[4,128]{1,0:T(4,128)S(1)}, f32[4,128]{1,0:T(4,128)S(1)}, u32[]{:S(2)}, u32[]{:S(2)}) collective-permute-start(f32[4,128]{1,0:T(4,128)S(1)} %get-tuple-element.31), channel_id=1, source_target_pairs={{0,1},{1,0},{2,3},{3,2},{4,5},{5,4},{6,7},{7,6},{8,9},{9,8},{10,11... | collective-permute-start | bytes 6152 | tf_op jit(solution)/shard_map/ppermute | solution.py:383
  41.6 0.6 collective-permute-start.7
  43.1 1.4 %last_edges.1 = (f32[32,128]{1,0:T(8,128)}, f32[4,16,128]{2,1,0:T(8,128)S(1)}) custom-call(s32[1]{0:T(128)} %bitcast.even_ref, f32[2,8]{1,0:T(2,128)S(1)} %reshape.153.wave_ref, f32[32,128]{1,0:T(8,128)S(1)} %get-tuple-element.26.e_ref, f32[32,128]{1,0:T(8,128)S(1)} %bitcast.20, f32[32,128]{1,0:T(8,128)S(1)} %get-tuple-element.30.own_ref, ...), custom_call_target="tpu_custom_call" | custom-call | tf_op jit(solution)/shard_map/last_edges/pallas_call | solution.py:345
  44.5 0.7 broadcast_in_dim.4
  45.2 21.3 %all-to-all-start = ((f32[32,16,128]{2,1,0:T(8,128)}), f32[32,16,128]{2,1,0:T(8,128)S(1)}, u32[]{:S(2)}, u32[]{:S(2)}) async-start(f32[32,16,128]{2,1,0:T(8,128)} %bitcast.12), calls=%async_computation | async-start | bytes 524288 | tf_op jit(solution)/shard_map/all_to_all | solution.py:442
  66.5 0.6 dynamic_slice.6
  67.8 9.0 %all-to-all-done.share_ref = f32[32,16,128]{2,1,0:T(8,128)S(1)} async-done(((f32[32,16,128]{2,1,0:T(8,128)}), f32[32,16,128]{2,1,0:T(8,128)S(1)}, u32[]{:S(2)}, u32[]{:S(2)}) %all-to-all-start) | async-done | bytes 262176 | tf_op jit(solution)/shard_map/all_to_all | solution.py:442
  76.8 12.3 %far.1 = f32[1,512]{1,0:T(1,128)S(1)} custom-call(f32[1]{0:T(128)S(6)} %mul.45.wave_ref, f32[32,16,128]{2,1,0:T(8,128)S(1)} %all-to-all-done.share_ref, f32[2,512]{1,0:T(2,128)S(1)} %constant_dynamic-slice_fusion.angles_ref), custom_call_target="tpu_custom_call" | custom-call | tf_op jit(solution)/shard_map/far/pallas_call | solution.py:345
  89.1 10.0 %all_to_all.11 = f32[16,1,512]{2,1,0:T(1,128)S(1)} all-to-all(f32[16,1,512]{2,1,0:T(1,128)S(1)} %broadcast_in_dim.5), channel_id=1, replica_groups=mesh['grp'=2,'dom'=16] {'dom'}, dimensions={0} | all-to-all | bytes 65536 | tf_op jit(solution)/shard_map/all_to_all | solution.py:455
  99.2 0.6 reshape.166
  (50 shorter events, 2.5 us)
Async XLA Ops:
  0.6 67.1 %copy-start = (f32[2,2048]{1,0:T(2,128)S(1)}, f32[2,2048]{1,0:T(2,128)}, u32[]{:S(2)}) copy-start(f32[2,2048]{1,0:T(2,128)} %param.29) | copy-start | bytes 49156
  0.6 3.6 %copy-start.8 = (f32[7168]{0:T(1024)S(1)}, f32[7168]{0:T(1024)}, u32[]{:S(2)}) copy-start(f32[7168]{0:T(1024)} %param.16) | copy-start | bytes 86020
  0.7 0.7 copy-start.5
  0.7 3.5 %copy-start.6 = (f32[7168]{0:T(1024)S(1)}, f32[7168]{0:T(1024)}, u32[]{:S(2)}) copy-start(f32[7168]{0:T(1024)} %param.22) | copy-start | bytes 86020
  2.9 1.3 %collective-permute-start = (f32[4,128]{1,0:T(4,128)S(1)}, f32[4,128]{1,0:T(4,128)S(1)}, u32[]{:S(2)}, u32[]{:S(2)}) collective-permute-start(f32[4,128]{1,0:T(4,128)S(1)} %get-tuple-element.21), channel_id=1, source_target_pairs={{0,1},{1,0},{2,3},{3,2},{4,5},{5,4},{6,7},{7,6},{8,9},{9,8},{10,11... | collective-permute-start | bytes 6152 | tf_op jit(solution)/shard_map/ppermute | solution.py:383
  3.4 0.8 collective-permute-start.1
  4.9 0.9 copy-start.1
  5.8 0.9 copy-start.3
  6.7 13.9 %copy-start.7 = (f32[4096]{0:T(1024)S(1)}, f32[4096]{0:T(1024)}, u32[]{:S(2)}) copy-start(f32[4096]{0:T(1024)} %param.21) | copy-start | bytes 49156
  6.7 21.4 %copy-start.2 = (s32[3,7168]{1,0:T(4,128)S(1)}, s32[3,7168]{1,0:T(4,128)}, u32[]{:S(2)}) copy-start(s32[3,7168]{1,0:T(4,128)} %edges_ref.3) | copy-start | bytes 258052
  6.7 21.4 %copy-start.4 = (s32[3,7168]{1,0:T(4,128)S(1)}, s32[3,7168]{1,0:T(4,128)}, u32[]{:S(2)}) copy-start(s32[3,7168]{1,0:T(4,128)} %signs_ref.3) | copy-start | bytes 258052
  14.7 5.9 %collective-permute-start.2 = (f32[4,128]{1,0:T(4,128)S(1)}, f32[4,128]{1,0:T(4,128)S(1)}, u32[]{:S(2)}, u32[]{:S(2)}) collective-permute-start(f32[4,128]{1,0:T(4,128)S(1)} %get-tuple-element.24), channel_id=1, source_target_pairs={{0,1},{1,0},{2,3},{3,2},{4,5},{5,4},{6,7},{7,6},{8,9},{9,8},{10,11... | collective-permute-start | bytes 6152 | tf_op jit(solution)/shard_map/ppermute | solution.py:383
  19.8 0.8 collective-permute-start.3
  20.6 0.7 copy-start.12
  20.6 0.7 copy-start.10
  20.6 0.7 copy-start.16
  21.7 6.2 %copy-start.18 = (f32[4]{0:T(128)S(1)}, f32[4]{0:T(128)}, u32[]{:S(2)}) copy-start(f32[4]{0:T(128)} %param.28) | copy-start | bytes 52
  21.7 6.3 %collective-permute-start.4 = (f32[4,128]{1,0:T(4,128)S(1)}, f32[4,128]{1,0:T(4,128)S(1)}, u32[]{:S(2)}, u32[]{:S(2)}) collective-permute-start(f32[4,128]{1,0:T(4,128)S(1)} %get-tuple-element.27), channel_id=1, source_target_pairs={{0,1},{1,0},{2,3},{3,2},{4,5},{5,4},{6,7},{7,6},{8,9},{9,8},{10,11... | collective-permute-start | bytes 6152 | tf_op jit(solution)/shard_map/ppermute | solution.py:383
  27.2 0.8 collective-permute-start.5
  36.6 5.9 %collective-permute-start.6 = (f32[4,128]{1,0:T(4,128)S(1)}, f32[4,128]{1,0:T(4,128)S(1)}, u32[]{:S(2)}, u32[]{:S(2)}) collective-permute-start(f32[4,128]{1,0:T(4,128)S(1)} %get-tuple-element.31), channel_id=1, source_target_pairs={{0,1},{1,0},{2,3},{3,2},{4,5},{5,4},{6,7},{7,6},{8,9},{9,8},{10,11... | collective-permute-start | bytes 6152 | tf_op jit(solution)/shard_map/ppermute | solution.py:383
  41.6 0.9 collective-permute-start.7
  42.3 0.7 copy-start.14
  42.4 0.7 copy-start.13
  45.2 31.5 %all-to-all-start = ((f32[32,16,128]{2,1,0:T(8,128)}), f32[32,16,128]{2,1,0:T(8,128)S(1)}, u32[]{:S(2)}, u32[]{:S(2)}) async-start(f32[32,16,128]{2,1,0:T(8,128)} %bitcast.12), calls=%async_computation | async-start | bytes 524288 | tf_op jit(solution)/shard_map/all_to_all | solution.py:442
  (4 other events, 2.7 us)

commit v2 on v1

v2 whole, which is shorter than its diff:
```python
import functools
import math

import jax
import jax.numpy as jnp
from jax import lax
from jax.experimental import pallas as pl
from jax.experimental.pallas import tpu as pltpu
from jax.sharding import PartitionSpec as P

STEPS = 2
FREQ = 4
LANES = 128
AXES = ("grp", "dom")

time_step = 0.25

HALF_SINE = (
    4.442865965050709 * (1 - 1e-7),
    -7.307366951967784 * (1 - 1e-7),
    3.594064346893813 * (1 - 1e-7),
    -0.7824719355799322 * (1 - 1e-7),
)
TWO = 2.0000004768371582

PARAMS = pltpu.CompilerParams(vmem_limit_bytes=48 * 1024 * 1024)
VMEM_SPEC = pl.BlockSpec(memory_space=pltpu.VMEM)
SMEM_SPEC = pl.BlockSpec(memory_space=pltpu.SMEM)
HBM_SPEC = pl.BlockSpec(memory_space=pl.ANY)


def fetch(pairs, sems):
    copies = [
        pltpu.make_async_copy(source, target, sems.at[at])
        for at, (source, target) in enumerate(pairs)
    ]
    for copy in copies:
        copy.start()
    for copy in copies:
        copy.wait()


def lookup(table_ref, first, last, index):
    asked = index.shape[0]
    if asked < 8:
        index = jnp.concatenate([index] * (8 // asked), 0)
    row_of = lax.shift_right_logical(index, 7)
    lane_of = lax.bitwise_and(index, LANES - 1)
    found = jnp.zeros(index.shape, jnp.float32)
    for row in range(first, last):
        line = jnp.broadcast_to(table_ref[row : row + 1, :], index.shape)
        hit = jnp.take_along_axis(line, lane_of, axis=1, mode="promise_in_bounds")
        found = jnp.where(row_of == row, hit, found)
    return found[:asked]


def spread(index, values, rows):
    padded = -(-rows // 16) * 16
    one = jnp.ones((), jnp.bfloat16)
    zero = jnp.zeros((), jnp.bfloat16)
    row_of = lax.shift_right_logical(index, 7).astype(jnp.int16)
    lane_of = lax.bitwise_and(index, LANES - 1).astype(jnp.int16)
    high = values.astype(jnp.bfloat16)
    low = (values - high.astype(jnp.float32)).astype(jnp.bfloat16)
    row_iota = lax.broadcasted_iota(jnp.int32, (padded, LANES), 0).astype(jnp.int16)
    lane_iota = lax.broadcasted_iota(jnp.int32, (LANES, LANES), 0).astype(jnp.int16)
    lefts = []
    rights = []
    for at in range(index.shape[0]):
        span = slice(at, at + 1)
        hit = row_iota == jnp.broadcast_to(row_of[span], (padded, LANES))
        left = [
            jnp.where(hit, jnp.broadcast_to(part[span], (padded, LANES)), zero)
            for part in (high, low)
        ]
        lefts.append(jnp.concatenate(left, 0))
        rights.append(
            jnp.where(lane_iota == jnp.broadcast_to(lane_of[span], (LANES, LANES)), one, zero)
        )
    both = lax.dot_general(
        jnp.concatenate(lefts, 1),
        jnp.concatenate(rights, 1),
        (((1,), (1,)), ((), ())),
        preferred_element_type=jnp.float32,
    )
    return both[:rows] + both[padded : padded + rows]


def gather_sends(even, table_ref, lists, send_a_ref, send_b_ref):
    found = lookup(table_ref, 0, table_ref.shape[0], lists)
    half = send_a_ref.shape[0]
    send_a_ref[...] = jnp.where(even, found[:half], found[half:])
    send_b_ref[...] = jnp.where(even, found[half:], found[:half])


def first_kernel(
    even_ref, e_hbm, next_hbm, prev_hbm, send_a_ref, send_b_ref, e_ref, lists_ref, sems
):
    half = next_hbm.shape[0]
    fetch(
        [
            (e_hbm, e_ref),
            (next_hbm, lists_ref.at[pl.ds(0, half)]),
            (prev_hbm, lists_ref.at[pl.ds(half, half)]),
        ],
        sems,
    )
    gather_sends(even_ref[0] == 1, e_ref, lists_ref[...], send_a_ref, send_b_ref)


def own_curl(table_ref, own_rows, index_ref, signs_ref, curl_ref):
    face_rows = curl_ref.shape[0]
    for at in range(0, face_rows, 8):
        curl = None
        for k in range(3):
            span = slice(k * face_rows + at, k * face_rows + at + 8)
            term = signs_ref[span, :] * lookup(table_ref, 0, own_rows, index_ref[span, :])
            curl = term if curl is None else curl + term
        curl_ref[at : at + 8, :] = curl


def prepare_kernel(
    e_ref,
    edges_hbm,
    signs_hbm,
    b_hbm,
    mu_hbm,
    eps_hbm,
    face_hbm,
    edge_hbm,
    live_hbm,
    geom_hbm,
    acc_hbm,
    index_ref,
    signs_ref,
    curl_ref,
    b_ref,
    mu_ref,
    eps_ref,
    face_ref,
    edge_ref,
    live_ref,
    geom_ref,
    acc_ref,
    raw_edges,
    raw_signs,
    sems,
):
    fetch(
        [
            (edges_hbm, raw_edges),
            (signs_hbm, raw_signs),
            (b_hbm, b_ref),
            (mu_hbm, mu_ref),
            (eps_hbm, eps_ref),
            (face_hbm, face_ref),
            (edge_hbm, edge_ref),
            (live_hbm, live_ref),
            (geom_hbm, geom_ref),
            (acc_hbm, acc_ref),
        ],
        sems,
    )
    face_rows = b_ref.shape[0]
    for k in range(3):
        for at in range(face_rows):
            lanes = slice(at * LANES, (at + 1) * LANES)
            to = k * face_rows + at
            index_ref[to : to + 1, :] = raw_edges[k : k + 1, lanes]
            signs_ref[to : to + 1, :] = raw_signs[k : k + 1, lanes].astype(jnp.float32)
    own_curl(e_ref, e_ref.shape[0], index_ref, signs_ref, curl_ref)


def again_kernel(e_ref, index_ref, signs_ref, curl_ref):
    own_curl(e_ref, e_ref.shape[0], index_ref, signs_ref, curl_ref)


def faces_kernel(
    even_ref,
    got_a_ref,
    got_b_ref,
    index_ref,
    signs_ref,
    curl_ref,
    b_ref,
    mu_ref,
    b_out_ref,
    own_ref,
    send_a_ref,
    send_b_ref,
    table_ref,
):
    even = even_ref[0] == 1
    own_rows = own_ref.shape[0]
    halo_rows = got_a_ref.shape[0]
    face_rows = b_ref.shape[0]
    rows = own_rows + 2 * halo_rows
    got_a = got_a_ref[...]
    got_b = got_b_ref[...]
    table_ref[own_rows : own_rows + halo_rows, :] = jnp.where(even, got_b, got_a)
    table_ref[own_rows + halo_rows : rows, :] = jnp.where(even, got_a, got_b)
    total = jnp.zeros((rows, LANES), jnp.float32)
    for at in range(0, face_rows, 8):
        spans = [slice(k * face_rows + at, k * face_rows + at + 8) for k in range(3)]
        curl = curl_ref[at : at + 8, :]
        for span in spans:
            curl = curl + signs_ref[span, :] * lookup(table_ref, own_rows, rows, index_ref[span, :])
        b_new = b_ref[at : at + 8, :] - time_step * curl
        b_out_ref[at : at + 8, :] = b_new
        scaled = mu_ref[at : at + 8, :] * b_new
        total = total + spread(
            jnp.concatenate([index_ref[span, :] for span in spans], 0),
            jnp.concatenate([signs_ref[span, :] * scaled for span in spans], 0),
            rows,
        )
    own_ref[...] = total[:own_rows]
    to_prev = total[own_rows : own_rows + halo_rows]
    to_next = total[own_rows + halo_rows :]
    send_a_ref[...] = jnp.where(even, to_next, to_prev)
    send_b_ref[...] = jnp.where(even, to_prev, to_next)


def edges_update(even, e_ref, eps_ref, own_ref, got_a_ref, got_b_ref, lists, e_out_ref):
    got_a = got_a_ref[...]
    got_b = got_b_ref[...]
    from_next = jnp.where(even, got_a, got_b)
    from_prev = jnp.where(even, got_b, got_a)
    back = spread(lists, jnp.concatenate([from_next, from_prev], 0), e_ref.shape[0])
    e_out_ref[...] = e_ref[...] + time_step * eps_ref[...] * (own_ref[...] + back)


def edges_kernel(
    even_ref,
    e_ref,
    eps_ref,
    own_ref,
    got_a_ref,
    got_b_ref,
    lists_ref,
    e_out_ref,
    send_a_ref,
    send_b_ref,
):
    even = even_ref[0] == 1
    lists = lists_ref[...]
    edges_update(even, e_ref, eps_ref, own_ref, got_a_ref, got_b_ref, lists, e_out_ref)
    gather_sends(even, e_out_ref, lists, send_a_ref, send_b_ref)


def early_kernel(
    coef_ref,
    b_first_ref,
    b_last_ref,
    e_first_ref,
    face_ref,
    edge_ref,
    live_ref,
    geom_ref,
    acc_ref,
    early_ref,
    base_ref,
):
    face_rows = b_first_ref.shape[0]
    live = live_ref[...].astype(jnp.float32)
    faces = face_ref[...]
    b_first = lookup(b_first_ref, 0, face_rows, faces)
    b_last = lookup(b_last_ref, 0, face_rows, faces)
    e_first = lookup(e_first_ref, 0, e_first_ref.shape[0], edge_ref[...])
    normal = geom_ref[0:3, :]
    centre = geom_ref[6:9, :]
    base = []
    for q in range(FREQ):
        for part in range(2):
            at = 2 * q + part
            value = acc_ref[at : at + 1, :] + coef_ref[0, at] * b_first + coef_ref[1, at] * b_last
            early_ref[q, 3 * part : 3 * part + 3, :] = normal * (value * live)
            at_edge = 2 * FREQ + at
            base.append(acc_ref[at_edge : at_edge + 1, :] + coef_ref[0, at] * e_first)
        early_ref[q, 6:9, :] = centre
    base_ref[...] = jnp.concatenate(base, 0)


def last_kernel(
    even_ref,
    coef_ref,
    e_ref,
    eps_ref,
    own_ref,
    got_a_ref,
    got_b_ref,
    lists_ref,
    edge_ref,
    live_ref,
    geom_ref,
    early_ref,
    base_ref,
    e_out_ref,
    share_ref,
):
    even = even_ref[0] == 1
    edges_update(
        even, e_ref, eps_ref, own_ref, got_a_ref, got_b_ref, lists_ref[...], e_out_ref
    )
    e_last = lookup(e_out_ref, 0, e_ref.shape[0], edge_ref[...])
    live = live_ref[...].astype(jnp.float32)
    tangent = geom_ref[3:6, :]
    for q in range(FREQ):
        rows = [early_ref[q, 0:6, :]]
        for part in range(2):
            at = 2 * q + part
            value = base_ref[at : at + 1, :] + coef_ref[1, at] * e_last
            rows.append(tangent * (value * live))
        rows.append(early_ref[q, 6:9, :])
        rows.append(jnp.zeros((1, LANES), jnp.float32))
        block = jnp.concatenate(rows, 0)
        share_ref[q] = block


def three(value):
    high = value.astype(jnp.bfloat16).astype(jnp.float32)
    middle = (value - high).astype(jnp.bfloat16).astype(jnp.float32)
    return high, middle, value - high - middle


def waves(turns):
    f = turns - jnp.round(turns)
    s = f * f
    half = HALF_SINE[3] * s + HALF_SINE[2]
    half = half * s + HALF_SINE[1]
    half = half * s + HALF_SINE[0]
    half = half * f
    square = half * half
    rest = TWO - square
    cosine = 1.0 - square
    sine = half * (rest * lax.rsqrt(rest))
    return cosine.astype(jnp.bfloat16), sine.astype(jnp.bfloat16)


def cross(left, right):
    return [
        left[1] * right[2] - left[2] * right[1],
        left[2] * right[0] - left[0] * right[2],
        left[0] * right[1] - left[1] * right[0],
    ]


def far_kernel(
    turns_ref, share_ref, angles_ref, power_ref, left_ref, wave_a, wave_b, group, rows, cols, scale
):
    sources = share_ref.shape[0]
    width = angles_ref.shape[1]
    polar = angles_ref[0:1, :]
    azimuth = angles_ref[1:2, :]
    sine = jnp.sin(polar)
    dirs = [sine * jnp.cos(azimuth), sine * jnp.sin(azimuth), jnp.cos(polar)]
    turns = turns_ref[0]
    scaled = jnp.concatenate(
        [jnp.zeros((4, width), jnp.float32)]
        + [one * turns for one in dirs]
        + [jnp.zeros((1, width), jnp.float32)],
        0,
    )
    t1, t2, t3 = three(scaled)
    right = jnp.concatenate([t1, t2, t3, t1, t2, t1], 0).astype(jnp.bfloat16)
    blocks = sources // group
    chunks = group * LANES // rows
    pieces = [(low, min(low + cols, 2 * width)) for low in range(0, 2 * width, cols)]
    per_chunk = -(-len(pieces) // chunks)

    def centres(at):
        for one in range(group):
            u1, u2, u3 = three(share_ref[at * group + one, 8:16, :])
            stack = jnp.concatenate([u1, u1, u1, u2, u2, u3], 0)
            left_ref[one * LANES : (one + 1) * LANES, :] = stack.T.astype(jnp.bfloat16)

    def project(chunk):
        left = left_ref[chunk * rows : (chunk + 1) * rows, :]
        return jnp.dot(left, right, preferred_element_type=jnp.float32)

    def currents(at):
        return jnp.concatenate([share_ref[at * group + one] for one in range(group)], 1).astype(
            jnp.bfloat16
        )

    def collect(current, source, total, piece):
        low, high = pieces[piece]
        return total + jnp.dot(current, source[:, low:high], preferred_element_type=jnp.float32)

    def half(next_at, done_at, target, source, totals):
        totals = list(totals)
        current = currents(done_at)
        ahead = project(0)
        for chunk in range(chunks):
            theta = ahead
            if chunk + 1 < chunks:
                ahead = project(chunk + 1)
            cosine, sine = waves(theta)
            target[chunk * rows : (chunk + 1) * rows, 0:width] = cosine
            target[chunk * rows : (chunk + 1) * rows, width : 2 * width] = sine
            for piece in range(chunk * per_chunk, min((chunk + 1) * per_chunk, len(pieces))):
                totals[piece] = collect(current, source, totals[piece], piece)
        centres(next_at)
        return totals

    def body(at, totals):
        totals = half(2 * at + 1, jnp.maximum(2 * at - 1, 0), wave_a, wave_b, totals)
        return tuple(half(jnp.minimum(2 * at + 2, blocks - 1), 2 * at, wave_b, wave_a, totals))

    centres(0)
    wave_b[...] = jnp.zeros_like(wave_b)
    totals = tuple(jnp.zeros((16, high - low), jnp.float32) for low, high in pieces)
    totals = lax.fori_loop(0, blocks // 2, body, totals)
    current = currents(blocks - 1)
    total = jnp.concatenate(
        [collect(current, wave_b, total, piece) for piece, total in enumerate(totals)], 1
    )

    def p_row(at):
        return total[at : at + 1, 0:width]

    def q_row(at):
        return total[at : at + 1, width : 2 * width]

    n_real = [p_row(i) - q_row(3 + i) for i in range(3)]
    n_imag = [q_row(i) + p_row(3 + i) for i in range(3)]
    l_real = [p_row(6 + i) - q_row(9 + i) for i in range(3)]
    l_imag = [q_row(6 + i) + p_row(9 + i) for i in range(3)]
    power = jnp.zeros((1, width), jnp.float32)
    for n_part, l_part in ((n_real, l_real), (n_imag, l_imag)):
        outer = cross(dirs, cross(dirs, n_part))
        inner = cross(dirs, l_part)
        for i in range(3):
            gap = outer[i] - inner[i]
            power = power + gap * gap
    power_ref[...] = power * scale


def call(kernel, scalars, arrays, outs, scratch=(), name=None, far_arrays=()):
    return pl.pallas_call(
        kernel,
        out_shape=[jax.ShapeDtypeStruct(shape, kind) for shape, kind in outs],
        in_specs=[SMEM_SPEC] * len(scalars)
        + [VMEM_SPEC] * len(arrays)
        + [HBM_SPEC] * len(far_arrays),
        out_specs=[VMEM_SPEC] * len(outs),
        scratch_shapes=list(scratch),
        compiler_params=PARAMS,
        name=name,
    )(*scalars, *arrays, *far_arrays)


def per_device(
    e_field,
    b_field,
    face_edges,
    face_signs,
    send_prev,
    send_next,
    eps_inv,
    mu_inv,
    huy_face,
    huy_edge,
    huy_live,
    huy_geom,
    huy_acc,
    wavenum,
    angles,
):
    grp_size = lax.axis_size("grp")
    dom_size = lax.axis_size("dom")
    parts = grp_size * dom_size
    me = lax.axis_index(AXES)
    even = (1 - me % 2).astype(jnp.int32).reshape(1)
    pairs_a = [(i, i ^ 1) for i in range(parts)]
    pairs_b = [(i, i + 1) for i in range(1, parts - 1, 2)]
    pairs_b = pairs_b + [(j, i) for i, j in pairs_b]

    def swap(send_a, send_b):
        return lax.ppermute(send_a, AXES, pairs_a), lax.ppermute(send_b, AXES, pairs_b)

    def table(array):
        return array.reshape(-1, LANES)

    def f32(shape):
        return (shape, jnp.float32)

    def i32(shape):
        return (shape, jnp.int32)

    next_table, prev_table = table(send_next), table(send_prev)
    own = (e_field.shape[0] // LANES, LANES)
    halo = next_table.shape
    lists = (2 * halo[0], LANES)
    faces = (b_field.shape[0] // LANES, LANES)
    ends = (3 * faces[0], LANES)
    sample = (1, LANES)
    rows = own[0] + 2 * halo[0]

    moments = time_step * jnp.arange(1, STEPS + 1, dtype=jnp.float32)
    phase = moments[:, None] * wavenum[None, :]
    coef = jnp.stack([jnp.cos(phase), -jnp.sin(phase)], 2).reshape(STEPS, 2 * FREQ)
    blocks = dom_size // FREQ
    width = angles.shape[1] // blocks
    place = lax.axis_index("dom")
    own_angles = lax.dynamic_slice_in_dim(angles, (place % blocks) * width, width, axis=1)
    turns = lax.dynamic_slice_in_dim(wavenum, place // blocks, 1) * (0.5 / math.pi)

    *send, e_table, list_table = call(
        first_kernel,
        [even],
        [],
        [f32(halo), f32(halo), f32(own), i32(lists)],
        [pltpu.SemaphoreType.DMA((3,))],
        name="first",
        far_arrays=[table(e_field), next_table, prev_table],
    )
    got = swap(*send)
    index, signs, curl, b_table, mu_table, eps_table, face_ids, edge_ids, live, geom, acc = call(
        prepare_kernel,
        [],
        [e_table],
        [
            i32(ends),
            f32(ends),
            f32(faces),
            f32(faces),
            f32(faces),
            f32(own),
            i32(sample),
            i32(sample),
            i32(sample),
            f32(huy_geom.shape),
            f32(huy_acc.shape),
        ],
        [
            pltpu.VMEM(face_edges.shape, jnp.int32),
            pltpu.VMEM(face_signs.shape, jnp.int32),
            pltpu.SemaphoreType.DMA((10,)),
        ],
        name="prepare",
        far_arrays=[
            face_edges,
            face_signs,
            table(b_field),
            table(mu_inv),
            table(eps_inv),
            table(huy_face),
            table(huy_edge),
            table(huy_live),
            huy_geom,
            huy_acc,
        ],
    )
    b_steps = []
    e_steps = []
    for step in range(STEPS):
        if step > 0:
            (curl,) = call(
                again_kernel, [], [e_table, index, signs], [f32(faces)], name="own_curl"
            )
        b_table, own_sum, back_a, back_b = call(
            faces_kernel,
            [even],
            [*got, index, signs, curl, b_table, mu_table],
            [f32(faces), f32(own), f32(halo), f32(halo)],
            [pltpu.VMEM((rows, LANES), jnp.float32)],
            name="faces",
        )
        b_steps.append(b_table)
        back = swap(back_a, back_b)
        common = [e_table, eps_table, own_sum, *back, list_table]
        if step < STEPS - 1:
            e_table, *send = call(
                edges_kernel, [even], common, [f32(own), f32(halo), f32(halo)], name="edges"
            )
            e_steps.append(e_table)
            got = swap(*send)
    early, base = call(
        early_kernel,
        [coef],
        [*b_steps, *e_steps, face_ids, edge_ids, live, geom, acc],
        [f32((FREQ, 16, LANES)), f32((2 * FREQ, LANES))],
        name="early",
    )
    e_table, share = call(
        last_kernel,
        [even, coef],
        common + [edge_ids, live, geom, early, base],
        [f32(own), f32((FREQ, 16, LANES))],
        name="last_edges",
    )
    shares = jnp.broadcast_to(
        share[None, :, None], (grp_size, FREQ, blocks, 16, LANES)
    ).reshape(parts, 16, LANES)
    shares, own_angles, turns = lax.optimization_barrier((shares, own_angles, turns))
    shares = lax.all_to_all(shares, AXES, 0, 0, tiled=True)
    group = 4
    (power,) = call(
        functools.partial(
            far_kernel, group=group, rows=64, cols=256, scale=1.0 / (LANES * parts)
        ),
        [turns],
        [shares, own_angles],
        [f32((1, width))],
        [
            pltpu.VMEM((group * LANES, 48), jnp.bfloat16),
            pltpu.VMEM((group * LANES, 2 * width), jnp.bfloat16),
            pltpu.VMEM((group * LANES, 2 * width), jnp.bfloat16),
        ],
        name="far",
    )
    power = lax.all_to_all(
        jnp.broadcast_to(power, (dom_size, width)), "dom", 0, 0, tiled=True
    ).reshape(FREQ, blocks * width)
    return (e_table.reshape(-1), b_table.reshape(-1), power)


def solution(mesh):
    return jax.shard_map(
        per_device,
        mesh=mesh,
        in_specs=(
            P(("grp", "dom")),
            P(("grp", "dom")),
            P(None, ("grp", "dom")),
            P(None, ("grp", "dom")),
            P(("grp", "dom")),
            P(("grp", "dom")),
            P(("grp", "dom")),
            P(("grp", "dom")),
            P(("grp", "dom")),
            P(("grp", "dom")),
            P(("grp", "dom")),
            P(None, ("grp", "dom")),
            P(None, ("grp", "dom")),
            P(),
            P(None, "grp"),
        ),
        out_specs=(P(("grp", "dom")), P(("grp", "dom")), P(None, "grp")),
        check_vma=False,
    )
```

time: 100 us -> 76.3 us (0.76)
  blocking collectives: 9.99 us -> 36.9 us
  starting transfers between devices: 39.9 us -> 15.5 us
  Pallas kernels: 30.8 us -> 14.8 us
  waiting for transfers between devices: 9.36 us -> 0.04 us
  local copies, waits for them, and re-layouts: 8.03 us -> 6.66 us
    all_to_all x0 -> x1, blocking collectives: none -> 26.9 us  [per_device(): shares = lax.all_to_all(shares, AXES, 0, 0, tiled=True)]
    all_to_all x1 -> x0, starting transfers between devices: 21.3 us -> none  [per_device(): shares = lax.all_to_all(shares, AXES, 0, 0, tiled=True)]
    pallas_call x6 -> x9, Pallas kernels: 30.8 us -> 14.8 us  [call(): pl.pallas_call(kernel, out_shape=[jax.ShapeDtypeStruct(shape, kind) for s...]
    all_to_all x1 -> x0, waiting for transfers between devices: 8.99 us -> none  [per_device(): shares = lax.all_to_all(shares, AXES, 0, 0, tiled=True)]
    ppermute x4, starting transfers between devices: 16.1 us -> 12.8 us  [swap(): lax.ppermute(send_a, AXES, pairs_a)]
    unnamed x38 -> x32, local copies, waits for them, and re-layouts: 5.88 us -> 5.21 us
  transfers between devices with their start and end apart: 9 -> 8, of which waited for: 3 -> 0; matrix products, arithmetic and copies ran while one was open for 1% -> 1% of each run, Pallas kernels for 0% -> 4%
where the time goes in v2:
time: 76.3 us; the launch traced here: 75.8 us
  blocking collectives  36.9 us (48%)
  starting transfers between devices  15.5 us (20%)
  Pallas kernels  14.8 us (19%)
  local copies, waits for them, and re-layouts  6.66 us (9%)
  between operations  1.65 us (2%)
    all_to_all x1, blocking collectives, per_device(): shares = lax.all_to_all(shares, AXES, 0, 0, tiled=True)  26.9 us
    pallas_call x9, Pallas kernels, call(): pl.pallas_call(kernel, out_shape=[jax.ShapeDtypeStruct(shape, kind) for s...  14.8 us
    ppermute x4, starting transfers between devices, swap(): lax.ppermute(send_a, AXES, pairs_a)  12.8 us
    all_to_all x1, blocking collectives, per_device(): lax.all_to_all(jnp.broadcast_to(power, (dom_size, width)), 'dom', 0, 0, t...  9.99 us
    unnamed x32, local copies, waits for them, and re-layouts  5.21 us
    ppermute x4, starting transfers between devices, swap(): lax.ppermute(send_b, AXES, pairs_b)  2.73 us
  transfers between devices with their start and end apart: 8, of which 0 were waited for; matrix products, arithmetic and copies ran while one was open for 1% of the time, Pallas kernels for 4%

profile of v2, /device:TPU:0, one launch (start us, length us, event | category | flops | bytes accessed | tf_op | source)
XLA Modules:
  0.0 75.8 jit_solution(2515233540245730820)
XLA Ops:
  0.7 0.6 copy-done.11
  2.1 0.6 collective-permute-start.1
  2.8 0.6 copy-done.12
  3.4 0.9 %copy-done.1 = s32[3,7168]{1,0:T(4,128)S(1)} copy-done((s32[3,7168]{1,0:T(4,128)S(1)}, s32[3,7168]{1,0:T(4,128)}, u32[]{:S(2)}) %copy-start.1) | copy-done | bytes 86040
  4.3 0.9 %copy-done.2 = s32[3,7168]{1,0:T(4,128)S(1)} copy-done((s32[3,7168]{1,0:T(4,128)S(1)}, s32[3,7168]{1,0:T(4,128)}, u32[]{:S(2)}) %copy-start.2) | copy-done | bytes 86040
  5.2 0.7 copy-done.7
  5.9 0.7 copy-done.9
  6.6 0.7 copy-done.14
  7.3 1.4 %prepare.1 = (s32[168,128]{1,0:T(8,128)S(1)}, f32[168,128]{1,0:T(8,128)S(1)}, f32[56,128]{1,0:T(8,128)S(1)}, f32[56,128]{1,0:T(8,128)S(1)}, f32[56,128]{1,0:T(8,...) custom-call(f32[32,128]{1,0:T(8,128)S(1)} %get-tuple-element.36.e_re, ...), custom_call_target="tpu_custom_call" | custom-call | tf_op jit(solution)/shard_map/prepare/pallas_call | solution.py:439
  8.7 1.7 %faces.2 = (f32[56,128]{1,0:T(8,128)S(1)}, f32[32,128]{1,0:T(8,128)S(1)}, f32[4,128]{1,0:T(4,128)S(1)}, f32[4,128]{1,0:T(4,128)S(1)}) custom-call(s32[1]{0:T(128)} %bitcast.even_ref, f32[4,128]{1,0:T(4,128)S(1)} %collective-permute-done.got_a_ref, f32[4,128]{1,0:T(4,128)S(1)} %collective-permute-done.1.got_b_ref, ...), custom_call_target="tpu_custom_call" | custom-call | tf_op jit(solution)/shard_map/faces/pallas_call | solution.py:439
  10.5 4.0 %collective-permute-start.2 = (f32[4,128]{1,0:T(4,128)S(1)}, f32[4,128]{1,0:T(4,128)S(1)}, u32[]{:S(2)}, u32[]{:S(2)}) collective-permute-start(f32[4,128]{1,0:T(4,128)S(1)} %get-tuple-element.46), channel_id=1, source_target_pairs={{0,1},{1,0},{2,3},{3,2},{4,5},{5,4},{6,7},{7,6},{8,9},{9,8},{10,11... | collective-permute-start | bytes 6152 | tf_op jit(solution)/shard_map/ppermute | solution.py:479
  14.5 0.6 collective-permute-start.3
  15.6 4.2 %collective-permute-start.4 = (f32[4,128]{1,0:T(4,128)S(1)}, f32[4,128]{1,0:T(4,128)S(1)}, u32[]{:S(2)}, u32[]{:S(2)}) collective-permute-start(f32[4,128]{1,0:T(4,128)S(1)} %get-tuple-element.50), channel_id=1, source_target_pairs={{0,1},{1,0},{2,3},{3,2},{4,5},{5,4},{6,7},{7,6},{8,9},{9,8},{10,11... | collective-permute-start | bytes 6152 | tf_op jit(solution)/shard_map/ppermute | solution.py:479
  19.8 0.6 collective-permute-start.5
  20.4 0.8 %own_curl.1.curl_ref = f32[56,128]{1,0:T(8,128)S(1)} custom-call(f32[32,128]{1,0:T(8,128)S(1)} %get-tuple-element.49.e_ref.e_first_ref, s32[168,128]{1,0:T(8,128)S(1)} %get-tuple-element.40.index_ref, f32[168,128]{1,0:T(8,128)S(1)} %get-tuple-element.41.signs_ref), custom_call_target="tpu_custom_call" | custom-call | tf_op jit(solution)/shard_map/own_curl/pallas_call | solution.py:439
  21.3 2.0 %faces.3 = (f32[56,128]{1,0:T(8,128)}, f32[32,128]{1,0:T(8,128)S(1)}, f32[4,128]{1,0:T(4,128)S(1)}, f32[4,128]{1,0:T(4,128)S(1)}) custom-call(s32[1]{0:T(128)} %bitcast.even_ref, f32[4,128]{1,0:T(4,128)S(1)} %collective-permute-done.4.got_a_ref, f32[4,128]{1,0:T(4,128)S(1)} %collective-permute-done.5.got_b_ref, s32[168,128]{1,0:T(8,128)S(1)} %get-tuple-element.40.index_ref, ...), custom_call_target="tpu_custom_call" | custom-call | tf_op jit(solution)/shard_map/faces/pallas_call | solution.py:439
  23.4 4.1 %collective-permute-start.6 = (f32[4,128]{1,0:T(4,128)S(1)}, f32[4,128]{1,0:T(4,128)S(1)}, u32[]{:S(2)}, u32[]{:S(2)}) collective-permute-start(f32[4,128]{1,0:T(4,128)S(1)} %get-tuple-element.54), channel_id=1, source_target_pairs={{0,1},{1,0},{2,3},{3,2},{4,5},{5,4},{6,7},{7,6},{8,9},{9,8},{10,11... | collective-permute-start | bytes 6152 | tf_op jit(solution)/shard_map/ppermute | solution.py:479
  27.5 0.8 %collective-permute-start.7 = (f32[4,128]{1,0:T(4,128)S(1)}, f32[4,128]{1,0:T(4,128)S(1)}, u32[]{:S(2)}, u32[]{:S(2)}) collective-permute-start(f32[4,128]{1,0:T(4,128)S(1)} %get-tuple-element.55), channel_id=1, source_target_pairs={{1,2},{3,4},{5,6},{7,8},{9,10},{11,12},{13,14},{15,16},{17,18},{19... | collective-permute-start | bytes 6152 | tf_op jit(solution)/shard_map/ppermute | solution.py:479
  29.8 0.8 %early.1 = (f32[4,16,128]{2,1,0:T(8,128)S(1)}, f32[8,128]{1,0:T(8,128)S(1)}) custom-call(f32[2,8]{1,0:T(2,128)S(1)} %reshape.153.coef_ref, f32[56,128]{1,0:T(8,128)S(1)} %get-tuple-element.52.b_ref.b_first_ref, f32[56,128]{1,0:T(8,128)S(1)} %copy-done.3, f32[32,128]{1,0:T(8,128)S(1)} %get-tuple-element.49.e_ref.e_first_ref, ...), custom_call_target="tpu_custom_call" | custom-call | tf_op jit(solution)/shard_map/early/pallas_call | solution.py:439
  30.6 1.4 %last_edges.1 = (f32[32,128]{1,0:T(8,128)}, f32[4,16,128]{2,1,0:T(8,128)S(1)}) custom-call(s32[1]{0:T(128)} %bitcast.even_ref, f32[2,8]{1,0:T(2,128)S(1)} %reshape.153.coef_ref, f32[32,128]{1,0:T(8,128)S(1)} %get-tuple-element.49.e_ref.e_first_ref, f32[32,128]{1,0:T(8,128)S(1)} %get-tuple-element.37.eps_ref, f32[32,128]{1,0:T(8,128)S(1)} %get-tuple-element.53.own_ref, ...), custom_call_target="tpu_custom_call" | custom-call | tf_op jit(solution)/shard_map/last_edges/pallas_call | solution.py:439
  32.0 26.9 %all_to_all.11.share_ref = f32[32,16,128]{2,1,0:T(8,128)S(1)} all-to-all(f32[32,16,128]{2,1,0:T(8,128)S(1)} %bitcast.25), channel_id=1, replica_groups=mesh['grp'=2,'dom'=16] {'grp','dom'}, dimensions={0} | all-to-all | bytes 524288 | tf_op jit(solution)/shard_map/all_to_all | solution.py:596
  58.9 6.2 %far.1 = f32[1,512]{1,0:T(1,128)S(1)} custom-call(f32[1]{0:T(128)S(6)} %mul.46.turns_ref, f32[32,16,128]{2,1,0:T(8,128)S(1)} %all_to_all.11.share_ref, f32[2,512]{1,0:T(2,128)S(1)} %constant_dynamic-slice_fusion.angles_ref), custom_call_target="tpu_custom_call" | custom-call | tf_op jit(solution)/shard_map/far/pallas_call | solution.py:439
  65.1 10.0 %all_to_all.12 = f32[16,1,512]{2,1,0:T(1,128)S(1)} all-to-all(f32[16,1,512]{2,1,0:T(1,128)S(1)} %broadcast_in_dim.5), channel_id=1, replica_groups=mesh['grp'=2,'dom'=16] {'dom'}, dimensions={0} | all-to-all | bytes 65536 | tf_op jit(solution)/shard_map/all_to_all | solution.py:612
  75.1 0.6 reshape.166
  (46 shorter events, 2.2 us)
Async XLA Ops:
  0.6 19.8 %copy-start = (f32[2,2048]{1,0:T(2,128)S(1)}, f32[2,2048]{1,0:T(2,128)}, u32[]{:S(2)}) copy-start(f32[2,2048]{1,0:T(2,128)} %param.29) | copy-start | bytes 49156
  0.6 0.7 copy-start.11
  0.7 0.7 copy-start.10
  0.7 2.1 %copy-start.8 = (f32[9,128]{1,0:T(8,128)S(1)}, f32[9,128]{1,0:T(8,128)}, u32[]{:S(2)}) copy-start(f32[9,128]{1,0:T(8,128)} %geom_hbm.1) | copy-start | bytes 13828
  0.7 0.7 copy-start.6
  0.7 2.1 %copy-start.13 = (s32[128]{0:T(128)S(1)}, s32[128]{0:T(128)}, u32[]{:S(2)}) copy-start(s32[128]{0:T(128)} %param.24) | copy-start | bytes 1540
  0.7 2.1 %copy-start.4 = (f32[7168]{0:T(1024)S(1)}, f32[7168]{0:T(1024)}, u32[]{:S(2)}) copy-start(f32[7168]{0:T(1024)} %param.16) | copy-start | bytes 86020
  0.7 2.1 %copy-start.5 = (f32[7168]{0:T(1024)S(1)}, f32[7168]{0:T(1024)}, u32[]{:S(2)}) copy-start(f32[7168]{0:T(1024)} %param.22) | copy-start | bytes 86020
  1.6 7.1 %collective-permute-start = (f32[4,128]{1,0:T(4,128)S(1)}, f32[4,128]{1,0:T(4,128)S(1)}, u32[]{:S(2)}, u32[]{:S(2)}) collective-permute-start(f32[4,128]{1,0:T(4,128)S(1)} %get-tuple-element.38), channel_id=1, source_target_pairs={{0,1},{1,0},{2,3},{3,2},{4,5},{5,4},{6,7},{7,6},{8,9},{9,8},{10,11... | collective-permute-start | bytes 6152 | tf_op jit(solution)/shard_map/ppermute | solution.py:479
  2.1 6.6 %collective-permute-start.1 = (f32[4,128]{1,0:T(4,128)S(1)}, f32[4,128]{1,0:T(4,128)S(1)}, u32[]{:S(2)}, u32[]{:S(2)}) collective-permute-start(f32[4,128]{1,0:T(4,128)S(1)} %get-tuple-element.39), channel_id=1, source_target_pairs={{1,2},{3,4},{5,6},{7,8},{9,10},{11,12},{13,14},{15,16},{17,18},{19... | collective-permute-start | bytes 6152 | tf_op jit(solution)/shard_map/ppermute | solution.py:479
  2.8 0.7 copy-start.12
  3.4 0.9 %copy-start.1 = (s32[3,7168]{1,0:T(4,128)S(1)}, s32[3,7168]{1,0:T(4,128)}, u32[]{:S(2)}) copy-start(s32[3,7168]{1,0:T(4,128)} %edges_hbm.1) | copy-start | bytes 258052
  4.3 0.9 %copy-start.2 = (s32[3,7168]{1,0:T(4,128)S(1)}, s32[3,7168]{1,0:T(4,128)}, u32[]{:S(2)}) copy-start(s32[3,7168]{1,0:T(4,128)} %signs_hbm.1) | copy-start | bytes 258052
  5.2 0.7 copy-start.7
  5.9 0.7 copy-start.9
  6.6 0.7 copy-start.14
  10.5 4.6 %copy-start.15 = (f32[4]{0:T(128)S(1)}, f32[4]{0:T(128)}, u32[]{:S(2)}) copy-start(f32[4]{0:T(128)} %param.28) | copy-start | bytes 52
  10.5 4.8 %collective-permute-start.2 = (f32[4,128]{1,0:T(4,128)S(1)}, f32[4,128]{1,0:T(4,128)S(1)}, u32[]{:S(2)}, u32[]{:S(2)}) collective-permute-start(f32[4,128]{1,0:T(4,128)S(1)} %get-tuple-element.46), channel_id=1, source_target_pairs={{0,1},{1,0},{2,3},{3,2},{4,5},{5,4},{6,7},{7,6},{8,9},{9,8},{10,11... | collective-permute-start | bytes 6152 | tf_op jit(solution)/shard_map/ppermute | solution.py:479
  14.5 0.8 %collective-permute-start.3 = (f32[4,128]{1,0:T(4,128)S(1)}, f32[4,128]{1,0:T(4,128)S(1)}, u32[]{:S(2)}, u32[]{:S(2)}) collective-permute-start(f32[4,128]{1,0:T(4,128)S(1)} %get-tuple-element.47), channel_id=1, source_target_pairs={{1,2},{3,4},{5,6},{7,8},{9,10},{11,12},{13,14},{15,16},{17,18},{19... | collective-permute-start | bytes 6152 | tf_op jit(solution)/shard_map/ppermute | solution.py:479
  15.6 5.7 %collective-permute-start.4 = (f32[4,128]{1,0:T(4,128)S(1)}, f32[4,128]{1,0:T(4,128)S(1)}, u32[]{:S(2)}, u32[]{:S(2)}) collective-permute-start(f32[4,128]{1,0:T(4,128)S(1)} %get-tuple-element.50), channel_id=1, source_target_pairs={{0,1},{1,0},{2,3},{3,2},{4,5},{5,4},{6,7},{7,6},{8,9},{9,8},{10,11... | collective-permute-start | bytes 6152 | tf_op jit(solution)/shard_map/ppermute | solution.py:479
  19.8 1.5 %collective-permute-start.5 = (f32[4,128]{1,0:T(4,128)S(1)}, f32[4,128]{1,0:T(4,128)S(1)}, u32[]{:S(2)}, u32[]{:S(2)}) collective-permute-start(f32[4,128]{1,0:T(4,128)S(1)} %get-tuple-element.51), channel_id=1, source_target_pairs={{1,2},{3,4},{5,6},{7,8},{9,10},{11,12},{13,14},{15,16},{17,18},{19... | collective-permute-start | bytes 6152 | tf_op jit(solution)/shard_map/ppermute | solution.py:479
  23.4 7.2 %collective-permute-start.6 = (f32[4,128]{1,0:T(4,128)S(1)}, f32[4,128]{1,0:T(4,128)S(1)}, u32[]{:S(2)}, u32[]{:S(2)}) collective-permute-start(f32[4,128]{1,0:T(4,128)S(1)} %get-tuple-element.54), channel_id=1, source_target_pairs={{0,1},{1,0},{2,3},{3,2},{4,5},{5,4},{6,7},{7,6},{8,9},{9,8},{10,11... | collective-permute-start | bytes 6152 | tf_op jit(solution)/shard_map/ppermute | solution.py:479
  27.5 2.2 %copy-start.3 = (f32[56,128]{1,0:T(8,128)S(1)}, f32[56,128]{1,0:T(8,128)}, u32[]{:S(2)}) copy-start(f32[56,128]{1,0:T(8,128)} %get-tuple-element.59.b_last_ref) | copy-start | bytes 86020
  27.5 3.1 %collective-permute-start.7 = (f32[4,128]{1,0:T(4,128)S(1)}, f32[4,128]{1,0:T(4,128)S(1)}, u32[]{:S(2)}, u32[]{:S(2)}) collective-permute-start(f32[4,128]{1,0:T(4,128)S(1)} %get-tuple-element.55), channel_id=1, source_target_pairs={{1,2},{3,4},{5,6},{7,8},{9,10},{11,12},{13,14},{15,16},{17,18},{19... | collective-permute-start | bytes 6152 | tf_op jit(solution)/shard_map/ppermute | solution.py:479

commit v3 on v2

v3 whole, which is shorter than its diff:
```python
import functools
import math

import jax
import jax.numpy as jnp
from jax import lax
from jax.experimental import pallas as pl
from jax.experimental.pallas import tpu as pltpu
from jax.sharding import PartitionSpec as P

STEPS = 2
FREQ = 4
LANES = 128
AXES = ("grp", "dom")

time_step = 0.25

HALF_SINE = (
    4.442865965050709 * (1 - 1e-7),
    -7.307366951967784 * (1 - 1e-7),
    3.594064346893813 * (1 - 1e-7),
    -0.7824719355799322 * (1 - 1e-7),
)
TWO = 2.0000004768371582

PARAMS = pltpu.CompilerParams(vmem_limit_bytes=48 * 1024 * 1024)
VMEM_SPEC = pl.BlockSpec(memory_space=pltpu.VMEM)
SMEM_SPEC = pl.BlockSpec(memory_space=pltpu.SMEM)
HBM_SPEC = pl.BlockSpec(memory_space=pltpu.HBM)


def fetch(pairs, sems):
    copies = [
        pltpu.make_async_copy(source, target, sems.at[at])
        for at, (source, target) in enumerate(pairs)
    ]
    for copy in copies:
        copy.start()
    for copy in copies:
        copy.wait()


def lookup(table_ref, first, last, index):
    asked = index.shape[0]
    if asked < 8:
        index = jnp.concatenate([index] * (8 // asked), 0)
    row_of = lax.shift_right_logical(index, 7)
    lane_of = lax.bitwise_and(index, LANES - 1)
    found = jnp.zeros(index.shape, jnp.float32)
    for row in range(first, last):
        line = jnp.broadcast_to(table_ref[row : row + 1, :], index.shape)
        hit = jnp.take_along_axis(line, lane_of, axis=1, mode="promise_in_bounds")
        found = jnp.where(row_of == row, hit, found)
    return found[:asked]


def spread(index, values, rows):
    padded = -(-rows // 16) * 16
    one = jnp.ones((), jnp.bfloat16)
    zero = jnp.zeros((), jnp.bfloat16)
    row_of = lax.shift_right_logical(index, 7).astype(jnp.int16)
    lane_of = lax.bitwise_and(index, LANES - 1).astype(jnp.int16)
    high = values.astype(jnp.bfloat16)
    low = (values - high.astype(jnp.float32)).astype(jnp.bfloat16)
    row_iota = lax.broadcasted_iota(jnp.int32, (padded, LANES), 0).astype(jnp.int16)
    lane_iota = lax.broadcasted_iota(jnp.int32, (LANES, LANES), 0).astype(jnp.int16)
    lefts = []
    rights = []
    for at in range(index.shape[0]):
        span = slice(at, at + 1)
        hit = row_iota == jnp.broadcast_to(row_of[span], (padded, LANES))
        left = [
            jnp.where(hit, jnp.broadcast_to(part[span], (padded, LANES)), zero)
            for part in (high, low)
        ]
        lefts.append(jnp.concatenate(left, 0))
        rights.append(
            jnp.where(lane_iota == jnp.broadcast_to(lane_of[span], (LANES, LANES)), one, zero)
        )
    both = lax.dot_general(
        jnp.concatenate(lefts, 1),
        jnp.concatenate(rights, 1),
        (((1,), (1,)), ((), ())),
        preferred_element_type=jnp.float32,
    )
    return both[:rows] + both[padded : padded + rows]


def lookup_row(table_ref, index):
    rows = table_ref.shape[0]
    row_of = lax.shift_right_logical(index, 7)
    lane_of = jnp.broadcast_to(lax.bitwise_and(index, LANES - 1), (8, LANES))
    iota = lax.broadcasted_iota(jnp.int32, (8, LANES), 0)
    found = jnp.zeros((8, LANES), jnp.float32)
    for row in range(0, rows, 8):
        hit = jnp.take_along_axis(
            table_ref[row : row + 8, :], lane_of, axis=1, mode="promise_in_bounds"
        )
        found = jnp.where(iota + row == row_of, hit, found)
    return jnp.sum(found, axis=0, keepdims=True)


def neighbours(flags_ref, got_a_ref, got_b_ref):
    even = flags_ref[0] == 1
    got_a = got_a_ref[...]
    got_b = got_b_ref[...]
    return jnp.where(even, got_b, got_a), jnp.where(even, got_a, got_b)


class Greeting:
    def __init__(self, rows, halo):
        self.edges = rows[0:halo]
        self.eps = rows[halo : 2 * halo]
        self.send_next = rows[2 * halo : 3 * halo].astype(jnp.int32)
        self.send_prev = rows[3 * halo : 4 * halo].astype(jnp.int32)
        self.huy_edge = rows[4 * halo : 4 * halo + 1].astype(jnp.int32)
        self.huy_eps = rows[4 * halo + 1 : 4 * halo + 2]


def greeting_rows(halo):
    return -(-(4 * halo + 2) // 8) * 8


def first_kernel(
    flags_ref,
    e_hbm,
    eps_hbm,
    next_hbm,
    prev_hbm,
    edge_hbm,
    live_hbm,
    send_a_ref,
    send_b_ref,
    e_ref,
    eps_ref,
    lists_ref,
    edge_ref,
    live_ref,
    sems,
):
    half = next_hbm.shape[0]
    fetch(
        [
            (e_hbm, e_ref),
            (eps_hbm, eps_ref),
            (next_hbm, lists_ref.at[pl.ds(0, half)]),
            (prev_hbm, lists_ref.at[pl.ds(half, half)]),
            (edge_hbm, edge_ref),
            (live_hbm, live_ref),
        ],
        sems,
    )
    even = flags_ref[0] == 1
    lists = lists_ref[...]
    e_found = lookup(e_ref, 0, e_ref.shape[0], lists)
    eps_found = lookup(eps_ref, 0, eps_ref.shape[0], lists)
    edge_ids = edge_ref[...]
    live_eps = lookup_row(eps_ref, edge_ids) * live_ref[...].astype(jnp.float32)
    both = [lists.astype(jnp.float32), edge_ids.astype(jnp.float32), live_eps]
    spare = send_a_ref.shape[0] - 4 * half - 2
    both.append(jnp.zeros((spare, LANES), jnp.float32))
    to_next = jnp.concatenate([e_found[:half], eps_found[:half]] + both, 0)
    to_prev = jnp.concatenate([e_found[half:], eps_found[half:]] + both, 0)
    send_a_ref[...] = jnp.where(even, to_next, to_prev)
    send_b_ref[...] = jnp.where(even, to_prev, to_next)


def own_curl(table_ref, own_rows, index_ref, signs_ref, curl_ref):
    face_rows = curl_ref.shape[0]
    for at in range(0, face_rows, 8):
        curl = None
        for k in range(3):
            span = slice(k * face_rows + at, k * face_rows + at + 8)
            term = signs_ref[span, :] * lookup(table_ref, 0, own_rows, index_ref[span, :])
            curl = term if curl is None else curl + term
        curl_ref[at : at + 8, :] = curl


def prepare_kernel(
    flags_ref,
    wave_ref,
    e_ref,
    edges_hbm,
    signs_hbm,
    b_hbm,
    mu_hbm,
    face_hbm,
    geom_hbm,
    acc_hbm,
    angles_hbm,
    index_ref,
    signs_ref,
    curl_ref,
    b_ref,
    mu_ref,
    face_ref,
    geom_ref,
    acc_ref,
    dirs_ref,
    raw_edges,
    raw_signs,
    raw_angles,
    sems,
):
    width = dirs_ref.shape[1]
    if angles_hbm.shape[1] == width:
        angles = angles_hbm
    else:
        angles = angles_hbm.at[:, pl.ds(pl.multiple_of(flags_ref[3] * width, LANES), width)]
    fetch(
        [
            (edges_hbm, raw_edges),
            (signs_hbm, raw_signs),
            (b_hbm, b_ref),
            (mu_hbm, mu_ref),
            (face_hbm, face_ref),
            (geom_hbm, geom_ref),
            (acc_hbm, acc_ref),
            (angles, raw_angles),
        ],
        sems,
    )
    face_rows = b_ref.shape[0]
    for k in range(3):
        for at in range(face_rows):
            lanes = slice(at * LANES, (at + 1) * LANES)
            to = k * face_rows + at
            index_ref[to : to + 1, :] = raw_edges[k : k + 1, lanes]
            signs_ref[to : to + 1, :] = raw_signs[k : k + 1, lanes].astype(jnp.float32)
    own_curl(e_ref, e_ref.shape[0], index_ref, signs_ref, curl_ref)
    polar = raw_angles[0:1, :]
    azimuth = raw_angles[1:2, :]
    sine = jnp.sin(polar)
    dirs_ref[0:1, :] = sine * jnp.cos(azimuth)
    dirs_ref[1:2, :] = sine * jnp.sin(azimuth)
    dirs_ref[2:3, :] = jnp.cos(polar)
    dirs_ref[3:8, :] = jnp.zeros((5, width), jnp.float32)


def faces_update(
    table_ref, first, last, index_ref, signs_ref, curl_ref, b_ref, mu_ref, b_out_ref
):
    face_rows = b_ref.shape[0]
    total = jnp.zeros((last, LANES), jnp.float32)
    for at in range(0, face_rows, 8):
        spans = [slice(k * face_rows + at, k * face_rows + at + 8) for k in range(3)]
        curl = None if curl_ref is None else curl_ref[at : at + 8, :]
        for span in spans:
            term = signs_ref[span, :] * lookup(table_ref, first, last, index_ref[span, :])
            curl = term if curl is None else curl + term
        b_new = b_ref[at : at + 8, :] - time_step * curl
        b_out_ref[at : at + 8, :] = b_new
        scaled = mu_ref[at : at + 8, :] * b_new
        total = total + spread(
            jnp.concatenate([index_ref[span, :] for span in spans], 0),
            jnp.concatenate([signs_ref[span, :] * scaled for span in spans], 0),
            last,
        )
    return total


def clear(ref, first):
    rows = ref.shape[1] - first

    def body(at, none):
        ref[at, first:, :] = jnp.zeros((rows, LANES), jnp.float32)
        return none

    lax.fori_loop(0, ref.shape[0], body, 0, unroll=8)


def first_step_kernel(
    flags_ref,
    got_a_ref,
    got_b_ref,
    index_ref,
    signs_ref,
    curl_ref,
    b_ref,
    mu_ref,
    e_ref,
    eps_ref,
    lists_ref,
    b_out_ref,
    part_ref,
    near_ref,
    send_ref,
    table_ref,
    left_ref,
    right_ref,
):
    me = flags_ref[1]
    parts = send_ref.shape[0]
    own = e_ref.shape[0]
    halo = lists_ref.shape[0] // 2
    rows = own + 2 * halo
    from_prev, from_next = neighbours(flags_ref, got_a_ref, got_b_ref)
    prev = Greeting(from_prev, halo)
    after = Greeting(from_next, halo)
    table_ref[own : own + halo, :] = prev.edges
    table_ref[own + halo : rows, :] = after.edges
    total = faces_update(
        table_ref, own, rows, index_ref, signs_ref, curl_ref, b_ref, mu_ref, b_out_ref
    )
    to_prev = total[own : own + halo]
    to_next = total[own + halo :]
    part_ref[...] = e_ref[...] + time_step * eps_ref[...] * total[:own]
    known = lookup(part_ref, 0, own, lists_ref[...])
    left_ref[...] = spread(prev.send_next, to_prev, own)
    right_ref[...] = spread(after.send_prev, to_next, own)
    lefts = lookup(left_ref, 0, own, jnp.concatenate([prev.send_next, prev.send_prev], 0))
    rights = lookup(right_ref, 0, own, jnp.concatenate([after.send_prev, after.send_next], 0))
    near_ref[...] = jnp.concatenate([lefts[:halo], rights[:halo]], 0)
    clear(send_ref, 0)

    @pl.when(me >= 1)
    def _():
        send_ref[me - 1] = jnp.concatenate([to_prev, known[halo:]], 0)

    @pl.when(me + 1 < parts)
    def _():
        send_ref[me + 1] = jnp.concatenate([to_next, known[:halo]], 0)

    @pl.when(me >= 2)
    def _():
        send_ref[me - 2, 0:halo, :] = lefts[halo:]

    @pl.when(me + 2 < parts)
    def _():
        send_ref[me + 2, 0:halo, :] = rights[halo:]


def arrived(ref, me, by, first, last):
    parts = ref.shape[0]
    there = jnp.logical_and(me + by >= 0, me + by < parts)
    at = jnp.clip(me + by, 0, parts - 1)
    return jnp.where(there, ref[at, first:last, :], 0.0)


def second_step_kernel(
    flags_ref,
    coef_ref,
    got_a_ref,
    got_b_ref,
    shares_ref,
    part_ref,
    near_ref,
    eps_ref,
    lists_ref,
    index_ref,
    signs_ref,
    b_ref,
    mu_ref,
    face_ref,
    edge_ref,
    live_ref,
    geom_ref,
    acc_ref,
    b_out_ref,
    part_out_ref,
    send_ref,
    table_ref,
    e_ref,
    left_ref,
    right_ref,
    block_ref,
    dom_size,
):
    me = flags_ref[1]
    parts = send_ref.shape[0]
    own = part_ref.shape[0]
    halo = lists_ref.shape[0] // 2
    rows = own + 2 * halo
    from_prev, from_next = neighbours(flags_ref, got_a_ref, got_b_ref)
    prev = Greeting(from_prev, halo)
    after = Greeting(from_next, halo)
    back = jnp.concatenate(
        [arrived(shares_ref, me, 1, 0, halo), arrived(shares_ref, me, -1, 0, halo)], 0
    )
    e_new = part_ref[...] + time_step * eps_ref[...] * spread(lists_ref[...], back, own)
    e_ref[...] = e_new
    table_ref[0:own, :] = e_new
    table_ref[own : own + halo, :] = arrived(shares_ref, me, -1, halo, 2 * halo) + (
        time_step * prev.eps * (arrived(shares_ref, me, -2, 0, halo) + near_ref[0:halo, :])
    )
    table_ref[own + halo : rows, :] = arrived(shares_ref, me, 1, halo, 2 * halo) + (
        time_step * after.eps * (arrived(shares_ref, me, 2, 0, halo) + near_ref[halo:, :])
    )
    total = faces_update(
        table_ref, 0, rows, index_ref, signs_ref, None, b_ref, mu_ref, b_out_ref
    )
    to_prev = total[own : own + halo]
    to_next = total[own + halo :]
    part_out_ref[...] = e_new + time_step * eps_ref[...] * total[:own]
    left_ref[...] = spread(prev.send_next, to_prev, own)
    right_ref[...] = spread(after.send_prev, to_next, own)
    to_left = lookup_row(left_ref, prev.huy_edge) * (time_step * prev.huy_eps)
    to_right = lookup_row(right_ref, after.huy_edge) * (time_step * after.huy_eps)
    faces = face_ref[...]
    edges = edge_ref[...]
    samples = (
        (lookup_row(b_ref, faces), lookup_row(b_out_ref, faces)),
        (lookup_row(e_ref, edges), lookup_row(part_out_ref, edges)),
    )
    live = live_ref[...].astype(jnp.float32)
    normal = geom_ref[0:3, :]
    for q in range(FREQ):
        values = []
        for kind in range(2):
            for part in range(2):
                at = 2 * q + part
                row = 2 * FREQ * kind + at
                value = acc_ref[row : row + 1, :]
                for step in range(STEPS):
                    value = value + coef_ref[step, at] * samples[kind][step]
                values.append(value * live)
        block_ref[q] = jnp.concatenate(
            [
                normal * values[0],
                normal * values[1],
                geom_ref[3:6, :],
                values[2],
                values[3],
                to_left,
                geom_ref[6:9, :],
                to_right,
            ],
            0,
        )
    blocks = dom_size // FREQ

    def body(at, none):
        send_ref[at, 0:16, :] = block_ref[lax.rem(at, dom_size) // blocks]
        return none

    lax.fori_loop(0, parts, body, 0, unroll=8)
    clear(send_ref, 16)

    @pl.when(me >= 1)
    def _():
        send_ref[me - 1, 16 : 16 + halo, :] = to_prev

    @pl.when(me + 1 < parts)
    def _():
        send_ref[me + 1, 16 : 16 + halo, :] = to_next


def three(value):
    high = value.astype(jnp.bfloat16).astype(jnp.float32)
    middle = (value - high).astype(jnp.bfloat16).astype(jnp.float32)
    return high, middle, value - high - middle


def waves(turns):
    f = turns - jnp.round(turns)
    s = f * f
    half = HALF_SINE[3] * s + HALF_SINE[2]
    half = half * s + HALF_SINE[1]
    half = half * s + HALF_SINE[0]
    half = half * f
    square = half * half
    rest = TWO - square
    cosine = 1.0 - square
    sine = half * (rest * lax.rsqrt(rest))
    return cosine.astype(jnp.bfloat16), sine.astype(jnp.bfloat16)


def cross(left, right):
    return [
        left[1] * right[2] - left[2] * right[1],
        left[2] * right[0] - left[0] * right[2],
        left[0] * right[1] - left[1] * right[0],
    ]


def far_kernel(
    flags_ref,
    coef_ref,
    wave_ref,
    share_ref,
    dirs_ref,
    part_ref,
    eps_ref,
    lists_ref,
    e_out_ref,
    power_ref,
    left_ref,
    wave_a,
    wave_b,
    group,
    rows,
    cols,
    scale,
):
    me = flags_ref[1]
    freq = flags_ref[2]
    halo = lists_ref.shape[0] // 2
    back = jnp.concatenate(
        [arrived(share_ref, me, 1, 16, 16 + halo), arrived(share_ref, me, -1, 16, 16 + halo)], 0
    )
    e_out_ref[...] = part_ref[...] + time_step * eps_ref[...] * spread(
        lists_ref[...], back, part_ref.shape[0]
    )
    sources = share_ref.shape[0]
    width = dirs_ref.shape[1]
    dirs = [dirs_ref[i : i + 1, :] for i in range(3)]
    turns = wave_ref[freq] * (0.5 / math.pi)
    scaled = jnp.concatenate(
        [jnp.zeros((4, width), jnp.float32)]
        + [one * turns for one in dirs]
        + [jnp.zeros((1, width), jnp.float32)],
        0,
    )
    t1, t2, t3 = three(scaled)
    right = jnp.concatenate([t1, t2, t3, t1, t2, t1], 0).astype(jnp.bfloat16)
    real = coef_ref[STEPS - 1, 2 * freq]
    imag = coef_ref[STEPS - 1, 2 * freq + 1]
    blocks = sources // group
    chunks = group * LANES // rows
    pieces = [(low, min(low + cols, 2 * width)) for low in range(0, 2 * width, cols)]
    per_chunk = -(-len(pieces) // chunks)

    def centres(at):
        for one in range(group):
            u1, u2, u3 = three(share_ref[at * group + one, 8:16, :])
            stack = jnp.concatenate([u1, u1, u1, u2, u2, u3], 0)
            left_ref[one * LANES : (one + 1) * LANES, :] = stack.T.astype(jnp.bfloat16)

    def project(chunk):
        left = left_ref[chunk * rows : (chunk + 1) * rows, :]
        return jnp.dot(left, right, preferred_element_type=jnp.float32)

    def currents(at):
        pieces = []
        for one in range(group):
            source = at * group + one
            share = share_ref[source, 0:16, :]
            late = arrived(share_ref, source, 1, 11, 12) + arrived(share_ref, source, -1, 15, 16)
            tangent = share[6:9]
            pieces.append(
                jnp.concatenate(
                    [
                        share[0:6],
                        tangent * (share[9:10] + real * late),
                        tangent * (share[10:11] + imag * late),
                        jnp.zeros((4, LANES), jnp.float32),
                    ],
                    0,
                )
            )
        return jnp.concatenate(pieces, 1).astype(jnp.bfloat16)

    def collect(current, source, total, piece):
        low, high = pieces[piece]
        return total + jnp.dot(current, source[:, low:high], preferred_element_type=jnp.float32)

    def half(next_at, done_at, target, source, totals):
        totals = list(totals)
        current = currents(done_at)
        ahead = project(0)
        for chunk in range(chunks):
            theta = ahead
            if chunk + 1 < chunks:
                ahead = project(chunk + 1)
            cosine, sine = waves(theta)
            target[chunk * rows : (chunk + 1) * rows, 0:width] = cosine
            target[chunk * rows : (chunk + 1) * rows, width : 2 * width] = sine
            for piece in range(chunk * per_chunk, min((chunk + 1) * per_chunk, len(pieces))):
                totals[piece] = collect(current, source, totals[piece], piece)
        centres(next_at)
        return totals

    def body(at, totals):
        totals = half(2 * at + 1, jnp.maximum(2 * at - 1, 0), wave_a, wave_b, totals)
        return tuple(half(jnp.minimum(2 * at + 2, blocks - 1), 2 * at, wave_b, wave_a, totals))

    centres(0)
    wave_b[...] = jnp.zeros_like(wave_b)
    totals = tuple(jnp.zeros((16, high - low), jnp.float32) for low, high in pieces)
    totals = lax.fori_loop(0, blocks // 2, body, totals)
    current = currents(blocks - 1)
    total = jnp.concatenate(
        [collect(current, wave_b, total, piece) for piece, total in enumerate(totals)], 1
    )

    def p_row(at):
        return total[at : at + 1, 0:width]

    def q_row(at):
        return total[at : at + 1, width : 2 * width]

    n_real = [p_row(i) - q_row(3 + i) for i in range(3)]
    n_imag = [q_row(i) + p_row(3 + i) for i in range(3)]
    l_real = [p_row(6 + i) - q_row(9 + i) for i in range(3)]
    l_imag = [q_row(6 + i) + p_row(9 + i) for i in range(3)]
    power = jnp.zeros((1, width), jnp.float32)
    for n_part, l_part in ((n_real, l_real), (n_imag, l_imag)):
        outer = cross(dirs, cross(dirs, n_part))
        inner = cross(dirs, l_part)
        for i in range(3):
            gap = outer[i] - inner[i]
            power = power + gap * gap
    power_ref[...] = power * scale


def call(kernel, scalars, arrays, outs, scratch=(), name=None, far_arrays=()):
    return pl.pallas_call(
        kernel,
        out_shape=[jax.ShapeDtypeStruct(shape, kind) for shape, kind in outs],
        in_specs=[SMEM_SPEC] * len(scalars)
        + [VMEM_SPEC] * len(arrays)
        + [HBM_SPEC] * len(far_arrays),
        out_specs=[VMEM_SPEC] * len(outs),
        scratch_shapes=list(scratch),
        compiler_params=PARAMS,
        name=name,
    )(
        *scalars,
        *arrays,
        *[pltpu.with_memory_space_constraint(one, pltpu.HBM) for one in far_arrays],
    )


def per_device(
    e_field,
    b_field,
    face_edges,
    face_signs,
    send_prev,
    send_next,
    eps_inv,
    mu_inv,
    huy_face,
    huy_edge,
    huy_live,
    huy_geom,
    huy_acc,
    wavenum,
    angles,
):
    grp_size = lax.axis_size("grp")
    dom_size = lax.axis_size("dom")
    parts = grp_size * dom_size
    me = lax.axis_index(AXES)
    place = lax.axis_index("dom")
    blocks = dom_size // FREQ
    width = angles.shape[1] // blocks
    flags = jnp.stack([1 - me % 2, me, place // blocks, place % blocks]).astype(jnp.int32)
    pairs_a = [(i, i ^ 1) for i in range(parts)]
    pairs_b = [(i, i + 1) for i in range(1, parts - 1, 2)]
    pairs_b = pairs_b + [(j, i) for i, j in pairs_b]

    def table(array):
        return array.reshape(-1, LANES)

    def f32(*shape):
        return (shape, jnp.float32)

    def i32(*shape):
        return (shape, jnp.int32)

    def scratch(*shape, kind=jnp.float32):
        return pltpu.VMEM(shape, kind)

    own = e_field.shape[0] // LANES
    halo = send_next.shape[0] // LANES
    faces = b_field.shape[0] // LANES
    rows = own + 2 * halo
    greeting = greeting_rows(halo)
    moments = time_step * jnp.arange(1, STEPS + 1, dtype=jnp.float32)
    phase = moments[:, None] * wavenum[None, :]
    coef = jnp.stack([jnp.cos(phase), -jnp.sin(phase)], 2).reshape(STEPS, 2 * FREQ)
    if width % LANES:
        angles = lax.dynamic_slice_in_dim(angles, (place % blocks) * width, width, axis=1)

    send_a, send_b, e_table, eps_table, lists, edge_ids, live = call(
        first_kernel,
        [flags],
        [],
        [
            f32(greeting, LANES),
            f32(greeting, LANES),
            f32(own, LANES),
            f32(own, LANES),
            i32(2 * halo, LANES),
            i32(1, LANES),
            i32(1, LANES),
        ],
        [pltpu.SemaphoreType.DMA((6,))],
        name="first",
        far_arrays=[
            table(e_field),
            table(eps_inv),
            table(send_next),
            table(send_prev),
            table(huy_edge),
            table(huy_live),
        ],
    )
    got_a = lax.ppermute(send_a, AXES, pairs_a)
    got_b = lax.ppermute(send_b, AXES, pairs_b)
    index, signs, curl, b_table, mu_table, face_ids, geom, acc, dirs = call(
        prepare_kernel,
        [flags, wavenum],
        [e_table],
        [
            i32(3 * faces, LANES),
            f32(3 * faces, LANES),
            f32(faces, LANES),
            f32(faces, LANES),
            f32(faces, LANES),
            i32(1, LANES),
            f32(*huy_geom.shape),
            f32(*huy_acc.shape),
            f32(8, width),
        ],
        [
            scratch(*face_edges.shape, kind=jnp.int32),
            scratch(*face_signs.shape, kind=jnp.int32),
            scratch(2, width),
            pltpu.SemaphoreType.DMA((8,)),
        ],
        name="prepare",
        far_arrays=[
            face_edges,
            face_signs,
            table(b_field),
            table(mu_inv),
            table(huy_face),
            huy_geom,
            huy_acc,
            angles,
        ],
    )
    b_table, part, near, send = call(
        first_step_kernel,
        [flags],
        [got_a, got_b, index, signs, curl, b_table, mu_table, e_table, eps_table, lists],
        [f32(faces, LANES), f32(own, LANES), f32(2 * halo, LANES), f32(parts, 2 * halo, LANES)],
        [scratch(rows, LANES), scratch(own, LANES), scratch(own, LANES)],
        name="first_step",
    )
    shares = lax.all_to_all(send, AXES, 0, 0, tiled=True)
    b_table, part, send = call(
        functools.partial(second_step_kernel, dom_size=dom_size),
        [flags, coef],
        [got_a, got_b, shares, part, near, eps_table, lists, index, signs, b_table, mu_table]
        + [face_ids, edge_ids, live, geom, acc],
        [f32(faces, LANES), f32(own, LANES), f32(parts, 24, LANES)],
        [
            scratch(rows, LANES),
            scratch(own, LANES),
            scratch(own, LANES),
            scratch(own, LANES),
            scratch(FREQ, 16, LANES),
        ],
        name="second_step",
    )
    shares = lax.all_to_all(send, AXES, 0, 0, tiled=True)
    group = 4
    e_table, power = call(
        functools.partial(far_kernel, group=group, rows=64, cols=256, scale=1.0 / (LANES * parts)),
        [flags, coef, wavenum],
        [shares, dirs, part, eps_table, lists],
        [f32(own, LANES), f32(1, width)],
        [
            scratch(group * LANES, 48, kind=jnp.bfloat16),
            scratch(group * LANES, 2 * width, kind=jnp.bfloat16),
            scratch(group * LANES, 2 * width, kind=jnp.bfloat16),
        ],
        name="far",
    )
    power = lax.all_to_all(
        jnp.broadcast_to(power, (dom_size, width)), "dom", 0, 0, tiled=True
    ).reshape(FREQ, blocks * width)
    return (e_table.reshape(-1), b_table.reshape(-1), power)


def solution(mesh):
    return jax.shard_map(
        per_device,
        mesh=mesh,
        in_specs=(
            P(("grp", "dom")),
            P(("grp", "dom")),
            P(None, ("grp", "dom")),
            P(None, ("grp", "dom")),
            P(("grp", "dom")),
            P(("grp", "dom")),
            P(("grp", "dom")),
            P(("grp", "dom")),
            P(("grp", "dom")),
            P(("grp", "dom")),
            P(("grp", "dom")),
            P(None, ("grp", "dom")),
            P(None, ("grp", "dom")),
            P(),
            P(None, "grp"),
        ),
        out_specs=(P(("grp", "dom")), P(("grp", "dom")), P(None, "grp")),
        check_vma=False,
    )
```

time: 76.3 us -> 66.6 us (0.87)
  blocking collectives: 36.9 us -> 24.5 us
  waiting for transfers between devices: 0.04 us -> 7.93 us
  local copies, waits for them, and re-layouts: 6.66 us -> 1.49 us
  Pallas kernels: 14.8 us -> 19.3 us
  starting transfers between devices: 15.5 us -> 12 us
  between operations: 1.65 us -> 0.74 us
    ppermute x8 -> x2, starting transfers between devices: 15.5 us -> 1.17 us  [the longest x1 0.65 us: per_device(): got_b = lax.ppermute(send_b, AXES, pairs_b)]
    all_to_all x1, blocking collectives: 26.9 us -> 14.8 us  [per_device(): shares = lax.all_to_all(send, AXES, 0, 0, tiled=True)]
    all_to_all x0 -> x1, starting transfers between devices: none -> 10.8 us  [per_device(): shares = lax.all_to_all(send, AXES, 0, 0, tiled=True)]
    all_to_all x0 -> x1, waiting for transfers between devices: none -> 7.92 us  [per_device(): shares = lax.all_to_all(send, AXES, 0, 0, tiled=True)]
    unnamed x32 -> x2, local copies, waits for them, and re-layouts: 5.21 us -> 0.65 us
    pallas_call x9 -> x5, Pallas kernels: 14.8 us -> 19.3 us  [call(): pl.pallas_call(kernel, out_shape=[jax.ShapeDtypeStruct(shape, kind) for s...]
  transfers between devices with their start and end apart: 8 -> 3, of which waited for: 0 -> 1; matrix products, arithmetic and copies ran while one was open for 1% -> 0% of each run, Pallas kernels for 4% -> 4%
where the time goes in v3:
time: 66.6 us; the launch traced here: 66.2 us
  blocking collectives  24.5 us (37%)
  Pallas kernels  19.3 us (29%)
  starting transfers between devices  12 us (18%)
  waiting for transfers between devices  7.93 us (12%)
  local copies, waits for them, and re-layouts  1.49 us (2%)
  between operations  0.74 us (1%)
    pallas_call x5, Pallas kernels, call(): pl.pallas_call(kernel, out_shape=[jax.ShapeDtypeStruct(shape, kind) for s...  19.3 us
    all_to_all x1, blocking collectives, per_device(): shares = lax.all_to_all(send, AXES, 0, 0, tiled=True)  14.8 us
    all_to_all x1, starting transfers between devices, per_device(): shares = lax.all_to_all(send, AXES, 0, 0, tiled=True)  10.8 us
    all_to_all x1, blocking collectives, per_device(): lax.all_to_all(jnp.broadcast_to(power, (dom_size, width)), 'dom', 0, 0, t...  9.76 us
    all_to_all x1, waiting for transfers between devices, per_device(): shares = lax.all_to_all(send, AXES, 0, 0, tiled=True)  7.92 us
  transfers between devices with their start and end apart: 3, of which 1 were waited for; matrix products, arithmetic and copies ran while one was open for 0% of the time, Pallas kernels for 4%

profile of v3, /device:TPU:0, one launch (start us, length us, event | category | flops | bytes accessed | tf_op | source)
XLA Modules:
  0.0 66.2 jit_solution(4804687398397367850)
XLA Ops:
  0.7 0.1 pad_add_fusion.flags_ref
  0.7 1.5 %first.1 = (f32[24,128]{1,0:T(8,128)S(1)}, f32[24,128]{1,0:T(8,128)S(1)}, f32[32,128]{1,0:T(8,128)S(1)}, f32[32,128]{1,0:T(8,128)S(1)}, s32[8,128]{1,0:T(8,128)S...) custom-call(s32[4]{0:T(128)S(1)} %pad_add_fusion.flags_ref, f32[32,128]{1,0:T(8,128)} %bitcast.19, f32[32,128]{1,0:T(8,128)} %bitcast.20, ...), custom_call_target="tpu_custom_call" | custom-call | tf_op jit(solution)/shard_map/first/pallas_call | solution.py:607
  2.2 0.5 collective-permute-start
  2.7 0.7 collective-permute-start.1
  3.4 0.0 copy-start
  3.4 0.6 copy-done
  4.1 2.4 %prepare.1 = (s32[168,128]{1,0:T(8,128)S(1)}, f32[168,128]{1,0:T(8,128)S(1)}, f32[56,128]{1,0:T(8,128)S(1)}, f32[56,128]{1,0:T(8,128)S(1)}, f32[56,128]{1,0:T(8,...) custom-call(s32[4]{0:T(128)S(1)} %pad_add_fusion.flags_ref, ...), custom_call_target="tpu_custom_call" | custom-call | tf_op jit(solution)/shard_map/prepare/pallas_call | solution.py:607
  6.5 0.0 collective-permute-done.got_a_ref
  6.5 0.0 collective-permute-done.1.got_b_ref
  6.5 3.3 %first_step.1 = (f32[56,128]{1,0:T(8,128)S(1)}, f32[32,128]{1,0:T(8,128)S(1)}, f32[8,128]{1,0:T(8,128)S(1)}, f32[32,8,128]{2,1,0:T(8,128)}) custom-call(s32[4]{0:T(128)S(1)} %pad_add_fusion.flags_ref, f32[24,128]{1,0:T(8,128)S(1)} %collective-permute-done.got_a_ref, f32[24,128]{1,0:T(8,128)S(1)} %collective-permute-done.1.got_b_ref, ...), custom_call_target="tpu_custom_call" | custom-call | tf_op jit(solution)/shard_map/first_step/pallas_call | solution.py:607
  9.9 10.8 %all-to-all-start = ((f32[32,8,128]{2,1,0:T(8,128)}), f32[32,8,128]{2,1,0:T(8,128)S(1)}, u32[]{:S(2)}, u32[]{:S(2)}) async-start(f32[32,8,128]{2,1,0:T(8,128)} %get-tuple-element.38), calls=%async_computation | async-start | bytes 262144 | tf_op jit(solution)/shard_map/all_to_all | solution.py:743
  20.7 0.1 multiply_cosine_fusion
  20.8 0.1 copy.18
  20.9 0.1 reshape.145.coef_ref
  21.0 7.9 %all-to-all-done.shares_ref = f32[32,8,128]{2,1,0:T(8,128)S(1)} async-done(((f32[32,8,128]{2,1,0:T(8,128)}), f32[32,8,128]{2,1,0:T(8,128)S(1)}, u32[]{:S(2)}, u32[]{:S(2)}) %all-to-all-start) | async-done | bytes 131104 | tf_op jit(solution)/shard_map/all_to_all | solution.py:743
  28.9 4.7 %second_step.1 = (f32[56,128]{1,0:T(8,128)}, f32[32,128]{1,0:T(8,128)S(1)}, f32[32,24,128]{2,1,0:T(8,128)S(1)}) custom-call(s32[4]{0:T(128)S(1)} %pad_add_fusion.flags_ref, f32[2,8]{1,0:T(2,128)S(1)} %reshape.145.coef_ref, f32[24,128]{1,0:T(8,128)S(1)} %collective-permute-done.got_a_ref, f32[24,128]{1,0:T(8,128)S(1)} %collective-permute-done.1.got_b_ref, ...), custom_call_target="tpu_custom_call" | custom-call | tf_op jit(solution)/shard_map/second_step/pallas_call | solution.py:607
  33.7 14.8 %all_to_all.16.share_ref = f32[32,24,128]{2,1,0:T(8,128)S(1)} all-to-all(f32[32,24,128]{2,1,0:T(8,128)S(1)} %get-tuple-element.47), channel_id=1, replica_groups=mesh['grp'=2,'dom'=16] {'grp','dom'}, dimensions={0} | all-to-all | bytes 786432 | tf_op jit(solution)/shard_map/all_to_all | solution.py:759
  48.5 7.3 %far.1 = (f32[32,128]{1,0:T(8,128)}, f32[1,512]{1,0:T(1,128)S(1)}) custom-call(s32[4]{0:T(128)S(1)} %pad_add_fusion.flags_ref, f32[2,8]{1,0:T(2,128)S(1)} %reshape.145.coef_ref, f32[4]{0:T(128)S(1)} %copy-done, f32[32,24,128]{2,1,0:T(8,128)S(1)} %all_to_all.16.share_ref, f32[8,512]{1,0:T(8,128)S(1)} %get-tuple-element.48.dirs_ref, ...), custom_call_target="tpu_custom_call" | custom-call | tf_op jit(solution)/shard_map/far/pallas_call | solution.py:607
  55.7 9.8 %all_to_all.17 = f32[16,1,512]{2,1,0:T(1,128)S(1)} all-to-all(f32[16,1,512]{2,1,0:T(1,128)S(1)} %broadcast_in_dim.2), channel_id=1, replica_groups=mesh['grp'=2,'dom'=16] {'dom'}, dimensions={0} | all-to-all | bytes 65536 | tf_op jit(solution)/shard_map/all_to_all | solution.py:773
  65.5 0.1 reduce
  65.6 0.6 reshape.157
  (3 shorter events, 0.0 us)
Async XLA Ops:
  2.2 4.3 %collective-permute-start = (f32[24,128]{1,0:T(8,128)S(1)}, f32[24,128]{1,0:T(8,128)S(1)}, u32[]{:S(2)}, u32[]{:S(2)}) collective-permute-start(f32[24,128]{1,0:T(8,128)S(1)} %get-tuple-element.28), channel_id=1, source_target_pairs={{0,1},{1,0},{2,3},{3,2},{4,5},{5,4},{6,7},{7,6},{8,9},{9,8},{10,11... | collective-permute-start | bytes 36872 | tf_op jit(solution)/shard_map/ppermute | solution.py:700
  2.7 3.8 %collective-permute-start.1 = (f32[24,128]{1,0:T(8,128)S(1)}, f32[24,128]{1,0:T(8,128)S(1)}, u32[]{:S(2)}, u32[]{:S(2)}) collective-permute-start(f32[24,128]{1,0:T(8,128)S(1)} %get-tuple-element.29), channel_id=1, source_target_pairs={{1,2},{3,4},{5,6},{7,8},{9,10},{11,12},{13,14},{15,16},{17,18},{19... | collective-permute-start | bytes 36872 | tf_op jit(solution)/shard_map/ppermute | solution.py:701
  3.4 0.7 copy-start
  9.9 19.1 %all-to-all-start = ((f32[32,8,128]{2,1,0:T(8,128)}), f32[32,8,128]{2,1,0:T(8,128)S(1)}, u32[]{:S(2)}, u32[]{:S(2)}) async-start(f32[32,8,128]{2,1,0:T(8,128)} %get-tuple-element.38), calls=%async_computation | async-start | bytes 262144 | tf_op jit(solution)/shard_map/all_to_all | solution.py:743

commit v4 on v3

--- a/solution.py
+++ b/solution.py
@@ -23,7 +23,7 @@
 )
 TWO = 2.0000004768371582
 
-PARAMS = pltpu.CompilerParams(vmem_limit_bytes=48 * 1024 * 1024)
+PARAMS = pltpu.CompilerParams(vmem_limit_bytes=40 * 1024 * 1024)
 VMEM_SPEC = pl.BlockSpec(memory_space=pltpu.VMEM)
 SMEM_SPEC = pl.BlockSpec(memory_space=pltpu.SMEM)
 HBM_SPEC = pl.BlockSpec(memory_space=pltpu.HBM)
@@ -178,6 +178,7 @@
 
 def prepare_kernel(
     flags_ref,
+    coef_ref,
     wave_ref,
     e_ref,
     edges_hbm,
@@ -202,6 +203,7 @@
     raw_angles,
     sems,
 ):
+    del coef_ref
     width = dirs_ref.shape[1]
     if angles_hbm.shape[1] == width:
         angles = angles_hbm
@@ -234,7 +236,10 @@
     dirs_ref[0:1, :] = sine * jnp.cos(azimuth)
     dirs_ref[1:2, :] = sine * jnp.sin(azimuth)
     dirs_ref[2:3, :] = jnp.cos(polar)
-    dirs_ref[3:8, :] = jnp.zeros((5, width), jnp.float32)
+    dirs_ref[3:4, :] = jnp.zeros((1, width), jnp.float32)
+    turns = wave_ref[flags_ref[2]] * (0.5 / math.pi)
+    dirs_ref[4:7, :] = dirs_ref[0:3, :] * turns
+    dirs_ref[7:8, :] = jnp.zeros((1, width), jnp.float32)
 
 
 def faces_update(
@@ -259,11 +264,9 @@
     return total
 
 
-def clear(ref, first):
-    rows = ref.shape[1] - first
-
+def fill(ref, block_of):
     def body(at, none):
-        ref[at, first:, :] = jnp.zeros((rows, LANES), jnp.float32)
+        ref[at] = block_of(at)
         return none
 
     lax.fori_loop(0, ref.shape[0], body, 0, unroll=8)
@@ -281,6 +284,7 @@
     e_ref,
     eps_ref,
     lists_ref,
+    geom_ref,
     b_out_ref,
     part_ref,
     near_ref,
@@ -311,15 +315,18 @@
     lefts = lookup(left_ref, 0, own, jnp.concatenate([prev.send_next, prev.send_prev], 0))
     rights = lookup(right_ref, 0, own, jnp.concatenate([after.send_prev, after.send_next], 0))
     near_ref[...] = jnp.concatenate([lefts[:halo], rights[:halo]], 0)
-    clear(send_ref, 0)
+    blank = jnp.zeros((2 * halo, LANES), jnp.float32)
+    gap = jnp.zeros((1, LANES), jnp.float32)
+    place = jnp.concatenate([geom_ref[3:6, :], gap, geom_ref[6:9, :], gap], 0)
+    fill(send_ref, lambda at: jnp.concatenate([blank, place], 0))
 
     @pl.when(me >= 1)
     def _():
-        send_ref[me - 1] = jnp.concatenate([to_prev, known[halo:]], 0)
+        send_ref[me - 1, 0 : 2 * halo, :] = jnp.concatenate([to_prev, known[halo:]], 0)
 
     @pl.when(me + 1 < parts)
     def _():
-        send_ref[me + 1] = jnp.concatenate([to_next, known[:halo]], 0)
+        send_ref[me + 1, 0 : 2 * halo, :] = jnp.concatenate([to_next, known[:halo]], 0)
 
     @pl.when(me >= 2)
     def _():
@@ -418,31 +425,24 @@
             [
                 normal * values[0],
                 normal * values[1],
-                geom_ref[3:6, :],
                 values[2],
                 values[3],
                 to_left,
-                geom_ref[6:9, :],
                 to_right,
+                jnp.zeros((2 + halo, LANES), jnp.float32),
             ],
             0,
         )
     blocks = dom_size // FREQ
-
-    def body(at, none):
-        send_ref[at, 0:16, :] = block_ref[lax.rem(at, dom_size) // blocks]
-        return none
-
-    lax.fori_loop(0, parts, body, 0, unroll=8)
-    clear(send_ref, 16)
+    fill(send_ref, lambda at: block_ref[lax.rem(at, dom_size) // blocks])
 
     @pl.when(me >= 1)
     def _():
-        send_ref[me - 1, 16 : 16 + halo, :] = to_prev
+        send_ref[me - 1, 12 : 12 + halo, :] = to_prev
 
     @pl.when(me + 1 < parts)
     def _():
-        send_ref[me + 1, 16 : 16 + halo, :] = to_next
+        send_ref[me + 1, 12 : 12 + halo, :] = to_next
 
 
 def three(value):
@@ -473,114 +473,129 @@
     ]
 
 
+def phases_kernel(place_ref, dirs_ref, waves_hbm, left_ref, stage, sems, first, rows):
+    sources = place_ref.shape[0]
+    width = dirs_ref.shape[1]
+    row = lax.broadcasted_iota(jnp.int32, (8, width), 0)
+    scaled = jnp.where(row >= 4, dirs_ref[...], 0.0)
+    t1, t2, t3 = three(scaled)
+    right = jnp.concatenate([t1, t2, t3, t1, t2, t1], 0).astype(jnp.bfloat16)
+    group = 4
+    span = group * LANES
+    chunks = span // rows
+
+    def centres(at, half):
+        for one in range(group):
+            u1, u2, u3 = three(place_ref[at * group + one, first : first + 8, :])
+            stack = jnp.concatenate([u1, u1, u1, u2, u2, u3], 0)
+            left_ref[half, one * LANES : (one + 1) * LANES, :] = stack.T.astype(jnp.bfloat16)
+
+    def project(chunk, half):
+        left = left_ref[half, chunk * rows : (chunk + 1) * rows, :]
+        return jnp.dot(left, right, preferred_element_type=jnp.float32)
+
+    def block(at, half):
+        ahead = project(0, half)
+        for chunk in range(chunks):
+            theta = ahead
+            if chunk + 1 < chunks:
+                ahead = project(chunk + 1, half)
+            cosine, sine = waves(theta)
+            to = slice(chunk * rows, (chunk + 1) * rows)
+            stage[half, to, 0:width] = cosine
+            stage[half, to, width : 2 * width] = sine
+            if chunk == 0:
+                centres(jnp.minimum(at + 1, sources // group - 1), 1 - half)
+
+    def store(at, half):
+        to = pl.ds(pl.multiple_of(at * span, span), span)
+        return pltpu.make_async_copy(stage.at[half], waves_hbm.at[to], sems.at[half])
+
+    def body(at, none):
+        for half in range(2):
+
+            @pl.when(at >= 1)
+            def _():
+                store(2 * at - 2 + half, half).wait()
+
+            block(2 * at + half, half)
+            store(2 * at + half, half).start()
+        return none
+
+    centres(0, 0)
+    pairs = sources // (2 * group)
+    lax.fori_loop(0, pairs, body, 0)
+    for half in range(2):
+        store(2 * pairs - 2 + half, half).wait()
+
+
 def far_kernel(
     flags_ref,
     coef_ref,
-    wave_ref,
+    place_ref,
     share_ref,
     dirs_ref,
     part_ref,
     eps_ref,
     lists_ref,
+    waves_hbm,
     e_out_ref,
     power_ref,
-    left_ref,
-    wave_a,
-    wave_b,
-    group,
-    rows,
-    cols,
+    waves_ref,
+    sems,
     scale,
 ):
+    span = waves_ref.shape[1]
+    group = span // LANES
+    sources = share_ref.shape[0]
+
+    def load(at):
+        rows = pl.ds(pl.multiple_of(at * span, span), span)
+        return pltpu.make_async_copy(waves_hbm.at[rows], waves_ref.at[at], sems.at[at])
+
+    def begin(at, none):
+        load(at).start()
+        return none
+
+    lax.fori_loop(0, sources // group, begin, 0)
     me = flags_ref[1]
     freq = flags_ref[2]
     halo = lists_ref.shape[0] // 2
     back = jnp.concatenate(
-        [arrived(share_ref, me, 1, 16, 16 + halo), arrived(share_ref, me, -1, 16, 16 + halo)], 0
+        [arrived(share_ref, me, 1, 12, 12 + halo), arrived(share_ref, me, -1, 12, 12 + halo)], 0
     )
     e_out_ref[...] = part_ref[...] + time_step * eps_ref[...] * spread(
         lists_ref[...], back, part_ref.shape[0]
     )
-    sources = share_ref.shape[0]
     width = dirs_ref.shape[1]
     dirs = [dirs_ref[i : i + 1, :] for i in range(3)]
-    turns = wave_ref[freq] * (0.5 / math.pi)
-    scaled = jnp.concatenate(
-        [jnp.zeros((4, width), jnp.float32)]
-        + [one * turns for one in dirs]
-        + [jnp.zeros((1, width), jnp.float32)],
-        0,
-    )
-    t1, t2, t3 = three(scaled)
-    right = jnp.concatenate([t1, t2, t3, t1, t2, t1], 0).astype(jnp.bfloat16)
     real = coef_ref[STEPS - 1, 2 * freq]
     imag = coef_ref[STEPS - 1, 2 * freq + 1]
-    blocks = sources // group
-    chunks = group * LANES // rows
-    pieces = [(low, min(low + cols, 2 * width)) for low in range(0, 2 * width, cols)]
-    per_chunk = -(-len(pieces) // chunks)
-
-    def centres(at):
-        for one in range(group):
-            u1, u2, u3 = three(share_ref[at * group + one, 8:16, :])
-            stack = jnp.concatenate([u1, u1, u1, u2, u2, u3], 0)
-            left_ref[one * LANES : (one + 1) * LANES, :] = stack.T.astype(jnp.bfloat16)
-
-    def project(chunk):
-        left = left_ref[chunk * rows : (chunk + 1) * rows, :]
-        return jnp.dot(left, right, preferred_element_type=jnp.float32)
-
-    def currents(at):
+
+    def body(at, total):
         pieces = []
         for one in range(group):
             source = at * group + one
-            share = share_ref[source, 0:16, :]
-            late = arrived(share_ref, source, 1, 11, 12) + arrived(share_ref, source, -1, 15, 16)
-            tangent = share[6:9]
+            share = share_ref[source, 0:8, :]
+            late = arrived(share_ref, source, 1, 8, 9) + arrived(share_ref, source, -1, 9, 10)
+            tangent = place_ref[source, 2 * halo : 2 * halo + 3, :]
             pieces.append(
                 jnp.concatenate(
                     [
                         share[0:6],
-                        tangent * (share[9:10] + real * late),
-                        tangent * (share[10:11] + imag * late),
+                        tangent * (share[6:7] + real * late),
+                        tangent * (share[7:8] + imag * late),
                         jnp.zeros((4, LANES), jnp.float32),
                     ],
                     0,
                 )
             )
-        return jnp.concatenate(pieces, 1).astype(jnp.bfloat16)
-
-    def collect(current, source, total, piece):
-        low, high = pieces[piece]
-        return total + jnp.dot(current, source[:, low:high], preferred_element_type=jnp.float32)
-
-    def half(next_at, done_at, target, source, totals):
-        totals = list(totals)
-        current = currents(done_at)
-        ahead = project(0)
-        for chunk in range(chunks):
-            theta = ahead
-            if chunk + 1 < chunks:
-                ahead = project(chunk + 1)
-            cosine, sine = waves(theta)
-            target[chunk * rows : (chunk + 1) * rows, 0:width] = cosine
-            target[chunk * rows : (chunk + 1) * rows, width : 2 * width] = sine
-            for piece in range(chunk * per_chunk, min((chunk + 1) * per_chunk, len(pieces))):
-                totals[piece] = collect(current, source, totals[piece], piece)
-        centres(next_at)
-        return totals
-
-    def body(at, totals):
-        totals = half(2 * at + 1, jnp.maximum(2 * at - 1, 0), wave_a, wave_b, totals)
-        return tuple(half(jnp.minimum(2 * at + 2, blocks - 1), 2 * at, wave_b, wave_a, totals))
-
-    centres(0)
-    wave_b[...] = jnp.zeros_like(wave_b)
-    totals = tuple(jnp.zeros((16, high - low), jnp.float32) for low, high in pieces)
-    totals = lax.fori_loop(0, blocks // 2, body, totals)
-    current = currents(blocks - 1)
-    total = jnp.concatenate(
-        [collect(current, wave_b, total, piece) for piece, total in enumerate(totals)], 1
+        current = jnp.concatenate(pieces, 1).astype(jnp.bfloat16)
+        load(at).wait()
+        return total + jnp.dot(current, waves_ref[at], preferred_element_type=jnp.float32)
+
+    total = lax.fori_loop(
+        0, sources // group, body, jnp.zeros((16, 2 * width), jnp.float32), unroll=4
     )
 
     def p_row(at):
@@ -603,14 +618,14 @@
     power_ref[...] = power * scale
 
 
-def call(kernel, scalars, arrays, outs, scratch=(), name=None, far_arrays=()):
+def call(kernel, scalars, arrays, outs, scratch=(), name=None, far_arrays=(), far_outs=()):
     return pl.pallas_call(
         kernel,
-        out_shape=[jax.ShapeDtypeStruct(shape, kind) for shape, kind in outs],
+        out_shape=[jax.ShapeDtypeStruct(shape, kind) for shape, kind in outs] + list(far_outs),
         in_specs=[SMEM_SPEC] * len(scalars)
         + [VMEM_SPEC] * len(arrays)
         + [HBM_SPEC] * len(far_arrays),
-        out_specs=[VMEM_SPEC] * len(outs),
+        out_specs=[VMEM_SPEC] * len(outs) + [HBM_SPEC] * len(far_outs),
         scratch_shapes=list(scratch),
         compiler_params=PARAMS,
         name=name,
@@ -701,7 +716,7 @@
     got_b = lax.ppermute(send_b, AXES, pairs_b)
     index, signs, curl, b_table, mu_table, face_ids, geom, acc, dirs = call(
         prepare_kernel,
-        [flags, wavenum],
+        [flags, coef, wavenum],
         [e_table],
         [
             i32(3 * faces, LANES),
@@ -735,8 +750,8 @@
     b_table, part, near, send = call(
         first_step_kernel,
         [flags],
-        [got_a, got_b, index, signs, curl, b_table, mu_table, e_table, eps_table, lists],
-        [f32(faces, LANES), f32(own, LANES), f32(2 * halo, LANES), f32(parts, 2 * halo, LANES)],
+        [got_a, got_b, index, signs, curl, b_table, mu_table, e_table, eps_table, lists, geom],
+        [f32(faces, LANES), f32(own, LANES), f32(2 * halo, LANES), f32(parts, 2 * halo + 8, LANES)],
         [scratch(rows, LANES), scratch(own, LANES), scratch(own, LANES)],
         name="first_step",
     )
@@ -746,29 +761,41 @@
         [flags, coef],
         [got_a, got_b, shares, part, near, eps_table, lists, index, signs, b_table, mu_table]
         + [face_ids, edge_ids, live, geom, acc],
-        [f32(faces, LANES), f32(own, LANES), f32(parts, 24, LANES)],
+        [f32(faces, LANES), f32(own, LANES), f32(parts, 12 + halo, LANES)],
         [
             scratch(rows, LANES),
             scratch(own, LANES),
             scratch(own, LANES),
             scratch(own, LANES),
-            scratch(FREQ, 16, LANES),
+            scratch(FREQ, 12 + halo, LANES),
         ],
         name="second_step",
     )
-    shares = lax.all_to_all(send, AXES, 0, 0, tiled=True)
-    group = 4
+    late_shares = lax.all_to_all(send, AXES, 0, 0, tiled=True)
+    (wave_table,) = call(
+        functools.partial(phases_kernel, first=2 * halo, rows=64),
+        [],
+        [shares, dirs],
+        [],
+        [
+            scratch(2, 4 * LANES, 48, kind=jnp.bfloat16),
+            scratch(2, 4 * LANES, 2 * width, kind=jnp.bfloat16),
+            pltpu.SemaphoreType.DMA((2,)),
+        ],
+        name="phases",
+        far_outs=[pltpu.HBM((parts * LANES, 2 * width), jnp.bfloat16)],
+    )
     e_table, power = call(
-        functools.partial(far_kernel, group=group, rows=64, cols=256, scale=1.0 / (LANES * parts)),
-        [flags, coef, wavenum],
-        [shares, dirs, part, eps_table, lists],
+        functools.partial(far_kernel, scale=1.0 / (LANES * parts)),
+        [flags, coef],
+        [shares, late_shares, dirs, part, eps_table, lists],
         [f32(own, LANES), f32(1, width)],
         [
-            scratch(group * LANES, 48, kind=jnp.bfloat16),
-            scratch(group * LANES, 2 * width, kind=jnp.bfloat16),
-            scratch(group * LANES, 2 * width, kind=jnp.bfloat16),
+            scratch(parts // 4, 4 * LANES, 2 * width, kind=jnp.bfloat16),
+            pltpu.SemaphoreType.DMA((parts // 4,)),
         ],
         name="far",
+        far_arrays=[wave_table],
     )
     power = lax.all_to_all(
         jnp.broadcast_to(power, (dom_size, width)), "dom", 0, 0, tiled=True

time: 66.6 us -> 63.7 us (0.956)
  starting transfers between devices: 12 us -> 3.75 us
  waiting for transfers between devices: 7.93 us -> 2.43 us
  blocking collectives: 24.5 us -> 29.9 us
  Pallas kernels: 19.3 us -> 24.1 us
    all_to_all x1, starting transfers between devices: 10.8 us -> 2.58 us  [per_device(): late_shares = lax.all_to_all(send, AXES, 0, 0, tiled=True)]
    all_to_all x1, waiting for transfers between devices: 7.92 us -> 2.42 us  [per_device(): late_shares = lax.all_to_all(send, AXES, 0, 0, tiled=True)]
    all_to_all x1, blocking collectives: 14.8 us -> 19.9 us  [per_device(): shares = lax.all_to_all(send, AXES, 0, 0, tiled=True)]
    pallas_call x5 -> x6, Pallas kernels: 19.3 us -> 24.1 us  [call(): pl.pallas_call(kernel, out_shape=[jax.ShapeDtypeStruct(shape, kind) for s...]
  transfers between devices with their start and end apart: 3 -> 3, of which waited for: 1 -> 1; matrix products, arithmetic and copies ran while one was open for 0% -> 2% of each run, Pallas kernels for 4% -> 16%
where the time goes in v4:
time: 63.7 us; the launch traced here: 63.3 us
  blocking collectives  29.9 us (47%)
  Pallas kernels  24.1 us (38%)
  starting transfers between devices  3.75 us (6%)
  waiting for transfers between devices  2.43 us (4%)
  local copies, waits for them, and re-layouts  1.5 us (2%)
  other arithmetic  0.93 us (1%)
  between operations  0.76 us (1%)
    pallas_call x6, Pallas kernels, call(): pl.pallas_call(kernel, out_shape=[jax.ShapeDtypeStruct(shape, kind) for s...  24.1 us
    all_to_all x1, blocking collectives, per_device(): shares = lax.all_to_all(send, AXES, 0, 0, tiled=True)  19.9 us
    all_to_all x1, blocking collectives, per_device(): lax.all_to_all(jnp.broadcast_to(power, (dom_size, width)), 'dom', 0, 0, t...  9.95 us
    all_to_all x1, starting transfers between devices, per_device(): late_shares = lax.all_to_all(send, AXES, 0, 0, tiled=True)  2.58 us
    all_to_all x1, waiting for transfers between devices, per_device(): late_shares = lax.all_to_all(send, AXES, 0, 0, tiled=True)  2.42 us
  transfers between devices with their start and end apart: 3, of which 1 were waited for; matrix products, arithmetic and copies ran while one was open for 2% of the time, Pallas kernels for 16%

profile of v4, /device:TPU:0, one launch (start us, length us, event | category | flops | bytes accessed | tf_op | source)
XLA Modules:
  0.0 63.3 jit_solution(11342882656515533499)
XLA Ops:
  0.7 0.1 pad_add_fusion.flags_ref
  0.7 1.5 %first.1 = (f32[24,128]{1,0:T(8,128)S(1)}, f32[24,128]{1,0:T(8,128)S(1)}, f32[32,128]{1,0:T(8,128)S(1)}, f32[32,128]{1,0:T(8,128)S(1)}, s32[8,128]{1,0:T(8,128)S...) custom-call(s32[4]{0:T(128)S(1)} %pad_add_fusion.flags_ref, f32[32,128]{1,0:T(8,128)} %bitcast.19, f32[32,128]{1,0:T(8,128)} %bitcast.20, ...), custom_call_target="tpu_custom_call" | custom-call | tf_op jit(solution)/shard_map/first/pallas_call | solution.py:622
  2.2 0.5 collective-permute-start
  2.7 0.7 %collective-permute-start.1 = (f32[24,128]{1,0:T(8,128)S(1)}, f32[24,128]{1,0:T(8,128)S(1)}, u32[]{:S(2)}, u32[]{:S(2)}) collective-permute-start(f32[24,128]{1,0:T(8,128)S(1)} %get-tuple-element.29), channel_id=1, source_target_pairs={{1,2},{3,4},{5,6},{7,8},{9,10},{11,12},{13,14},{15,16},{17,18},{19... | collective-permute-start | bytes 36872 | tf_op jit(solution)/shard_map/ppermute | solution.py:716
  3.4 0.8 %multiply_cosine_fusion = (f32[2,4,1]{1,0,2:T(2,128)S(1)}, f32[2,4,1]{1,0,2:T(2,128)S(1)}) fusion(f32[4]{0:T(128)} %wave_ref.1, f32[2]{0:T(128)S(1)} %add_multiply_fusion), kind=kLoop, calls=%fused_computation.2 | loop fusion | flops 16 | bytes 88 | tf_op jit(solution)/shard_map/cos | solution.py:687
  4.2 0.1 copy.18
  4.3 0.1 reshape.145.coef_ref
  4.4 0.0 copy-start
  4.4 0.7 %copy-done = f32[4]{0:T(128)S(1)} copy-done((f32[4]{0:T(128)S(1)}, f32[4]{0:T(128)}, u32[]{:S(2)}) %copy-start) | copy-done | bytes 40
  5.0 2.5 %prepare.1 = (s32[168,128]{1,0:T(8,128)S(1)}, f32[168,128]{1,0:T(8,128)S(1)}, f32[56,128]{1,0:T(8,128)S(1)}, f32[56,128]{1,0:T(8,128)S(1)}, f32[56,128]{1,0:T(8,...) custom-call(s32[4]{0:T(128)S(1)} %pad_add_fusion.flags_ref, ...), custom_call_target="tpu_custom_call" | custom-call | tf_op jit(solution)/shard_map/prepare/pallas_call | solution.py:622
  7.5 0.0 collective-permute-done.got_a_ref
  7.5 0.0 collective-permute-done.1.got_b_ref
  7.5 2.7 %first_step.1 = (f32[56,128]{1,0:T(8,128)S(1)}, f32[32,128]{1,0:T(8,128)S(1)}, f32[8,128]{1,0:T(8,128)S(1)}, f32[32,16,128]{2,1,0:T(8,128)S(1)}) custom-call(s32[4]{0:T(128)S(1)} %pad_add_fusion.flags_ref, f32[24,128]{1,0:T(8,128)S(1)} %collective-permute-done.got_a_ref, f32[24,128]{1,0:T(8,128)S(1)} %collective-permute-done.1.got_b_ref, ...), custom_call_target="tpu_custom_call" | custom-call | tf_op jit(solution)/shard_map/first_step/pallas_call | solution.py:622
  10.2 19.9 %all_to_all.16.shares_ref.place_ref = f32[32,16,128]{2,1,0:T(8,128)S(1)} all-to-all(f32[32,16,128]{2,1,0:T(8,128)S(1)} %get-tuple-element.39), channel_id=1, replica_groups=mesh['grp'=2,'dom'=16] {'grp','dom'}, dimensions={0} | all-to-all | bytes 524288 | tf_op jit(solution)/shard_map/all_to_all | solution.py:758
  30.2 4.8 %second_step.1 = (f32[56,128]{1,0:T(8,128)}, f32[32,128]{1,0:T(8,128)S(1)}, f32[32,16,128]{2,1,0:T(8,128)}) custom-call(s32[4]{0:T(128)S(1)} %pad_add_fusion.flags_ref, f32[2,8]{1,0:T(2,128)S(1)} %reshape.145.coef_ref, f32[24,128]{1,0:T(8,128)S(1)} %collective-permute-done.got_a_ref, f32[24,128]{1,0:T(8,128)S(1)} %collective-permute-done.1.got_b_ref, ...), custom_call_target="tpu_custom_call" | custom-call | tf_op jit(solution)/shard_map/second_step/pallas_call | solution.py:622
  35.0 2.6 %all-to-all-start.1 = ((f32[32,16,128]{2,1,0:T(8,128)}), f32[32,16,128]{2,1,0:T(8,128)S(1)}, u32[]{:S(2)}, u32[]{:S(2)}) async-start(f32[32,16,128]{2,1,0:T(8,128)} %get-tuple-element.47), calls=%async_computation.1 | async-start | bytes 524288 | tf_op jit(solution)/shard_map/all_to_all | solution.py:774
  37.6 7.9 %phases.1.waves_hbm = bf16[4096,1024]{1,0:T(8,128)(2,1)} custom-call(f32[32,16,128]{2,1,0:T(8,128)S(1)} %all_to_all.16.shares_ref.place_ref, f32[8,512]{1,0:T(8,128)S(1)} %get-tuple-element.48.dirs_ref), custom_call_target="tpu_custom_call" | custom-call | tf_op jit(solution)/shard_map/phases/pallas_call | solution.py:622
  45.4 2.4 %all-to-all-done.1.share_ref = f32[32,16,128]{2,1,0:T(8,128)S(1)} async-done(((f32[32,16,128]{2,1,0:T(8,128)}), f32[32,16,128]{2,1,0:T(8,128)S(1)}, u32[]{:S(2)}, u32[]{:S(2)}) %all-to-all-start.1) | async-done | bytes 262176 | tf_op jit(solution)/shard_map/all_to_all | solution.py:774
  47.9 4.8 %far.1 = (f32[32,128]{1,0:T(8,128)}, f32[1,512]{1,0:T(1,128)S(1)}) custom-call(s32[4]{0:T(128)S(1)} %pad_add_fusion.flags_ref, f32[2,8]{1,0:T(2,128)S(1)} %reshape.145.coef_ref, f32[32,16,128]{2,1,0:T(8,128)S(1)} %all_to_all.16.shares_ref.place_ref, f32[32,16,128]{2,1,0:T(8,128)S(1)} %all-to-all-done.1.share_ref, f32[8,512]{1,0:T(8,128)S(1)} %get-tuple-element.48.dirs_ref, ...), custom_call_target="tpu_custom_call" | custom-call | tf_op jit(solution)/shard_map/far/pallas_call | solution.py:622
  52.7 9.9 %all_to_all.17 = f32[16,1,512]{2,1,0:T(1,128)S(1)} all-to-all(f32[16,1,512]{2,1,0:T(1,128)S(1)} %broadcast_in_dim.2), channel_id=1, replica_groups=mesh['grp'=2,'dom'=16] {'dom'}, dimensions={0} | all-to-all | bytes 65536 | tf_op jit(solution)/shard_map/all_to_all | solution.py:800
  62.6 0.1 reduce
  62.7 0.6 %reshape.157 = f32[4,2048]{1,0:T(4,128)} reshape(f32[16,512]{1,0:T(8,128)S(1)} %reduce) | data formatting | bytes 65536 | tf_op jit(solution)/shard_map/reshape | solution.py:802
  (3 shorter events, 0.0 us)
Async XLA Ops:
  2.2 5.3 %collective-permute-start = (f32[24,128]{1,0:T(8,128)S(1)}, f32[24,128]{1,0:T(8,128)S(1)}, u32[]{:S(2)}, u32[]{:S(2)}) collective-permute-start(f32[24,128]{1,0:T(8,128)S(1)} %get-tuple-element.28), channel_id=1, source_target_pairs={{0,1},{1,0},{2,3},{3,2},{4,5},{5,4},{6,7},{7,6},{8,9},{9,8},{10,11... | collective-permute-start | bytes 36872 | tf_op jit(solution)/shard_map/ppermute | solution.py:715
  2.7 4.8 %collective-permute-start.1 = (f32[24,128]{1,0:T(8,128)S(1)}, f32[24,128]{1,0:T(8,128)S(1)}, u32[]{:S(2)}, u32[]{:S(2)}) collective-permute-start(f32[24,128]{1,0:T(8,128)S(1)} %get-tuple-element.29), channel_id=1, source_target_pairs={{1,2},{3,4},{5,6},{7,8},{9,10},{11,12},{13,14},{15,16},{17,18},{19... | collective-permute-start | bytes 36872 | tf_op jit(solution)/shard_map/ppermute | solution.py:716
  4.4 0.7 %copy-start = (f32[4]{0:T(128)S(1)}, f32[4]{0:T(128)}, u32[]{:S(2)}) copy-start(f32[4]{0:T(128)} %wave_ref.1) | copy-start | bytes 52
  35.0 12.9 %all-to-all-start.1 = ((f32[32,16,128]{2,1,0:T(8,128)}), f32[32,16,128]{2,1,0:T(8,128)S(1)}, u32[]{:S(2)}, u32[]{:S(2)}) async-start(f32[32,16,128]{2,1,0:T(8,128)} %get-tuple-element.47), calls=%async_computation.1 | async-start | bytes 524288 | tf_op jit(solution)/shard_map/all_to_all | solution.py:774

commit v5 on v4

--- a/solution.py
+++ b/solution.py
@@ -115,10 +115,11 @@
         self.send_prev = rows[3 * halo : 4 * halo].astype(jnp.int32)
         self.huy_edge = rows[4 * halo : 4 * halo + 1].astype(jnp.int32)
         self.huy_eps = rows[4 * halo + 1 : 4 * halo + 2]
+        self.centres = rows[4 * halo + 2 : 4 * halo + 5]
 
 
 def greeting_rows(halo):
-    return -(-(4 * halo + 2) // 8) * 8
+    return -(-(4 * halo + 5) // 8) * 8
 
 
 def first_kernel(
@@ -129,6 +130,7 @@
     prev_hbm,
     edge_hbm,
     live_hbm,
+    geom_hbm,
     send_a_ref,
     send_b_ref,
     e_ref,
@@ -136,6 +138,7 @@
     lists_ref,
     edge_ref,
     live_ref,
+    geom_ref,
     sems,
 ):
     half = next_hbm.shape[0]
@@ -147,6 +150,7 @@
             (prev_hbm, lists_ref.at[pl.ds(half, half)]),
             (edge_hbm, edge_ref),
             (live_hbm, live_ref),
+            (geom_hbm, geom_ref),
         ],
         sems,
     )
@@ -156,8 +160,8 @@
     eps_found = lookup(eps_ref, 0, eps_ref.shape[0], lists)
     edge_ids = edge_ref[...]
     live_eps = lookup_row(eps_ref, edge_ids) * live_ref[...].astype(jnp.float32)
-    both = [lists.astype(jnp.float32), edge_ids.astype(jnp.float32), live_eps]
-    spare = send_a_ref.shape[0] - 4 * half - 2
+    both = [lists.astype(jnp.float32), edge_ids.astype(jnp.float32), live_eps, geom_ref[6:9, :]]
+    spare = send_a_ref.shape[0] - 4 * half - 5
     both.append(jnp.zeros((spare, LANES), jnp.float32))
     to_next = jnp.concatenate([e_found[:half], eps_found[:half]] + both, 0)
     to_prev = jnp.concatenate([e_found[half:], eps_found[half:]] + both, 0)
@@ -178,32 +182,30 @@
 
 def prepare_kernel(
     flags_ref,
-    coef_ref,
-    wave_ref,
     e_ref,
     edges_hbm,
     signs_hbm,
     b_hbm,
     mu_hbm,
     face_hbm,
-    geom_hbm,
     acc_hbm,
     angles_hbm,
+    wave_hbm,
     index_ref,
     signs_ref,
     curl_ref,
     b_ref,
     mu_ref,
     face_ref,
-    geom_ref,
     acc_ref,
     dirs_ref,
+    coef_ref,
     raw_edges,
     raw_signs,
     raw_angles,
+    wave_ref,
     sems,
 ):
-    del coef_ref
     width = dirs_ref.shape[1]
     if angles_hbm.shape[1] == width:
         angles = angles_hbm
@@ -216,9 +218,9 @@
             (b_hbm, b_ref),
             (mu_hbm, mu_ref),
             (face_hbm, face_ref),
-            (geom_hbm, geom_ref),
             (acc_hbm, acc_ref),
             (angles, raw_angles),
+            (wave_hbm, wave_ref),
         ],
         sems,
     )
@@ -240,6 +242,13 @@
     turns = wave_ref[flags_ref[2]] * (0.5 / math.pi)
     dirs_ref[4:7, :] = dirs_ref[0:3, :] * turns
     dirs_ref[7:8, :] = jnp.zeros((1, width), jnp.float32)
+    row = lax.broadcasted_iota(jnp.int32, coef_ref.shape, 0)
+    phase = jnp.zeros(coef_ref.shape, jnp.float32)
+    for step in range(STEPS):
+        for q in range(FREQ):
+            here = row // 2 == step * FREQ + q
+            phase = jnp.where(here, wave_ref[q] * (time_step * (step + 1)), phase)
+    coef_ref[...] = jnp.where(row % 2 == 0, jnp.cos(phase), -jnp.sin(phase))
 
 
 def faces_update(
@@ -315,18 +324,23 @@
     lefts = lookup(left_ref, 0, own, jnp.concatenate([prev.send_next, prev.send_prev], 0))
     rights = lookup(right_ref, 0, own, jnp.concatenate([after.send_prev, after.send_next], 0))
     near_ref[...] = jnp.concatenate([lefts[:halo], rights[:halo]], 0)
-    blank = jnp.zeros((2 * halo, LANES), jnp.float32)
-    gap = jnp.zeros((1, LANES), jnp.float32)
-    place = jnp.concatenate([geom_ref[3:6, :], gap, geom_ref[6:9, :], gap], 0)
-    fill(send_ref, lambda at: jnp.concatenate([blank, place], 0))
+    place = jnp.concatenate(
+        [
+            jnp.zeros((halo, LANES), jnp.float32),
+            geom_ref[6:9, :],
+            jnp.zeros((halo - 3, LANES), jnp.float32),
+        ],
+        0,
+    )
+    fill(send_ref, lambda at: place)
 
     @pl.when(me >= 1)
     def _():
-        send_ref[me - 1, 0 : 2 * halo, :] = jnp.concatenate([to_prev, known[halo:]], 0)
+        send_ref[me - 1] = jnp.concatenate([to_prev, known[halo:]], 0)
 
     @pl.when(me + 1 < parts)
     def _():
-        send_ref[me + 1, 0 : 2 * halo, :] = jnp.concatenate([to_next, known[:halo]], 0)
+        send_ref[me + 1] = jnp.concatenate([to_next, known[:halo]], 0)
 
     @pl.when(me >= 2)
     def _():
@@ -346,7 +360,6 @@
 
 def second_step_kernel(
     flags_ref,
-    coef_ref,
     got_a_ref,
     got_b_ref,
     shares_ref,
@@ -363,6 +376,7 @@
     live_ref,
     geom_ref,
     acc_ref,
+    coef_ref,
     b_out_ref,
     part_out_ref,
     send_ref,
@@ -410,7 +424,6 @@
         (lookup_row(e_ref, edges), lookup_row(part_out_ref, edges)),
     )
     live = live_ref[...].astype(jnp.float32)
-    normal = geom_ref[0:3, :]
     for q in range(FREQ):
         values = []
         for kind in range(2):
@@ -419,17 +432,16 @@
                 row = 2 * FREQ * kind + at
                 value = acc_ref[row : row + 1, :]
                 for step in range(STEPS):
-                    value = value + coef_ref[step, at] * samples[kind][step]
+                    to = step * 2 * FREQ + at
+                    value = value + coef_ref[to : to + 1, :] * samples[kind][step]
                 values.append(value * live)
         block_ref[q] = jnp.concatenate(
             [
-                normal * values[0],
-                normal * values[1],
-                values[2],
-                values[3],
+                geom_ref[0:6, :],
+                *values,
                 to_left,
                 to_right,
-                jnp.zeros((2 + halo, LANES), jnp.float32),
+                jnp.zeros((halo, LANES), jnp.float32),
             ],
             0,
         )
@@ -473,20 +485,58 @@
     ]
 
 
-def phases_kernel(place_ref, dirs_ref, waves_hbm, left_ref, stage, sems, first, rows):
-    sources = place_ref.shape[0]
+def phases_kernel(
+    flags_ref,
+    got_a_ref,
+    got_b_ref,
+    shares_ref,
+    dirs_ref,
+    kept_ref,
+    waves_hbm,
+    place_ref,
+    left_ref,
+    stage,
+    sems,
+    halo,
+    rows,
+):
+    me = flags_ref[1]
+    sources = shares_ref.shape[0]
     width = dirs_ref.shape[1]
+    from_prev, from_next = neighbours(flags_ref, got_a_ref, got_b_ref)
+
+    def placed(greeted):
+        return jnp.concatenate(
+            [
+                jnp.zeros((halo, LANES), jnp.float32),
+                Greeting(greeted, halo).centres,
+                jnp.zeros((halo - 3, LANES), jnp.float32),
+            ],
+            0,
+        )
+
+    fill(place_ref, lambda at: shares_ref[at])
+
+    @pl.when(me >= 1)
+    def _():
+        place_ref[me - 1] = placed(from_prev)
+
+    @pl.when(me + 1 < sources)
+    def _():
+        place_ref[me + 1] = placed(from_next)
+
     row = lax.broadcasted_iota(jnp.int32, (8, width), 0)
     scaled = jnp.where(row >= 4, dirs_ref[...], 0.0)
     t1, t2, t3 = three(scaled)
     right = jnp.concatenate([t1, t2, t3, t1, t2, t1], 0).astype(jnp.bfloat16)
-    group = 4
-    span = group * LANES
+    span = stage.shape[1]
+    group = span // LANES
     chunks = span // rows
+    kept = kept_ref.shape[0]
 
     def centres(at, half):
         for one in range(group):
-            u1, u2, u3 = three(place_ref[at * group + one, first : first + 8, :])
+            u1, u2, u3 = three(place_ref[at * group + one])
             stack = jnp.concatenate([u1, u1, u1, u2, u2, u3], 0)
             left_ref[half, one * LANES : (one + 1) * LANES, :] = stack.T.astype(jnp.bfloat16)
 
@@ -494,7 +544,7 @@
         left = left_ref[half, chunk * rows : (chunk + 1) * rows, :]
         return jnp.dot(left, right, preferred_element_type=jnp.float32)
 
-    def block(at, half):
+    def block(at, half, into):
         ahead = project(0, half)
         for chunk in range(chunks):
             theta = ahead
@@ -502,42 +552,44 @@
                 ahead = project(chunk + 1, half)
             cosine, sine = waves(theta)
             to = slice(chunk * rows, (chunk + 1) * rows)
-            stage[half, to, 0:width] = cosine
-            stage[half, to, width : 2 * width] = sine
+            into[to, 0:width] = cosine
+            into[to, width : 2 * width] = sine
             if chunk == 0:
                 centres(jnp.minimum(at + 1, sources // group - 1), 1 - half)
 
     def store(at, half):
-        to = pl.ds(pl.multiple_of(at * span, span), span)
+        to = pl.ds(pl.multiple_of((at - kept) * span, span), span)
         return pltpu.make_async_copy(stage.at[half], waves_hbm.at[to], sems.at[half])
 
     def body(at, none):
         for half in range(2):
 
-            @pl.when(at >= 1)
+            @pl.when(at > kept // 2)
             def _():
                 store(2 * at - 2 + half, half).wait()
 
-            block(2 * at + half, half)
+            block(2 * at + half, half, stage.at[half])
             store(2 * at + half, half).start()
         return none
 
+    pairs = sources // (2 * group)
     centres(0, 0)
-    pairs = sources // (2 * group)
-    lax.fori_loop(0, pairs, body, 0)
+    for at in range(kept):
+        block(at, at % 2, kept_ref.at[at])
+    lax.fori_loop(kept // 2, pairs, body, 0)
     for half in range(2):
         store(2 * pairs - 2 + half, half).wait()
 
 
 def far_kernel(
     flags_ref,
-    coef_ref,
-    place_ref,
     share_ref,
     dirs_ref,
+    coef_ref,
     part_ref,
     eps_ref,
     lists_ref,
+    kept_ref,
     waves_hbm,
     e_out_ref,
     power_ref,
@@ -545,58 +597,69 @@
     sems,
     scale,
 ):
-    span = waves_ref.shape[1]
+    kept = kept_ref.shape[0]
+    span = kept_ref.shape[1]
     group = span // LANES
     sources = share_ref.shape[0]
+    blocks = sources // group
 
     def load(at):
-        rows = pl.ds(pl.multiple_of(at * span, span), span)
-        return pltpu.make_async_copy(waves_hbm.at[rows], waves_ref.at[at], sems.at[at])
+        rows = pl.ds(pl.multiple_of((at - kept) * span, span), span)
+        return pltpu.make_async_copy(waves_hbm.at[rows], waves_ref.at[at - kept], sems.at[at - kept])
 
     def begin(at, none):
         load(at).start()
         return none
 
-    lax.fori_loop(0, sources // group, begin, 0)
+    lax.fori_loop(kept, blocks, begin, 0, unroll=6)
     me = flags_ref[1]
     freq = flags_ref[2]
-    halo = lists_ref.shape[0] // 2
-    back = jnp.concatenate(
-        [arrived(share_ref, me, 1, 12, 12 + halo), arrived(share_ref, me, -1, 12, 12 + halo)], 0
-    )
-    e_out_ref[...] = part_ref[...] + time_step * eps_ref[...] * spread(
-        lists_ref[...], back, part_ref.shape[0]
-    )
     width = dirs_ref.shape[1]
     dirs = [dirs_ref[i : i + 1, :] for i in range(3)]
-    real = coef_ref[STEPS - 1, 2 * freq]
-    imag = coef_ref[STEPS - 1, 2 * freq + 1]
-
-    def body(at, total):
+    first = 2 * FREQ * (STEPS - 1) + 2 * freq
+    real = coef_ref[pl.ds(first, 1), :]
+    imag = coef_ref[pl.ds(first + 1, 1), :]
+
+    def currents(at):
         pieces = []
         for one in range(group):
             source = at * group + one
-            share = share_ref[source, 0:8, :]
-            late = arrived(share_ref, source, 1, 8, 9) + arrived(share_ref, source, -1, 9, 10)
-            tangent = place_ref[source, 2 * halo : 2 * halo + 3, :]
+            share = share_ref[source, 0:10, :]
+            late = arrived(share_ref, source, 1, 10, 11) + arrived(share_ref, source, -1, 11, 12)
+            normal = share[0:3]
+            tangent = share[3:6]
             pieces.append(
                 jnp.concatenate(
                     [
-                        share[0:6],
-                        tangent * (share[6:7] + real * late),
-                        tangent * (share[7:8] + imag * late),
+                        normal * share[6:7],
+                        normal * share[7:8],
+                        tangent * (share[8:9] + real * late),
+                        tangent * (share[9:10] + imag * late),
                         jnp.zeros((4, LANES), jnp.float32),
                     ],
                     0,
                 )
             )
-        current = jnp.concatenate(pieces, 1).astype(jnp.bfloat16)
+        return jnp.concatenate(pieces, 1).astype(jnp.bfloat16)
+
+    halo = lists_ref.shape[0] // 2
+    back = jnp.concatenate(
+        [arrived(share_ref, me, 1, 12, 12 + halo), arrived(share_ref, me, -1, 12, 12 + halo)], 0
+    )
+    e_out_ref[...] = part_ref[...] + time_step * eps_ref[...] * spread(
+        lists_ref[...], back, part_ref.shape[0]
+    )
+    total = jnp.zeros((16, 2 * width), jnp.float32)
+    for at in range(kept):
+        total = total + jnp.dot(currents(at), kept_ref[at], preferred_element_type=jnp.float32)
+
+    def body(at, total):
         load(at).wait()
-        return total + jnp.dot(current, waves_ref[at], preferred_element_type=jnp.float32)
-
-    total = lax.fori_loop(
-        0, sources // group, body, jnp.zeros((16, 2 * width), jnp.float32), unroll=4
-    )
+        return total + jnp.dot(
+            currents(at), waves_ref[at - kept], preferred_element_type=jnp.float32
+        )
+
+    total = lax.fori_loop(kept, blocks, body, total, unroll=6)
 
     def p_row(at):
         return total[at : at + 1, 0:width]
@@ -682,13 +745,10 @@
     faces = b_field.shape[0] // LANES
     rows = own + 2 * halo
     greeting = greeting_rows(halo)
-    moments = time_step * jnp.arange(1, STEPS + 1, dtype=jnp.float32)
-    phase = moments[:, None] * wavenum[None, :]
-    coef = jnp.stack([jnp.cos(phase), -jnp.sin(phase)], 2).reshape(STEPS, 2 * FREQ)
     if width % LANES:
         angles = lax.dynamic_slice_in_dim(angles, (place % blocks) * width, width, axis=1)
 
-    send_a, send_b, e_table, eps_table, lists, edge_ids, live = call(
+    send_a, send_b, e_table, eps_table, lists, edge_ids, live, geom = call(
         first_kernel,
         [flags],
         [],
@@ -700,8 +760,9 @@
             i32(2 * halo, LANES),
             i32(1, LANES),
             i32(1, LANES),
-        ],
-        [pltpu.SemaphoreType.DMA((6,))],
+            f32(*huy_geom.shape),
+        ],
+        [pltpu.SemaphoreType.DMA((7,))],
         name="first",
         far_arrays=[
             table(e_field),
@@ -710,13 +771,14 @@
             table(send_prev),
             table(huy_edge),
             table(huy_live),
+            huy_geom,
         ],
     )
     got_a = lax.ppermute(send_a, AXES, pairs_a)
     got_b = lax.ppermute(send_b, AXES, pairs_b)
-    index, signs, curl, b_table, mu_table, face_ids, geom, acc, dirs = call(
+    index, signs, curl, b_table, mu_table, face_ids, acc, dirs, coef = call(
         prepare_kernel,
-        [flags, coef, wavenum],
+        [flags],
         [e_table],
         [
             i32(3 * faces, LANES),
@@ -725,14 +787,15 @@
             f32(faces, LANES),
             f32(faces, LANES),
             i32(1, LANES),
-            f32(*huy_geom.shape),
             f32(*huy_acc.shape),
             f32(8, width),
+            f32(2 * STEPS * FREQ, LANES),
         ],
         [
             scratch(*face_edges.shape, kind=jnp.int32),
             scratch(*face_signs.shape, kind=jnp.int32),
             scratch(2, width),
+            pltpu.SMEM(wavenum.shape, jnp.float32),
             pltpu.SemaphoreType.DMA((8,)),
         ],
         name="prepare",
@@ -742,25 +805,25 @@
             table(b_field),
             table(mu_inv),
             table(huy_face),
-            huy_geom,
             huy_acc,
             angles,
+            wavenum,
         ],
     )
     b_table, part, near, send = call(
         first_step_kernel,
         [flags],
         [got_a, got_b, index, signs, curl, b_table, mu_table, e_table, eps_table, lists, geom],
-        [f32(faces, LANES), f32(own, LANES), f32(2 * halo, LANES), f32(parts, 2 * halo + 8, LANES)],
+        [f32(faces, LANES), f32(own, LANES), f32(2 * halo, LANES), f32(parts, 2 * halo, LANES)],
         [scratch(rows, LANES), scratch(own, LANES), scratch(own, LANES)],
         name="first_step",
     )
     shares = lax.all_to_all(send, AXES, 0, 0, tiled=True)
     b_table, part, send = call(
         functools.partial(second_step_kernel, dom_size=dom_size),
-        [flags, coef],
+        [flags],
         [got_a, got_b, shares, part, near, eps_table, lists, index, signs, b_table, mu_table]
-        + [face_ids, edge_ids, live, geom, acc],
+        + [face_ids, edge_ids, live, geom, acc, coef],
         [f32(faces, LANES), f32(own, LANES), f32(parts, 12 + halo, LANES)],
         [
             scratch(rows, LANES),
@@ -772,30 +835,35 @@
         name="second_step",
     )
     late_shares = lax.all_to_all(send, AXES, 0, 0, tiled=True)
-    (wave_table,) = call(
-        functools.partial(phases_kernel, first=2 * halo, rows=64),
-        [],
-        [shares, dirs],
-        [],
+    group = 4
+    kept = 2
+    span = group * LANES
+    rest = parts // group - kept
+    kept_waves, far_waves = call(
+        functools.partial(phases_kernel, halo=halo, rows=64),
+        [flags],
+        [got_a, got_b, shares, dirs],
+        [((kept, span, 2 * width), jnp.bfloat16)],
         [
-            scratch(2, 4 * LANES, 48, kind=jnp.bfloat16),
-            scratch(2, 4 * LANES, 2 * width, kind=jnp.bfloat16),
+            scratch(parts, 2 * halo, LANES),
+            scratch(2, span, 48, kind=jnp.bfloat16),
+            scratch(2, span, 2 * width, kind=jnp.bfloat16),
             pltpu.SemaphoreType.DMA((2,)),
         ],
         name="phases",
-        far_outs=[pltpu.HBM((parts * LANES, 2 * width), jnp.bfloat16)],
+        far_outs=[pltpu.HBM((rest * span, 2 * width), jnp.bfloat16)],
     )
     e_table, power = call(
         functools.partial(far_kernel, scale=1.0 / (LANES * parts)),
-        [flags, coef],
-        [shares, late_shares, dirs, part, eps_table, lists],
+        [flags],
+        [late_shares, dirs, coef, part, eps_table, lists, kept_waves],
         [f32(own, LANES), f32(1, width)],
         [
-            scratch(parts // 4, 4 * LANES, 2 * width, kind=jnp.bfloat16),
-            pltpu.SemaphoreType.DMA((parts // 4,)),
+            scratch(rest, span, 2 * width, kind=jnp.bfloat16),
+            pltpu.SemaphoreType.DMA((rest,)),
         ],
         name="far",
-        far_arrays=[wave_table],
+        far_arrays=[far_waves],
     )
     power = lax.all_to_all(
         jnp.broadcast_to(power, (dom_size, width)), "dom", 0, 0, tiled=True

time: 63.7 us -> 61.3 us (0.962)
  local copies, waits for them, and re-layouts: 1.5 us -> 0.66 us
  other arithmetic: 0.93 us -> 0.15 us
    cos x1 -> x0, other arithmetic: 0.77 us -> none  [per_device(): jnp.cos(phase)]
    unnamed x2 -> x0, local copies, waits for them, and re-layouts: 0.66 us -> none
  transfers between devices with their start and end apart: 3 -> 3, of which waited for: 1 -> 1; matrix products, arithmetic and copies ran while one was open for 2% -> 0% of each run, Pallas kernels for 16% -> 17%
where the time goes in v5:
time: 61.3 us; the launch traced here: 60.9 us
  blocking collectives  29.7 us (48%)
  Pallas kernels  23.7 us (39%)
  starting transfers between devices  3.75 us (6%)
  waiting for transfers between devices  2.22 us (4%)
  between operations  0.74 us (1%)
  local copies, waits for them, and re-layouts  0.66 us (1%)
    pallas_call x6, Pallas kernels, call(): pl.pallas_call(kernel, out_shape=[jax.ShapeDtypeStruct(shape, kind) for s...  23.7 us
    all_to_all x1, blocking collectives, per_device(): shares = lax.all_to_all(send, AXES, 0, 0, tiled=True)  19.5 us
    all_to_all x1, blocking collectives, per_device(): lax.all_to_all(jnp.broadcast_to(power, (dom_size, width)), 'dom', 0, 0, t...  10.2 us
    all_to_all x1, starting transfers between devices, per_device(): late_shares = lax.all_to_all(send, AXES, 0, 0, tiled=True)  2.58 us
    all_to_all x1, waiting for transfers between devices, per_device(): late_shares = lax.all_to_all(send, AXES, 0, 0, tiled=True)  2.22 us
  transfers between devices with their start and end apart: 3, of which 1 were waited for; matrix products, arithmetic and copies ran while one was open for 0% of the time, Pallas kernels for 17%

profile of v5, /device:TPU:0, one launch (start us, length us, event | category | flops | bytes accessed | tf_op | source)
XLA Modules:
  0.0 60.9 jit_solution(8852023176282585031)
XLA Ops:
  0.7 0.1 pad_add_fusion.flags_ref
  0.7 1.5 %first.1 = (f32[24,128]{1,0:T(8,128)S(1)}, f32[24,128]{1,0:T(8,128)S(1)}, f32[32,128]{1,0:T(8,128)S(1)}, f32[32,128]{1,0:T(8,128)S(1)}, s32[8,128]{1,0:T(8,128)S...) custom-call(s32[4]{0:T(128)S(1)} %pad_add_fusion.flags_ref, f32[32,128]{1,0:T(8,128)} %bitcast.19, ...), custom_call_target="tpu_custom_call" | custom-call | tf_op jit(solution)/shard_map/first/pallas_call | solution.py:685
  2.3 0.5 collective-permute-start
  2.8 0.7 %collective-permute-start.1 = (f32[24,128]{1,0:T(8,128)S(1)}, f32[24,128]{1,0:T(8,128)S(1)}, u32[]{:S(2)}, u32[]{:S(2)}) collective-permute-start(f32[24,128]{1,0:T(8,128)S(1)} %get-tuple-element.32), channel_id=1, source_target_pairs={{1,2},{3,4},{5,6},{7,8},{9,10},{11,12},{13,14},{15,16},{17,18},{19... | collective-permute-start | bytes 36872 | tf_op jit(solution)/shard_map/ppermute | solution.py:778
  3.5 2.5 %prepare.1 = (s32[168,128]{1,0:T(8,128)S(1)}, f32[168,128]{1,0:T(8,128)S(1)}, f32[56,128]{1,0:T(8,128)S(1)}, f32[56,128]{1,0:T(8,128)S(1)}, f32[56,128]{1,0:T(8,...) custom-call(s32[4]{0:T(128)S(1)} %pad_add_fusion.flags_ref, ...), custom_call_target="tpu_custom_call" | custom-call | tf_op jit(solution)/shard_map/prepare/pallas_call | solution.py:685
  5.9 0.0 collective-permute-done.got_a_ref
  5.9 0.0 collective-permute-done.1.got_b_ref
  5.9 2.7 %first_step.1 = (f32[56,128]{1,0:T(8,128)S(1)}, f32[32,128]{1,0:T(8,128)S(1)}, f32[8,128]{1,0:T(8,128)S(1)}, f32[32,8,128]{2,1,0:T(8,128)S(1)}) custom-call(s32[4]{0:T(128)S(1)} %pad_add_fusion.flags_ref, f32[24,128]{1,0:T(8,128)S(1)} %collective-permute-done.got_a_ref, f32[24,128]{1,0:T(8,128)S(1)} %collective-permute-done.1.got_b_ref, ...), custom_call_target="tpu_custom_call" | custom-call | tf_op jit(solution)/shard_map/first_step/pallas_call | solution.py:685
  8.6 19.5 %all_to_all.16.shares_ref = f32[32,8,128]{2,1,0:T(8,128)S(1)} all-to-all(f32[32,8,128]{2,1,0:T(8,128)S(1)} %get-tuple-element.42), channel_id=1, replica_groups=mesh['grp'=2,'dom'=16] {'grp','dom'}, dimensions={0} | all-to-all | bytes 262144 | tf_op jit(solution)/shard_map/all_to_all | solution.py:821
  28.2 4.8 %second_step.1 = (f32[56,128]{1,0:T(8,128)}, f32[32,128]{1,0:T(8,128)S(1)}, f32[32,16,128]{2,1,0:T(8,128)}) custom-call(s32[4]{0:T(128)S(1)} %pad_add_fusion.flags_ref, f32[24,128]{1,0:T(8,128)S(1)} %collective-permute-done.got_a_ref, f32[24,128]{1,0:T(8,128)S(1)} %collective-permute-done.1.got_b_ref, f32[32,8,128]{2,1,0:T(8,128)S(1)} %all_to_all.16.shares_ref, ...), custom_call_target="tpu_custom_call" | custom-call | tf_op jit(solution)/shard_map/second_step/pallas_call | solution.py:685
  33.0 2.6 %all-to-all-start.1 = ((f32[32,16,128]{2,1,0:T(8,128)}), f32[32,16,128]{2,1,0:T(8,128)S(1)}, u32[]{:S(2)}, u32[]{:S(2)}) async-start(f32[32,16,128]{2,1,0:T(8,128)} %get-tuple-element.51), calls=%async_computation.1 | async-start | bytes 524288 | tf_op jit(solution)/shard_map/all_to_all | solution.py:837
  35.6 8.1 %phases.1 = (bf16[2,512,1024]{2,1,0:T(8,128)(2,1)S(1)}, bf16[3072,1024]{1,0:T(8,128)(2,1)}) custom-call(s32[4]{0:T(128)S(1)} %pad_add_fusion.flags_ref, f32[24,128]{1,0:T(8,128)S(1)} %collective-permute-done.got_a_ref, f32[24,128]{1,0:T(8,128)S(1)} %collective-permute-done.1.got_b_ref, f32[32,8,128]{2,1,0:T(8,128)S(1)} %all_to_all.16.shares_ref, ...), custom_call_target="tpu_custom_call" | custom-call | tf_op jit(solution)/shard_map/phases/pallas_call | solution.py:685
  43.6 2.2 %all-to-all-done.1.share_ref = f32[32,16,128]{2,1,0:T(8,128)S(1)} async-done(((f32[32,16,128]{2,1,0:T(8,128)}), f32[32,16,128]{2,1,0:T(8,128)S(1)}, u32[]{:S(2)}, u32[]{:S(2)}) %all-to-all-start.1) | async-done | bytes 262176 | tf_op jit(solution)/shard_map/all_to_all | solution.py:837
  45.8 4.1 %far.1 = (f32[32,128]{1,0:T(8,128)}, f32[1,512]{1,0:T(1,128)S(1)}) custom-call(s32[4]{0:T(128)S(1)} %pad_add_fusion.flags_ref, f32[32,16,128]{2,1,0:T(8,128)S(1)} %all-to-all-done.1.share_ref, f32[8,512]{1,0:T(8,128)S(1)} %get-tuple-element.52.dirs_ref, f32[16,128]{1,0:T(8,128)S(1)} %get-tuple-element.50.coef_ref, f32[32,128]{1,0:T(8,128)S(1)} %get-tuple-element.53.part_ref, ...), custom_call_target="tpu_custom_call" | custom-call | tf_op jit(solution)/shard_map/far/pallas_call | solution.py:685
  50.0 10.2 %all_to_all.17 = f32[16,1,512]{2,1,0:T(1,128)S(1)} all-to-all(f32[16,1,512]{2,1,0:T(1,128)S(1)} %broadcast_in_dim.2), channel_id=1, replica_groups=mesh['grp'=2,'dom'=16] {'dom'}, dimensions={0} | all-to-all | bytes 65536 | tf_op jit(solution)/shard_map/all_to_all | solution.py:868
  60.2 0.1 reduce
  60.3 0.6 %reshape.60 = f32[4,2048]{1,0:T(4,128)} reshape(f32[16,512]{1,0:T(8,128)S(1)} %reduce) | data formatting | bytes 65536 | tf_op jit(solution)/shard_map/reshape | solution.py:870
  (1 shorter events, 0.0 us)
Async XLA Ops:
  2.3 3.6 %collective-permute-start = (f32[24,128]{1,0:T(8,128)S(1)}, f32[24,128]{1,0:T(8,128)S(1)}, u32[]{:S(2)}, u32[]{:S(2)}) collective-permute-start(f32[24,128]{1,0:T(8,128)S(1)} %get-tuple-element.31), channel_id=1, source_target_pairs={{0,1},{1,0},{2,3},{3,2},{4,5},{5,4},{6,7},{7,6},{8,9},{9,8},{10,11... | collective-permute-start | bytes 36872 | tf_op jit(solution)/shard_map/ppermute | solution.py:777
  2.8 3.1 %collective-permute-start.1 = (f32[24,128]{1,0:T(8,128)S(1)}, f32[24,128]{1,0:T(8,128)S(1)}, u32[]{:S(2)}, u32[]{:S(2)}) collective-permute-start(f32[24,128]{1,0:T(8,128)S(1)} %get-tuple-element.32), channel_id=1, source_target_pairs={{1,2},{3,4},{5,6},{7,8},{9,10},{11,12},{13,14},{15,16},{17,18},{19... | collective-permute-start | bytes 36872 | tf_op jit(solution)/shard_map/ppermute | solution.py:778
  33.0 12.9 %all-to-all-start.1 = ((f32[32,16,128]{2,1,0:T(8,128)}), f32[32,16,128]{2,1,0:T(8,128)S(1)}, u32[]{:S(2)}, u32[]{:S(2)}) async-start(f32[32,16,128]{2,1,0:T(8,128)} %get-tuple-element.51), calls=%async_computation.1 | async-start | bytes 524288 | tf_op jit(solution)/shard_map/all_to_all | solution.py:837

commit v6 on v5

--- a/solution.py
+++ b/solution.py
@@ -182,6 +182,7 @@
 
 def prepare_kernel(
     flags_ref,
+    held_ref,
     e_ref,
     edges_hbm,
     signs_hbm,
@@ -191,6 +192,7 @@
     acc_hbm,
     angles_hbm,
     wave_hbm,
+    send_a_ref,
     index_ref,
     signs_ref,
     curl_ref,
@@ -206,6 +208,7 @@
     wave_ref,
     sems,
 ):
+    send_a_ref[...] = held_ref[...]
     width = dirs_ref.shape[1]
     if angles_hbm.shape[1] == width:
         angles = angles_hbm
@@ -294,6 +297,10 @@
     eps_ref,
     lists_ref,
     geom_ref,
+    face_ref,
+    live_ref,
+    acc_ref,
+    coef_ref,
     b_out_ref,
     part_ref,
     near_ref,
@@ -301,6 +308,8 @@
     table_ref,
     left_ref,
     right_ref,
+    block_ref,
+    dom_size,
 ):
     me = flags_ref[1]
     parts = send_ref.shape[0]
@@ -324,23 +333,30 @@
     lefts = lookup(left_ref, 0, own, jnp.concatenate([prev.send_next, prev.send_prev], 0))
     rights = lookup(right_ref, 0, own, jnp.concatenate([after.send_prev, after.send_next], 0))
     near_ref[...] = jnp.concatenate([lefts[:halo], rights[:halo]], 0)
-    place = jnp.concatenate(
-        [
-            jnp.zeros((halo, LANES), jnp.float32),
-            geom_ref[6:9, :],
-            jnp.zeros((halo - 3, LANES), jnp.float32),
-        ],
-        0,
-    )
-    fill(send_ref, lambda at: place)
+    live = live_ref[...].astype(jnp.float32)
+    sample = lookup_row(b_out_ref, face_ref[...])
+    for q in range(FREQ):
+        at = slice(2 * q, 2 * q + 2)
+        block_ref[q] = jnp.concatenate(
+            [
+                jnp.zeros((halo, LANES), jnp.float32),
+                geom_ref[6:9, :],
+                jnp.zeros((halo - 3, LANES), jnp.float32),
+                geom_ref[0:6, :],
+                (acc_ref[at, :] + coef_ref[at, :] * sample) * live,
+            ],
+            0,
+        )
+    blocks = dom_size // FREQ
+    fill(send_ref, lambda at: block_ref[lax.rem(at, dom_size) // blocks])
 
     @pl.when(me >= 1)
     def _():
-        send_ref[me - 1] = jnp.concatenate([to_prev, known[halo:]], 0)
+        send_ref[me - 1, 0 : 2 * halo, :] = jnp.concatenate([to_prev, known[halo:]], 0)
 
     @pl.when(me + 1 < parts)
     def _():
-        send_ref[me + 1] = jnp.concatenate([to_next, known[:halo]], 0)
+        send_ref[me + 1, 0 : 2 * halo, :] = jnp.concatenate([to_next, known[:halo]], 0)
 
     @pl.when(me >= 2)
     def _():
@@ -374,7 +390,6 @@
     face_ref,
     edge_ref,
     live_ref,
-    geom_ref,
     acc_ref,
     coef_ref,
     b_out_ref,
@@ -419,29 +434,22 @@
     to_right = lookup_row(right_ref, after.huy_edge) * (time_step * after.huy_eps)
     faces = face_ref[...]
     edges = edge_ref[...]
-    samples = (
-        (lookup_row(b_ref, faces), lookup_row(b_out_ref, faces)),
-        (lookup_row(e_ref, edges), lookup_row(part_out_ref, edges)),
-    )
     live = live_ref[...].astype(jnp.float32)
+    b_last = lookup_row(b_out_ref, faces) * live
+    samples = (lookup_row(e_ref, edges), lookup_row(part_out_ref, edges))
     for q in range(FREQ):
-        values = []
-        for kind in range(2):
-            for part in range(2):
-                at = 2 * q + part
-                row = 2 * FREQ * kind + at
-                value = acc_ref[row : row + 1, :]
-                for step in range(STEPS):
-                    to = step * 2 * FREQ + at
-                    value = value + coef_ref[to : to + 1, :] * samples[kind][step]
-                values.append(value * live)
+        at = 2 * FREQ + 2 * q
+        value = acc_ref[at : at + 2, :]
+        for step in range(STEPS):
+            to = step * 2 * FREQ + 2 * q
+            value = value + coef_ref[to : to + 2, :] * samples[step]
         block_ref[q] = jnp.concatenate(
             [
-                geom_ref[0:6, :],
-                *values,
+                b_last,
+                value * live,
                 to_left,
                 to_right,
-                jnp.zeros((halo, LANES), jnp.float32),
+                jnp.zeros((halo - 1, LANES), jnp.float32),
             ],
             0,
         )
@@ -450,11 +458,11 @@
 
     @pl.when(me >= 1)
     def _():
-        send_ref[me - 1, 12 : 12 + halo, :] = to_prev
+        send_ref[me - 1, 3:, :] = jnp.concatenate([to_right, to_prev], 0)
 
     @pl.when(me + 1 < parts)
     def _():
-        send_ref[me + 1, 12 : 12 + halo, :] = to_next
+        send_ref[me + 1, 3:, :] = jnp.concatenate([to_left, to_next], 0)
 
 
 def three(value):
@@ -485,6 +493,17 @@
     ]
 
 
+def direction_terms(dirs_ref):
+    row = lax.broadcasted_iota(jnp.int32, dirs_ref.shape, 0)
+    t1, t2, t3 = three(jnp.where(row >= 4, dirs_ref[...], 0.0))
+    return jnp.concatenate([t1, t2, t3, t1, t2, t1], 0).astype(jnp.bfloat16)
+
+
+def slot_terms(place):
+    u1, u2, u3 = three(place)
+    return jnp.concatenate([u1, u1, u1, u2, u2, u3], 0).T.astype(jnp.bfloat16)
+
+
 def phases_kernel(
     flags_ref,
     got_a_ref,
@@ -492,13 +511,14 @@
     shares_ref,
     dirs_ref,
     kept_ref,
+    place_ref,
     waves_hbm,
-    place_ref,
     left_ref,
     stage,
     sems,
     halo,
     rows,
+    late,
 ):
     me = flags_ref[1]
     sources = shares_ref.shape[0]
@@ -515,7 +535,7 @@
             0,
         )
 
-    fill(place_ref, lambda at: shares_ref[at])
+    fill(place_ref, lambda at: shares_ref[at, 0 : 2 * halo, :])
 
     @pl.when(me >= 1)
     def _():
@@ -525,10 +545,7 @@
     def _():
         place_ref[me + 1] = placed(from_next)
 
-    row = lax.broadcasted_iota(jnp.int32, (8, width), 0)
-    scaled = jnp.where(row >= 4, dirs_ref[...], 0.0)
-    t1, t2, t3 = three(scaled)
-    right = jnp.concatenate([t1, t2, t3, t1, t2, t1], 0).astype(jnp.bfloat16)
+    right = direction_terms(dirs_ref)
     span = stage.shape[1]
     group = span // LANES
     chunks = span // rows
@@ -536,9 +553,9 @@
 
     def centres(at, half):
         for one in range(group):
-            u1, u2, u3 = three(place_ref[at * group + one])
-            stack = jnp.concatenate([u1, u1, u1, u2, u2, u3], 0)
-            left_ref[half, one * LANES : (one + 1) * LANES, :] = stack.T.astype(jnp.bfloat16)
+            left_ref[half, one * LANES : (one + 1) * LANES, :] = slot_terms(
+                place_ref[at * group + one]
+            )
 
     def project(chunk, half):
         left = left_ref[half, chunk * rows : (chunk + 1) * rows, :]
@@ -572,7 +589,7 @@
             store(2 * at + half, half).start()
         return none
 
-    pairs = sources // (2 * group)
+    pairs = (sources // group - late) // 2
     centres(0, 0)
     for at in range(kept):
         block(at, at % 2, kept_ref.at[at])
@@ -583,39 +600,69 @@
 
 def far_kernel(
     flags_ref,
+    fixed_ref,
     share_ref,
+    place_ref,
     dirs_ref,
     coef_ref,
     part_ref,
     eps_ref,
     lists_ref,
+    edge_ref,
+    live_ref,
     kept_ref,
     waves_hbm,
+    power_ref,
+    e_hbm,
     e_out_ref,
-    power_ref,
     waves_ref,
+    stage,
+    left_ref,
+    late_ref,
+    delta_ref,
     sems,
+    halo,
+    rows,
     scale,
 ):
+    me = flags_ref[1]
+    freq = flags_ref[2]
     kept = kept_ref.shape[0]
+    late = stage.shape[0]
     span = kept_ref.shape[1]
     group = span // LANES
     sources = share_ref.shape[0]
     blocks = sources // group
+    width = dirs_ref.shape[1]
 
     def load(at):
-        rows = pl.ds(pl.multiple_of((at - kept) * span, span), span)
-        return pltpu.make_async_copy(waves_hbm.at[rows], waves_ref.at[at - kept], sems.at[at - kept])
+        to = pl.ds(pl.multiple_of((at - kept) * span, span), span)
+        return pltpu.make_async_copy(waves_hbm.at[to], waves_ref.at[at - kept], sems.at[at - kept])
 
     def begin(at, none):
         load(at).start()
         return none
 
-    lax.fori_loop(kept, blocks, begin, 0, unroll=6)
-    me = flags_ref[1]
-    freq = flags_ref[2]
-    width = dirs_ref.shape[1]
-    dirs = [dirs_ref[i : i + 1, :] for i in range(3)]
+    lax.fori_loop(kept, blocks - late, begin, 0, unroll=4)
+
+    def meet(at, none):
+        late_ref[pl.ds(at, 1), :] = arrived(share_ref, at, 1, 3, 4) + arrived(share_ref, at, -1, 4, 5)
+        return none
+
+    lax.fori_loop(0, sources, meet, 0, unroll=8)
+    back = jnp.concatenate(
+        [arrived(share_ref, me, 1, 4, 4 + halo), arrived(share_ref, me, -1, 4, 4 + halo)], 0
+    )
+    delta = time_step * eps_ref[...] * spread(lists_ref[...], back, part_ref.shape[0])
+    delta_ref[...] = delta
+    e_out_ref[...] = part_ref[...] + delta
+    e_copy = pltpu.make_async_copy(e_out_ref, e_hbm, sems.at[blocks - late - kept])
+    e_copy.start()
+
+    late_ref[pl.ds(me + 2, 1), :] = arrived(share_ref, me, 3, 3, 4) + arrived(share_ref, me, 1, 3, 4)
+    late_ref[pl.ds(me, 1), :] = lookup_row(delta_ref, edge_ref[...]) * live_ref[...].astype(
+        jnp.float32
+    )
     first = 2 * FREQ * (STEPS - 1) + 2 * freq
     real = coef_ref[pl.ds(first, 1), :]
     imag = coef_ref[pl.ds(first + 1, 1), :]
@@ -624,17 +671,18 @@
         pieces = []
         for one in range(group):
             source = at * group + one
-            share = share_ref[source, 0:10, :]
-            late = arrived(share_ref, source, 1, 10, 11) + arrived(share_ref, source, -1, 11, 12)
-            normal = share[0:3]
-            tangent = share[3:6]
+            fixed = fixed_ref[source, 2 * halo : 2 * halo + 8, :]
+            share = share_ref[source, 0:3, :]
+            extra = late_ref[pl.ds(source, 1), :]
+            normal = fixed[0:3]
+            tangent = fixed[3:6]
             pieces.append(
                 jnp.concatenate(
                     [
-                        normal * share[6:7],
-                        normal * share[7:8],
-                        tangent * (share[8:9] + real * late),
-                        tangent * (share[9:10] + imag * late),
+                        normal * (fixed[6:7] + real * share[0:1]),
+                        normal * (fixed[7:8] + imag * share[0:1]),
+                        tangent * (share[1:2] + real * extra),
+                        tangent * (share[2:3] + imag * extra),
                         jnp.zeros((4, LANES), jnp.float32),
                     ],
                     0,
@@ -642,24 +690,46 @@
             )
         return jnp.concatenate(pieces, 1).astype(jnp.bfloat16)
 
-    halo = lists_ref.shape[0] // 2
-    back = jnp.concatenate(
-        [arrived(share_ref, me, 1, 12, 12 + halo), arrived(share_ref, me, -1, 12, 12 + halo)], 0
-    )
-    e_out_ref[...] = part_ref[...] + time_step * eps_ref[...] * spread(
-        lists_ref[...], back, part_ref.shape[0]
-    )
+    right = direction_terms(dirs_ref)
+    chunks = span // rows
+
+    def project(chunk):
+        left = left_ref[chunk * rows : (chunk + 1) * rows, :]
+        return jnp.dot(left, right, preferred_element_type=jnp.float32)
+
+    def collect(at, source):
+        return jnp.dot(currents(at), source[...], preferred_element_type=jnp.float32)
+
+    def block(at, into, jobs, total):
+        for one in range(group):
+            left_ref[one * LANES : (one + 1) * LANES, :] = slot_terms(place_ref[at * group + one])
+        ahead = project(0)
+        for chunk in range(chunks):
+            theta = ahead
+            if chunk + 1 < chunks:
+                ahead = project(chunk + 1)
+            cosine, sine = waves(theta)
+            to = slice(chunk * rows, (chunk + 1) * rows)
+            into[to, 0:width] = cosine
+            into[to, width : 2 * width] = sine
+            if jobs and chunk % 4 == 0:
+                total = total + collect(*jobs.pop(0))
+        return total
+
     total = jnp.zeros((16, 2 * width), jnp.float32)
-    for at in range(kept):
-        total = total + jnp.dot(currents(at), kept_ref[at], preferred_element_type=jnp.float32)
+    jobs = [(at, kept_ref.at[at]) for at in range(kept)]
+    for at in range(late):
+        total = block(blocks - late + at, stage.at[at], jobs, total)
+        jobs.append((blocks - late + at, stage.at[at]))
 
     def body(at, total):
         load(at).wait()
-        return total + jnp.dot(
-            currents(at), waves_ref[at - kept], preferred_element_type=jnp.float32
-        )
-
-    total = lax.fori_loop(kept, blocks, body, total, unroll=6)
+        return total + collect(at, waves_ref.at[at - kept])
+
+    total = lax.fori_loop(kept, blocks - late, body, total, unroll=4)
+    for job in jobs:
+        total = total + collect(*job)
+    dirs = [dirs_ref[i : i + 1, :] for i in range(3)]
 
     def p_row(at):
         return total[at : at + 1, 0:width]
@@ -679,6 +749,7 @@
             gap = outer[i] - inner[i]
             power = power + gap * gap
     power_ref[...] = power * scale
+    e_copy.wait()
 
 
 def call(kernel, scalars, arrays, outs, scratch=(), name=None, far_arrays=(), far_outs=()):
@@ -774,13 +845,13 @@
             huy_geom,
         ],
     )
-    got_a = lax.ppermute(send_a, AXES, pairs_a)
     got_b = lax.ppermute(send_b, AXES, pairs_b)
-    index, signs, curl, b_table, mu_table, face_ids, acc, dirs, coef = call(
+    send_a, index, signs, curl, b_table, mu_table, face_ids, acc, dirs, coef = call(
         prepare_kernel,
         [flags],
-        [e_table],
+        [send_a, e_table],
         [
+            f32(greeting, LANES),
             i32(3 * faces, LANES),
             f32(3 * faces, LANES),
             f32(faces, LANES),
@@ -810,12 +881,19 @@
             wavenum,
         ],
     )
+    got_a = lax.ppermute(send_a, AXES, pairs_a)
     b_table, part, near, send = call(
-        first_step_kernel,
+        functools.partial(first_step_kernel, dom_size=dom_size),
         [flags],
-        [got_a, got_b, index, signs, curl, b_table, mu_table, e_table, eps_table, lists, geom],
-        [f32(faces, LANES), f32(own, LANES), f32(2 * halo, LANES), f32(parts, 2 * halo, LANES)],
-        [scratch(rows, LANES), scratch(own, LANES), scratch(own, LANES)],
+        [got_a, got_b, index, signs, curl, b_table, mu_table, e_table, eps_table, lists, geom]
+        + [face_ids, live, acc, coef],
+        [f32(faces, LANES), f32(own, LANES), f32(2 * halo, LANES), f32(parts, 2 * halo + 8, LANES)],
+        [
+            scratch(rows, LANES),
+            scratch(own, LANES),
+            scratch(own, LANES),
+            scratch(FREQ, 2 * halo + 8, LANES),
+        ],
         name="first_step",
     )
     shares = lax.all_to_all(send, AXES, 0, 0, tiled=True)
@@ -823,14 +901,14 @@
         functools.partial(second_step_kernel, dom_size=dom_size),
         [flags],
         [got_a, got_b, shares, part, near, eps_table, lists, index, signs, b_table, mu_table]
-        + [face_ids, edge_ids, live, geom, acc, coef],
-        [f32(faces, LANES), f32(own, LANES), f32(parts, 12 + halo, LANES)],
+        + [face_ids, edge_ids, live, acc, coef],
+        [f32(faces, LANES), f32(own, LANES), f32(parts, 4 + halo, LANES)],
         [
             scratch(rows, LANES),
             scratch(own, LANES),
             scratch(own, LANES),
             scratch(own, LANES),
-            scratch(FREQ, 12 + halo, LANES),
+            scratch(FREQ, 4 + halo, LANES),
         ],
         name="second_step",
     )
@@ -838,14 +916,14 @@
     group = 4
     kept = 2
     span = group * LANES
-    rest = parts // group - kept
-    kept_waves, far_waves = call(
-        functools.partial(phases_kernel, halo=halo, rows=64),
+    late = 2
+    rest = parts // group - kept - late
+    kept_waves, places, far_waves = call(
+        functools.partial(phases_kernel, halo=halo, rows=64, late=late),
         [flags],
         [got_a, got_b, shares, dirs],
-        [((kept, span, 2 * width), jnp.bfloat16)],
+        [((kept, span, 2 * width), jnp.bfloat16), f32(parts, 2 * halo, LANES)],
         [
-            scratch(parts, 2 * halo, LANES),
             scratch(2, span, 48, kind=jnp.bfloat16),
             scratch(2, span, 2 * width, kind=jnp.bfloat16),
             pltpu.SemaphoreType.DMA((2,)),
@@ -853,17 +931,24 @@
         name="phases",
         far_outs=[pltpu.HBM((rest * span, 2 * width), jnp.bfloat16)],
     )
-    e_table, power = call(
-        functools.partial(far_kernel, scale=1.0 / (LANES * parts)),
+    power, e_table = call(
+        functools.partial(far_kernel, halo=halo, rows=64, scale=1.0 / (LANES * parts)),
         [flags],
-        [late_shares, dirs, coef, part, eps_table, lists, kept_waves],
-        [f32(own, LANES), f32(1, width)],
+        [shares, late_shares, places, dirs, coef, part, eps_table, lists, edge_ids, live]
+        + [kept_waves],
+        [f32(1, width)],
         [
+            scratch(own, LANES),
             scratch(rest, span, 2 * width, kind=jnp.bfloat16),
-            pltpu.SemaphoreType.DMA((rest,)),
+            scratch(late, span, 2 * width, kind=jnp.bfloat16),
+            scratch(span, 48, kind=jnp.bfloat16),
+            scratch(parts + 8, LANES),
+            scratch(own, LANES),
+            pltpu.SemaphoreType.DMA((rest + 1,)),
         ],
         name="far",
         far_arrays=[far_waves],
+        far_outs=[pltpu.HBM((own, LANES), jnp.float32)],
     )
     power = lax.all_to_all(
         jnp.broadcast_to(power, (dom_size, width)), "dom", 0, 0, tiled=True

time: 61.3 us -> 60.3 us (0.984)
  starting transfers between devices: 3.75 us -> 7.62 us
  blocking collectives: 29.7 us -> 26.6 us
  Pallas kernels: 23.7 us -> 21.4 us
    ppermute x1, starting transfers between devices: 0.52 us -> 4.39 us  [per_device(): got_a = lax.ppermute(send_a, AXES, pairs_a)]
    all_to_all x1, blocking collectives: 19.5 us -> 16.2 us  [per_device(): shares = lax.all_to_all(send, AXES, 0, 0, tiled=True)]
    pallas_call x6, Pallas kernels: 23.7 us -> 21.4 us  [call(): pl.pallas_call(kernel, out_shape=[jax.ShapeDtypeStruct(shape, kind) for s...]
    ppermute x1, waiting for transfers between devices: 0.01 us -> 0.83 us  [per_device(): got_a = lax.ppermute(send_a, AXES, pairs_a)]
  transfers between devices with their start and end apart: 3 -> 3, of which waited for: 1 -> 2; matrix products, arithmetic and copies ran while one was open for 0% -> 0% of each run, Pallas kernels for 17% -> 15%
where the time goes in v6:
time: 60.3 us; the launch traced here: 59.9 us
  blocking collectives  26.6 us (44%)
  Pallas kernels  21.4 us (35%)
  starting transfers between devices  7.62 us (13%)
  waiting for transfers between devices  2.74 us (5%)
  between operations  0.73 us (1%)
  local copies, waits for them, and re-layouts  0.66 us (1%)
    pallas_call x6, Pallas kernels, call(): pl.pallas_call(kernel, out_shape=[jax.ShapeDtypeStruct(shape, kind) for s...  21.4 us
    all_to_all x1, blocking collectives, per_device(): shares = lax.all_to_all(send, AXES, 0, 0, tiled=True)  16.2 us
    all_to_all x1, blocking collectives, per_device(): lax.all_to_all(jnp.broadcast_to(power, (dom_size, width)), 'dom', 0, 0, t...  10.5 us
    ppermute x1, starting transfers between devices, per_device(): got_a = lax.ppermute(send_a, AXES, pairs_a)  4.39 us
    all_to_all x1, starting transfers between devices, per_device(): late_shares = lax.all_to_all(send, AXES, 0, 0, tiled=True)  2.56 us
    all_to_all x1, waiting for transfers between devices, per_device(): late_shares = lax.all_to_all(send, AXES, 0, 0, tiled=True)  1.91 us
  transfers between devices with their start and end apart: 3, of which 2 were waited for; matrix products, arithmetic and copies ran while one was open for 0% of the time, Pallas kernels for 15%

profile of v6, /device:TPU:0, one launch (start us, length us, event | category | flops | bytes accessed | tf_op | source)
XLA Modules:
  0.0 59.9 jit_solution(8230440645047957177)
XLA Ops:
  0.7 0.1 pad_add_fusion.flags_ref
  0.7 1.5 %first.1 = (f32[24,128]{1,0:T(8,128)S(1)}, f32[24,128]{1,0:T(8,128)S(1)}, f32[32,128]{1,0:T(8,128)S(1)}, f32[32,128]{1,0:T(8,128)S(1)}, s32[8,128]{1,0:T(8,128)S...) custom-call(s32[4]{0:T(128)S(1)} %pad_add_fusion.flags_ref, f32[32,128]{1,0:T(8,128)} %bitcast.19, ...), custom_call_target="tpu_custom_call" | custom-call | tf_op jit(solution)/shard_map/first/pallas_call | solution.py:756
  2.3 0.7 %collective-permute-start.1 = (f32[24,128]{1,0:T(8,128)S(1)}, f32[24,128]{1,0:T(8,128)S(1)}, u32[]{:S(2)}, u32[]{:S(2)}) collective-permute-start(f32[24,128]{1,0:T(8,128)S(1)} %get-tuple-element.36), channel_id=1, source_target_pairs={{1,2},{3,4},{5,6},{7,8},{9,10},{11,12},{13,14},{15,16},{17,18},{19... | collective-permute-start | bytes 36872 | tf_op jit(solution)/shard_map/ppermute | solution.py:848
  3.0 2.5 %prepare.1 = (f32[24,128]{1,0:T(8,128)S(1)}, s32[168,128]{1,0:T(8,128)S(1)}, f32[168,128]{1,0:T(8,128)S(1)}, f32[56,128]{1,0:T(8,128)S(1)}, f32[56,128]{1,0:T(8,...) custom-call(s32[4]{0:T(128)S(1)} %pad_add_fusion.flags_ref, ...), custom_call_target="tpu_custom_call" | custom-call | tf_op jit(solution)/shard_map/prepare/pallas_call | solution.py:756
  5.4 4.4 %collective-permute-start = (f32[24,128]{1,0:T(8,128)S(1)}, f32[24,128]{1,0:T(8,128)S(1)}, u32[]{:S(2)}, u32[]{:S(2)}) collective-permute-start(f32[24,128]{1,0:T(8,128)S(1)} %get-tuple-element.35), channel_id=1, source_target_pairs={{0,1},{1,0},{2,3},{3,2},{4,5},{5,4},{6,7},{7,6},{8,9},{9,8},{10,11... | collective-permute-start | bytes 36872 | tf_op jit(solution)/shard_map/ppermute | solution.py:884
  9.8 0.0 collective-permute-done.1.got_b_ref
  9.8 0.8 %collective-permute-done.got_a_ref = f32[24,128]{1,0:T(8,128)S(1)} collective-permute-done((f32[24,128]{1,0:T(8,128)S(1)}, f32[24,128]{1,0:T(8,128)S(1)}, u32[]{:S(2)}, u32[]{:S(2)}) %collective-permute-start) | collective-permute-done | bytes 12320 | tf_op jit(solution)/shard_map/ppermute | solution.py:884
  10.6 2.9 %first_step.1 = (f32[56,128]{1,0:T(8,128)S(1)}, f32[32,128]{1,0:T(8,128)S(1)}, f32[8,128]{1,0:T(8,128)S(1)}, f32[32,16,128]{2,1,0:T(8,128)S(1)}) custom-call(s32[4]{0:T(128)S(1)} %pad_add_fusion.flags_ref, f32[24,128]{1,0:T(8,128)S(1)} %collective-permute-done.got_a_ref, f32[24,128]{1,0:T(8,128)S(1)} %collective-permute-done.1.got_b_ref, ...), custom_call_target="tpu_custom_call" | custom-call | tf_op jit(solution)/shard_map/first_step/pallas_call | solution.py:756
  13.5 16.2 %all_to_all.16.shares_ref.fixed_ref = f32[32,16,128]{2,1,0:T(8,128)S(1)} all-to-all(f32[32,16,128]{2,1,0:T(8,128)S(1)} %get-tuple-element.49), channel_id=1, replica_groups=mesh['grp'=2,'dom'=16] {'grp','dom'}, dimensions={0} | all-to-all | bytes 524288 | tf_op jit(solution)/shard_map/all_to_all | solution.py:899
  29.7 4.8 %second_step.1 = (f32[56,128]{1,0:T(8,128)}, f32[32,128]{1,0:T(8,128)S(1)}, f32[32,8,128]{2,1,0:T(8,128)}) custom-call(s32[4]{0:T(128)S(1)} %pad_add_fusion.flags_ref, f32[24,128]{1,0:T(8,128)S(1)} %collective-permute-done.got_a_ref, f32[24,128]{1,0:T(8,128)S(1)} %collective-permute-done.1.got_b_ref, f32[32,16,128]{2,1,0:T(8,128)S(1)} %all_to_all.16.shares_ref.fixed_ref, ...), custom_call_target="tpu_custom_call" | custom-call | tf_op jit(solution)/shard_map/second_step/pallas_call | solution.py:756
  34.4 2.6 %all-to-all-start.1 = ((f32[32,8,128]{2,1,0:T(8,128)}), f32[32,8,128]{2,1,0:T(8,128)S(1)}, u32[]{:S(2)}, u32[]{:S(2)}) async-start(f32[32,8,128]{2,1,0:T(8,128)} %get-tuple-element.54), calls=%async_computation.1 | async-start | bytes 262144 | tf_op jit(solution)/shard_map/all_to_all | solution.py:915
  37.0 6.3 %phases.1 = (bf16[2,512,1024]{2,1,0:T(8,128)(2,1)S(1)}, f32[32,8,128]{2,1,0:T(8,128)S(1)}, bf16[2048,1024]{1,0:T(8,128)(2,1)}) custom-call(s32[4]{0:T(128)S(1)} %pad_add_fusion.flags_ref, f32[24,128]{1,0:T(8,128)S(1)} %collective-permute-done.got_a_ref, f32[24,128]{1,0:T(8,128)S(1)} %collective-permute-done.1.got_b_ref, ...), custom_call_target="tpu_custom_call" | custom-call | tf_op jit(solution)/shard_map/phases/pallas_call | solution.py:756
  43.3 1.9 %all-to-all-done.1.share_ref = f32[32,8,128]{2,1,0:T(8,128)S(1)} async-done(((f32[32,8,128]{2,1,0:T(8,128)}), f32[32,8,128]{2,1,0:T(8,128)S(1)}, u32[]{:S(2)}, u32[]{:S(2)}) %all-to-all-start.1) | async-done | bytes 131104 | tf_op jit(solution)/shard_map/all_to_all | solution.py:915
  45.2 3.4 %far.1 = (f32[1,512]{1,0:T(1,128)S(1)}, f32[32,128]{1,0:T(8,128)}) custom-call(s32[4]{0:T(128)S(1)} %pad_add_fusion.flags_ref, f32[32,16,128]{2,1,0:T(8,128)S(1)} %all_to_all.16.shares_ref.fixed_ref, f32[32,8,128]{2,1,0:T(8,128)S(1)} %all-to-all-done.1.share_ref, f32[32,8,128]{2,1,0:T(8,128)S(1)} %get-tuple-element.56.place_ref, ...), custom_call_target="tpu_custom_call" | custom-call | tf_op jit(solution)/shard_map/far/pallas_call | solution.py:756
  48.7 10.5 %all_to_all.17 = f32[16,1,512]{2,1,0:T(1,128)S(1)} all-to-all(f32[16,1,512]{2,1,0:T(1,128)S(1)} %broadcast_in_dim.2), channel_id=1, replica_groups=mesh['grp'=2,'dom'=16] {'dom'}, dimensions={0} | all-to-all | bytes 65536 | tf_op jit(solution)/shard_map/all_to_all | solution.py:953
  59.2 0.1 reduce
  59.3 0.6 %reshape.60 = f32[4,2048]{1,0:T(4,128)} reshape(f32[16,512]{1,0:T(8,128)S(1)} %reduce) | data formatting | bytes 65536 | tf_op jit(solution)/shard_map/reshape | solution.py:955
  (1 shorter events, 0.0 us)
Async XLA Ops:
  2.3 7.5 %collective-permute-start.1 = (f32[24,128]{1,0:T(8,128)S(1)}, f32[24,128]{1,0:T(8,128)S(1)}, u32[]{:S(2)}, u32[]{:S(2)}) collective-permute-start(f32[24,128]{1,0:T(8,128)S(1)} %get-tuple-element.36), channel_id=1, source_target_pairs={{1,2},{3,4},{5,6},{7,8},{9,10},{11,12},{13,14},{15,16},{17,18},{19... | collective-permute-start | bytes 36872 | tf_op jit(solution)/shard_map/ppermute | solution.py:848
  5.4 5.2 %collective-permute-start = (f32[24,128]{1,0:T(8,128)S(1)}, f32[24,128]{1,0:T(8,128)S(1)}, u32[]{:S(2)}, u32[]{:S(2)}) collective-permute-start(f32[24,128]{1,0:T(8,128)S(1)} %get-tuple-element.35), channel_id=1, source_target_pairs={{0,1},{1,0},{2,3},{3,2},{4,5},{5,4},{6,7},{7,6},{8,9},{9,8},{10,11... | collective-permute-start | bytes 36872 | tf_op jit(solution)/shard_map/ppermute | solution.py:884
  34.4 10.8 %all-to-all-start.1 = ((f32[32,8,128]{2,1,0:T(8,128)}), f32[32,8,128]{2,1,0:T(8,128)S(1)}, u32[]{:S(2)}, u32[]{:S(2)}) async-start(f32[32,8,128]{2,1,0:T(8,128)} %get-tuple-element.54), calls=%async_computation.1 | async-start | bytes 262144 | tf_op jit(solution)/shard_map/all_to_all | solution.py:915

commit v7 on v6

--- a/solution.py
+++ b/solution.py
@@ -115,11 +115,13 @@
         self.send_prev = rows[3 * halo : 4 * halo].astype(jnp.int32)
         self.huy_edge = rows[4 * halo : 4 * halo + 1].astype(jnp.int32)
         self.huy_eps = rows[4 * halo + 1 : 4 * halo + 2]
-        self.centres = rows[4 * halo + 2 : 4 * halo + 5]
+        self.normals = rows[4 * halo + 2 : 4 * halo + 5]
+        self.tangents = rows[4 * halo + 5 : 4 * halo + 8]
+        self.centres = rows[4 * halo + 8 : 4 * halo + 11]
 
 
 def greeting_rows(halo):
-    return -(-(4 * halo + 5) // 8) * 8
+    return -(-(4 * halo + 11) // 8) * 8
 
 
 def first_kernel(
@@ -160,8 +162,8 @@
     eps_found = lookup(eps_ref, 0, eps_ref.shape[0], lists)
     edge_ids = edge_ref[...]
     live_eps = lookup_row(eps_ref, edge_ids) * live_ref[...].astype(jnp.float32)
-    both = [lists.astype(jnp.float32), edge_ids.astype(jnp.float32), live_eps, geom_ref[6:9, :]]
-    spare = send_a_ref.shape[0] - 4 * half - 5
+    both = [lists.astype(jnp.float32), edge_ids.astype(jnp.float32), live_eps, geom_ref[...]]
+    spare = send_a_ref.shape[0] - 4 * half - 11
     both.append(jnp.zeros((spare, LANES), jnp.float32))
     to_next = jnp.concatenate([e_found[:half], eps_found[:half]] + both, 0)
     to_prev = jnp.concatenate([e_found[half:], eps_found[half:]] + both, 0)
@@ -335,36 +337,45 @@
     near_ref[...] = jnp.concatenate([lefts[:halo], rights[:halo]], 0)
     live = live_ref[...].astype(jnp.float32)
     sample = lookup_row(b_out_ref, face_ref[...])
+    none = jnp.zeros((halo - 2, LANES), jnp.float32)
     for q in range(FREQ):
         at = slice(2 * q, 2 * q + 2)
-        block_ref[q] = jnp.concatenate(
-            [
-                jnp.zeros((halo, LANES), jnp.float32),
-                geom_ref[6:9, :],
-                jnp.zeros((halo - 3, LANES), jnp.float32),
-                geom_ref[0:6, :],
-                (acc_ref[at, :] + coef_ref[at, :] * sample) * live,
-            ],
-            0,
-        )
+        known_now = (acc_ref[at, :] + coef_ref[at, :] * sample) * live
+        block_ref[q, 0] = jnp.concatenate([known_now, none], 0)
+        block_ref[q, 1] = jnp.concatenate([geom_ref[6:9, :], known_now[0:1]], 0)
+        block_ref[q, 2] = jnp.concatenate([geom_ref[0:3, :], known_now[1:2]], 0)
     blocks = dom_size // FREQ
-    fill(send_ref, lambda at: block_ref[lax.rem(at, dom_size) // blocks])
+
+    def freq(part):
+        return lax.rem(part, dom_size) // blocks
+
+    fill(send_ref, lambda at: block_ref[freq(at)])
 
     @pl.when(me >= 1)
     def _():
-        send_ref[me - 1, 0 : 2 * halo, :] = jnp.concatenate([to_prev, known[halo:]], 0)
+        send_ref[me - 1, 0] = to_prev
+        send_ref[me - 1, 1] = known[halo:]
+        send_ref[me - 1, 2] = block_ref[freq(me - 1), 0]
 
     @pl.when(me + 1 < parts)
     def _():
-        send_ref[me + 1, 0 : 2 * halo, :] = jnp.concatenate([to_next, known[:halo]], 0)
+        send_ref[me + 1, 0] = to_next
+        send_ref[me + 1, 1] = known[:halo]
+        send_ref[me + 1, 2] = block_ref[freq(me + 1), 0]
 
     @pl.when(me >= 2)
     def _():
-        send_ref[me - 2, 0:halo, :] = lefts[halo:]
+        send_ref[me - 2, 0] = lefts[halo:]
 
     @pl.when(me + 2 < parts)
     def _():
-        send_ref[me + 2, 0:halo, :] = rights[halo:]
+        send_ref[me + 2, 0] = rights[halo:]
+
+
+def arrived_group(ref, me, by, group):
+    parts = ref.shape[0]
+    there = jnp.logical_and(me + by >= 0, me + by < parts)
+    return jnp.where(there, ref[jnp.clip(me + by, 0, parts - 1), group], 0.0)
 
 
 def arrived(ref, me, by, first, last):
@@ -390,6 +401,7 @@
     face_ref,
     edge_ref,
     live_ref,
+    geom_ref,
     acc_ref,
     coef_ref,
     b_out_ref,
@@ -411,16 +423,16 @@
     prev = Greeting(from_prev, halo)
     after = Greeting(from_next, halo)
     back = jnp.concatenate(
-        [arrived(shares_ref, me, 1, 0, halo), arrived(shares_ref, me, -1, 0, halo)], 0
+        [arrived_group(shares_ref, me, 1, 0), arrived_group(shares_ref, me, -1, 0)], 0
     )
     e_new = part_ref[...] + time_step * eps_ref[...] * spread(lists_ref[...], back, own)
     e_ref[...] = e_new
     table_ref[0:own, :] = e_new
-    table_ref[own : own + halo, :] = arrived(shares_ref, me, -1, halo, 2 * halo) + (
-        time_step * prev.eps * (arrived(shares_ref, me, -2, 0, halo) + near_ref[0:halo, :])
-    )
-    table_ref[own + halo : rows, :] = arrived(shares_ref, me, 1, halo, 2 * halo) + (
-        time_step * after.eps * (arrived(shares_ref, me, 2, 0, halo) + near_ref[halo:, :])
+    table_ref[own : own + halo, :] = arrived_group(shares_ref, me, -1, 1) + (
+        time_step * prev.eps * (arrived_group(shares_ref, me, -2, 0) + near_ref[0:halo, :])
+    )
+    table_ref[own + halo : rows, :] = arrived_group(shares_ref, me, 1, 1) + (
+        time_step * after.eps * (arrived_group(shares_ref, me, 2, 0) + near_ref[halo:, :])
     )
     total = faces_update(
         table_ref, 0, rows, index_ref, signs_ref, None, b_ref, mu_ref, b_out_ref
@@ -449,7 +461,7 @@
                 value * live,
                 to_left,
                 to_right,
-                jnp.zeros((halo - 1, LANES), jnp.float32),
+                geom_ref[3:6, :],
             ],
             0,
         )
@@ -512,6 +524,7 @@
     dirs_ref,
     kept_ref,
     place_ref,
+    fixed_ref,
     waves_hbm,
     left_ref,
     stage,
@@ -525,25 +538,29 @@
     width = dirs_ref.shape[1]
     from_prev, from_next = neighbours(flags_ref, got_a_ref, got_b_ref)
 
-    def placed(greeted):
-        return jnp.concatenate(
-            [
-                jnp.zeros((halo, LANES), jnp.float32),
-                Greeting(greeted, halo).centres,
-                jnp.zeros((halo - 3, LANES), jnp.float32),
-            ],
-            0,
+    none = jnp.zeros((halo, LANES), jnp.float32)
+    fill(place_ref, lambda at: jnp.concatenate([none, shares_ref[at, 1]], 0))
+    fill(
+        fixed_ref,
+        lambda at: jnp.concatenate(
+            [shares_ref[at, 2, 0:3], shares_ref[at, 1, 3:4], shares_ref[at, 2, 3:4], none[0:3]], 0
+        ),
+    )
+
+    def near(part, greeted):
+        greeting = Greeting(greeted, halo)
+        place_ref[part] = jnp.concatenate([none, greeting.centres, none[0 : halo - 3]], 0)
+        fixed_ref[part] = jnp.concatenate(
+            [greeting.normals, shares_ref[part, 2, 0:2], greeting.tangents], 0
         )
-
-    fill(place_ref, lambda at: shares_ref[at, 0 : 2 * halo, :])
 
     @pl.when(me >= 1)
     def _():
-        place_ref[me - 1] = placed(from_prev)
+        near(me - 1, from_prev)
 
     @pl.when(me + 1 < sources)
     def _():
-        place_ref[me + 1] = placed(from_next)
+        near(me + 1, from_next)
 
     right = direction_terms(dirs_ref)
     span = stage.shape[1]
@@ -671,16 +688,16 @@
         pieces = []
         for one in range(group):
             source = at * group + one
-            fixed = fixed_ref[source, 2 * halo : 2 * halo + 8, :]
-            share = share_ref[source, 0:3, :]
+            fixed = fixed_ref[source]
+            share = share_ref[source]
             extra = late_ref[pl.ds(source, 1), :]
             normal = fixed[0:3]
-            tangent = fixed[3:6]
+            tangent = jnp.where(jnp.abs(source - me) == 1, fixed[5:8], share[5:8])
             pieces.append(
                 jnp.concatenate(
                     [
-                        normal * (fixed[6:7] + real * share[0:1]),
-                        normal * (fixed[7:8] + imag * share[0:1]),
+                        normal * (fixed[3:4] + real * share[0:1]),
+                        normal * (fixed[4:5] + imag * share[0:1]),
                         tangent * (share[1:2] + real * extra),
                         tangent * (share[2:3] + imag * extra),
                         jnp.zeros((4, LANES), jnp.float32),
@@ -887,12 +904,12 @@
         [flags],
         [got_a, got_b, index, signs, curl, b_table, mu_table, e_table, eps_table, lists, geom]
         + [face_ids, live, acc, coef],
-        [f32(faces, LANES), f32(own, LANES), f32(2 * halo, LANES), f32(parts, 2 * halo + 8, LANES)],
+        [f32(faces, LANES), f32(own, LANES), f32(2 * halo, LANES), f32(parts, 3, halo, LANES)],
         [
             scratch(rows, LANES),
             scratch(own, LANES),
             scratch(own, LANES),
-            scratch(FREQ, 2 * halo + 8, LANES),
+            scratch(FREQ, 3, halo, LANES),
         ],
         name="first_step",
     )
@@ -901,7 +918,7 @@
         functools.partial(second_step_kernel, dom_size=dom_size),
         [flags],
         [got_a, got_b, shares, part, near, eps_table, lists, index, signs, b_table, mu_table]
-        + [face_ids, edge_ids, live, acc, coef],
+        + [face_ids, edge_ids, live, geom, acc, coef],
         [f32(faces, LANES), f32(own, LANES), f32(parts, 4 + halo, LANES)],
         [
             scratch(rows, LANES),
@@ -918,11 +935,15 @@
     span = group * LANES
     late = 2
     rest = parts // group - kept - late
-    kept_waves, places, far_waves = call(
+    kept_waves, places, fixed, far_waves = call(
         functools.partial(phases_kernel, halo=halo, rows=64, late=late),
         [flags],
         [got_a, got_b, shares, dirs],
-        [((kept, span, 2 * width), jnp.bfloat16), f32(parts, 2 * halo, LANES)],
+        [
+            ((kept, span, 2 * width), jnp.bfloat16),
+            f32(parts, 2 * halo, LANES),
+            f32(parts, 8, LANES),
+        ],
         [
             scratch(2, span, 48, kind=jnp.bfloat16),
             scratch(2, span, 2 * width, kind=jnp.bfloat16),
@@ -934,7 +955,7 @@
     power, e_table = call(
         functools.partial(far_kernel, halo=halo, rows=64, scale=1.0 / (LANES * parts)),
         [flags],
-        [shares, late_shares, places, dirs, coef, part, eps_table, lists, edge_ids, live]
+        [fixed, late_shares, places, dirs, coef, part, eps_table, lists, edge_ids, live]
         + [kept_waves],
         [f32(1, width)],
         [

time: 60.3 us -> 59 us (0.978)
  blocking collectives: 26.6 us -> 25.3 us
    all_to_all x1, blocking collectives: 16.2 us -> 14.8 us  [per_device(): shares = lax.all_to_all(send, AXES, 0, 0, tiled=True)]
where the time goes in v7:
time: 59 us; the launch traced here: 58.6 us
  blocking collectives  25.3 us (43%)
  Pallas kernels  21.5 us (36%)
  starting transfers between devices  7.64 us (13%)
  waiting for transfers between devices  2.7 us (5%)
  between operations  0.73 us (1%)
  local copies, waits for them, and re-layouts  0.66 us (1%)
    pallas_call x6, Pallas kernels, call(): pl.pallas_call(kernel, out_shape=[jax.ShapeDtypeStruct(shape, kind) for s...  21.5 us
    all_to_all x1, blocking collectives, per_device(): shares = lax.all_to_all(send, AXES, 0, 0, tiled=True)  14.8 us
    all_to_all x1, blocking collectives, per_device(): lax.all_to_all(jnp.broadcast_to(power, (dom_size, width)), 'dom', 0, 0, t...  10.5 us
    ppermute x1, starting transfers between devices, per_device(): got_a = lax.ppermute(send_a, AXES, pairs_a)  4.39 us
    all_to_all x1, starting transfers between devices, per_device(): late_shares = lax.all_to_all(send, AXES, 0, 0, tiled=True)  2.59 us
    all_to_all x1, waiting for transfers between devices, per_device(): late_shares = lax.all_to_all(send, AXES, 0, 0, tiled=True)  1.86 us
  transfers between devices with their start and end apart: 3, of which 2 were waited for; matrix products, arithmetic and copies ran while one was open for 0% of the time, Pallas kernels for 15%

profile of v7, /device:TPU:0, one launch (start us, length us, event | category | flops | bytes accessed | tf_op | source)
XLA Modules:
  0.0 58.6 jit_solution(15853365679994938193)
XLA Ops:
  0.7 0.1 pad_add_fusion.flags_ref
  0.7 1.5 %first.1 = (f32[32,128]{1,0:T(8,128)S(1)}, f32[32,128]{1,0:T(8,128)S(1)}, f32[32,128]{1,0:T(8,128)S(1)}, f32[32,128]{1,0:T(8,128)S(1)}, s32[8,128]{1,0:T(8,128)S...) custom-call(s32[4]{0:T(128)S(1)} %pad_add_fusion.flags_ref, f32[32,128]{1,0:T(8,128)} %bitcast.19, ...), custom_call_target="tpu_custom_call" | custom-call | tf_op jit(solution)/shard_map/first/pallas_call | solution.py:773
  2.3 0.7 %collective-permute-start.1 = (f32[32,128]{1,0:T(8,128)S(1)}, f32[32,128]{1,0:T(8,128)S(1)}, u32[]{:S(2)}, u32[]{:S(2)}) collective-permute-start(f32[32,128]{1,0:T(8,128)S(1)} %get-tuple-element.37), channel_id=1, source_target_pairs={{1,2},{3,4},{5,6},{7,8},{9,10},{11,12},{13,14},{15,16},{17,18},{19... | collective-permute-start | bytes 49160 | tf_op jit(solution)/shard_map/ppermute | solution.py:865
  3.0 2.5 %prepare.1 = (f32[32,128]{1,0:T(8,128)S(1)}, s32[168,128]{1,0:T(8,128)S(1)}, f32[168,128]{1,0:T(8,128)S(1)}, f32[56,128]{1,0:T(8,128)S(1)}, f32[56,128]{1,0:T(8,...) custom-call(s32[4]{0:T(128)S(1)} %pad_add_fusion.flags_ref, ...), custom_call_target="tpu_custom_call" | custom-call | tf_op jit(solution)/shard_map/prepare/pallas_call | solution.py:773
  5.4 4.4 %collective-permute-start = (f32[32,128]{1,0:T(8,128)S(1)}, f32[32,128]{1,0:T(8,128)S(1)}, u32[]{:S(2)}, u32[]{:S(2)}) collective-permute-start(f32[32,128]{1,0:T(8,128)S(1)} %get-tuple-element.36), channel_id=1, source_target_pairs={{0,1},{1,0},{2,3},{3,2},{4,5},{5,4},{6,7},{7,6},{8,9},{9,8},{10,11... | collective-permute-start | bytes 49160 | tf_op jit(solution)/shard_map/ppermute | solution.py:901
  9.8 0.0 collective-permute-done.1.got_b_ref
  9.8 0.8 %collective-permute-done.got_a_ref = f32[32,128]{1,0:T(8,128)S(1)} collective-permute-done((f32[32,128]{1,0:T(8,128)S(1)}, f32[32,128]{1,0:T(8,128)S(1)}, u32[]{:S(2)}, u32[]{:S(2)}) %collective-permute-start) | collective-permute-done | bytes 16416 | tf_op jit(solution)/shard_map/ppermute | solution.py:901
  10.6 2.9 %first_step.1 = (f32[56,128]{1,0:T(8,128)S(1)}, f32[32,128]{1,0:T(8,128)S(1)}, f32[8,128]{1,0:T(8,128)S(1)}, f32[32,3,4,128]{3,2,1,0:T(4,128)S(1)}) custom-call(s32[4]{0:T(128)S(1)} %pad_add_fusion.flags_ref, f32[32,128]{1,0:T(8,128)S(1)} %collective-permute-done.got_a_ref, f32[32,128]{1,0:T(8,128)S(1)} %collective-permute-done.1.got_b_ref, ...), custom_call_target="tpu_custom_call" | custom-call | tf_op jit(solution)/shard_map/first_step/pallas_call | solution.py:773
  13.5 14.8 %all_to_all.16.shares_ref = f32[32,3,4,128]{3,2,1,0:T(4,128)S(1)} all-to-all(f32[32,3,4,128]{3,2,1,0:T(4,128)S(1)} %get-tuple-element.50), channel_id=1, replica_groups=mesh['grp'=2,'dom'=16] {'grp','dom'}, dimensions={0} | all-to-all | bytes 393216 | tf_op jit(solution)/shard_map/all_to_all | solution.py:916
  28.3 4.8 %second_step.1 = (f32[56,128]{1,0:T(8,128)}, f32[32,128]{1,0:T(8,128)S(1)}, f32[32,8,128]{2,1,0:T(8,128)}) custom-call(s32[4]{0:T(128)S(1)} %pad_add_fusion.flags_ref, f32[32,128]{1,0:T(8,128)S(1)} %collective-permute-done.got_a_ref, f32[32,128]{1,0:T(8,128)S(1)} %collective-permute-done.1.got_b_ref, f32[32,3,4,128]{3,2,1,0:T(4,128)S(1)} %all_to_all.16.shares_ref, ...), custom_call_target="tpu_custom_call" | custom-call | tf_op jit(solution)/shard_map/second_step/pallas_call | solution.py:773
  33.1 2.6 %all-to-all-start.1 = ((f32[32,8,128]{2,1,0:T(8,128)}), f32[32,8,128]{2,1,0:T(8,128)S(1)}, u32[]{:S(2)}, u32[]{:S(2)}) async-start(f32[32,8,128]{2,1,0:T(8,128)} %get-tuple-element.57), calls=%async_computation.1 | async-start | bytes 262144 | tf_op jit(solution)/shard_map/all_to_all | solution.py:932
  35.7 6.4 %phases.1 = (bf16[2,512,1024]{2,1,0:T(8,128)(2,1)S(1)}, f32[32,8,128]{2,1,0:T(8,128)S(1)}, f32[32,8,128]{2,1,0:T(8,128)S(1)}, bf16[2048,1024]{1,0:T(8,128)(2,1)}) custom-call(s32[4]{0:T(128)S(1)} %pad_add_fusion.flags_ref, f32[32,128]{1,0:T(8,128)S(1)} %collective-permute-done.got_a_ref, f32[32,128]{1,0:T(8,128)S(1)} %collective-permute-done.1.got_b_ref, ...), custom_call_target="tpu_custom_call" | custom-call | tf_op jit(solution)/shard_map/phases/pallas_call | solution.py:773
  42.1 1.9 %all-to-all-done.1.share_ref = f32[32,8,128]{2,1,0:T(8,128)S(1)} async-done(((f32[32,8,128]{2,1,0:T(8,128)}), f32[32,8,128]{2,1,0:T(8,128)S(1)}, u32[]{:S(2)}, u32[]{:S(2)}) %all-to-all-start.1) | async-done | bytes 131104 | tf_op jit(solution)/shard_map/all_to_all | solution.py:932
  43.9 3.4 %far.1 = (f32[1,512]{1,0:T(1,128)S(1)}, f32[32,128]{1,0:T(8,128)}) custom-call(s32[4]{0:T(128)S(1)} %pad_add_fusion.flags_ref, f32[32,8,128]{2,1,0:T(8,128)S(1)} %get-tuple-element.52.fixed_ref, f32[32,8,128]{2,1,0:T(8,128)S(1)} %all-to-all-done.1.share_ref, f32[32,8,128]{2,1,0:T(8,128)S(1)} %get-tuple-element.58.place_ref, ...), custom_call_target="tpu_custom_call" | custom-call | tf_op jit(solution)/shard_map/far/pallas_call | solution.py:773
  47.4 10.5 %all_to_all.17 = f32[16,1,512]{2,1,0:T(1,128)S(1)} all-to-all(f32[16,1,512]{2,1,0:T(1,128)S(1)} %broadcast_in_dim.2), channel_id=1, replica_groups=mesh['grp'=2,'dom'=16] {'dom'}, dimensions={0} | all-to-all | bytes 65536 | tf_op jit(solution)/shard_map/all_to_all | solution.py:974
  57.9 0.1 reduce
  58.0 0.6 %reshape.60 = f32[4,2048]{1,0:T(4,128)} reshape(f32[16,512]{1,0:T(8,128)S(1)} %reduce) | data formatting | bytes 65536 | tf_op jit(solution)/shard_map/reshape | solution.py:976
  (1 shorter events, 0.0 us)
Async XLA Ops:
  2.3 7.5 %collective-permute-start.1 = (f32[32,128]{1,0:T(8,128)S(1)}, f32[32,128]{1,0:T(8,128)S(1)}, u32[]{:S(2)}, u32[]{:S(2)}) collective-permute-start(f32[32,128]{1,0:T(8,128)S(1)} %get-tuple-element.37), channel_id=1, source_target_pairs={{1,2},{3,4},{5,6},{7,8},{9,10},{11,12},{13,14},{15,16},{17,18},{19... | collective-permute-start | bytes 49160 | tf_op jit(solution)/shard_map/ppermute | solution.py:865
  5.4 5.2 %collective-permute-start = (f32[32,128]{1,0:T(8,128)S(1)}, f32[32,128]{1,0:T(8,128)S(1)}, u32[]{:S(2)}, u32[]{:S(2)}) collective-permute-start(f32[32,128]{1,0:T(8,128)S(1)} %get-tuple-element.36), channel_id=1, source_target_pairs={{0,1},{1,0},{2,3},{3,2},{4,5},{5,4},{6,7},{7,6},{8,9},{9,8},{10,11... | collective-permute-start | bytes 49160 | tf_op jit(solution)/shard_map/ppermute | solution.py:901
  33.1 10.8 %all-to-all-start.1 = ((f32[32,8,128]{2,1,0:T(8,128)}), f32[32,8,128]{2,1,0:T(8,128)S(1)}, u32[]{:S(2)}, u32[]{:S(2)}) async-start(f32[32,8,128]{2,1,0:T(8,128)} %get-tuple-element.57), calls=%async_computation.1 | async-start | bytes 262144 | tf_op jit(solution)/shard_map/all_to_all | solution.py:932

commit v8 on v7

--- a/solution.py
+++ b/solution.py
@@ -606,13 +606,21 @@
             store(2 * at + half, half).start()
         return none
 
-    pairs = (sources // group - late) // 2
+    ends = sources // group - late
+    pairs = ends // 2
     centres(0, 0)
     for at in range(kept):
         block(at, at % 2, kept_ref.at[at])
-    lax.fori_loop(kept // 2, pairs, body, 0)
-    for half in range(2):
-        store(2 * pairs - 2 + half, half).wait()
+    if stage.shape[0] == ends - kept:
+        for at in range(kept, ends):
+            block(at, at % 2, stage.at[at - kept])
+            store(at, at - kept).start()
+        for at in range(kept, ends):
+            store(at, at - kept).wait()
+    else:
+        lax.fori_loop(kept // 2, pairs, body, 0)
+        for half in range(2):
+            store(2 * pairs - 2 + half, half).wait()
 
 
 def far_kernel(
@@ -935,6 +943,7 @@
     span = group * LANES
     late = 2
     rest = parts // group - kept - late
+    stages = rest if rest <= 4 else 2
     kept_waves, places, fixed, far_waves = call(
         functools.partial(phases_kernel, halo=halo, rows=64, late=late),
         [flags],
@@ -946,8 +955,8 @@
         ],
         [
             scratch(2, span, 48, kind=jnp.bfloat16),
-            scratch(2, span, 2 * width, kind=jnp.bfloat16),
-            pltpu.SemaphoreType.DMA((2,)),
+            scratch(stages, span, 2 * width, kind=jnp.bfloat16),
+            pltpu.SemaphoreType.DMA((stages,)),
         ],
         name="phases",
         far_outs=[pltpu.HBM((rest * span, 2 * width), jnp.bfloat16)],

time: 59 us -> 58.4 us (0.990)
  Pallas kernels: 21.5 us -> 20.8 us
  waiting for transfers between devices: 2.7 us -> 3.32 us
  blocking collectives: 25.3 us -> 24.7 us
    pallas_call x6, Pallas kernels: 21.5 us -> 20.8 us  [call(): pl.pallas_call(kernel, out_shape=[jax.ShapeDtypeStruct(shape, kind) for s...]
    all_to_all x1, waiting for transfers between devices: 1.86 us -> 2.48 us  [per_device(): late_shares = lax.all_to_all(send, AXES, 0, 0, tiled=True)]
    all_to_all x1, blocking collectives: 10.5 us -> 9.9 us  [per_device(): lax.all_to_all(jnp.broadcast_to(power, (dom_size, width)), 'dom', 0, 0, t...]
  transfers between devices with their start and end apart: 3 -> 3, of which waited for: 2 -> 2; matrix products, arithmetic and copies ran while one was open for 0% -> 0% of each run, Pallas kernels for 15% -> 14%
where the time goes in v8:
time: 58.4 us; the launch traced here: 58 us
  blocking collectives  24.7 us (42%)
  Pallas kernels  20.8 us (36%)
  starting transfers between devices  7.64 us (13%)
  waiting for transfers between devices  3.32 us (6%)
  between operations  0.73 us (1%)
  local copies, waits for them, and re-layouts  0.66 us (1%)
    pallas_call x6, Pallas kernels, call(): pl.pallas_call(kernel, out_shape=[jax.ShapeDtypeStruct(shape, kind) for s...  20.8 us
    all_to_all x1, blocking collectives, per_device(): shares = lax.all_to_all(send, AXES, 0, 0, tiled=True)  14.8 us
    all_to_all x1, blocking collectives, per_device(): lax.all_to_all(jnp.broadcast_to(power, (dom_size, width)), 'dom', 0, 0, t...  9.9 us
    ppermute x1, starting transfers between devices, per_device(): got_a = lax.ppermute(send_a, AXES, pairs_a)  4.39 us
    all_to_all x1, starting transfers between devices, per_device(): late_shares = lax.all_to_all(send, AXES, 0, 0, tiled=True)  2.59 us
    all_to_all x1, waiting for transfers between devices, per_device(): late_shares = lax.all_to_all(send, AXES, 0, 0, tiled=True)  2.48 us
  transfers between devices with their start and end apart: 3, of which 2 were waited for; matrix products, arithmetic and copies ran while one was open for 0% of the time, Pallas kernels for 14%

profile of v8, /device:TPU:0, one launch (start us, length us, event | category | flops | bytes accessed | tf_op | source)
XLA Modules:
  0.0 58.0 jit_solution(801943178305376529)
XLA Ops:
  0.7 0.1 pad_add_fusion.flags_ref
  0.7 1.5 %first.1 = (f32[32,128]{1,0:T(8,128)S(1)}, f32[32,128]{1,0:T(8,128)S(1)}, f32[32,128]{1,0:T(8,128)S(1)}, f32[32,128]{1,0:T(8,128)S(1)}, s32[8,128]{1,0:T(8,128)S...) custom-call(s32[4]{0:T(128)S(1)} %pad_add_fusion.flags_ref, f32[32,128]{1,0:T(8,128)} %bitcast.19, ...), custom_call_target="tpu_custom_call" | custom-call | tf_op jit(solution)/shard_map/first/pallas_call | solution.py:781
  2.3 0.7 %collective-permute-start.1 = (f32[32,128]{1,0:T(8,128)S(1)}, f32[32,128]{1,0:T(8,128)S(1)}, u32[]{:S(2)}, u32[]{:S(2)}) collective-permute-start(f32[32,128]{1,0:T(8,128)S(1)} %get-tuple-element.37), channel_id=1, source_target_pairs={{1,2},{3,4},{5,6},{7,8},{9,10},{11,12},{13,14},{15,16},{17,18},{19... | collective-permute-start | bytes 49160 | tf_op jit(solution)/shard_map/ppermute | solution.py:873
  3.0 2.5 %prepare.1 = (f32[32,128]{1,0:T(8,128)S(1)}, s32[168,128]{1,0:T(8,128)S(1)}, f32[168,128]{1,0:T(8,128)S(1)}, f32[56,128]{1,0:T(8,128)S(1)}, f32[56,128]{1,0:T(8,...) custom-call(s32[4]{0:T(128)S(1)} %pad_add_fusion.flags_ref, ...), custom_call_target="tpu_custom_call" | custom-call | tf_op jit(solution)/shard_map/prepare/pallas_call | solution.py:781
  5.4 4.4 %collective-permute-start = (f32[32,128]{1,0:T(8,128)S(1)}, f32[32,128]{1,0:T(8,128)S(1)}, u32[]{:S(2)}, u32[]{:S(2)}) collective-permute-start(f32[32,128]{1,0:T(8,128)S(1)} %get-tuple-element.36), channel_id=1, source_target_pairs={{0,1},{1,0},{2,3},{3,2},{4,5},{5,4},{6,7},{7,6},{8,9},{9,8},{10,11... | collective-permute-start | bytes 49160 | tf_op jit(solution)/shard_map/ppermute | solution.py:909
  9.8 0.0 collective-permute-done.1.got_b_ref
  9.8 0.8 %collective-permute-done.got_a_ref = f32[32,128]{1,0:T(8,128)S(1)} collective-permute-done((f32[32,128]{1,0:T(8,128)S(1)}, f32[32,128]{1,0:T(8,128)S(1)}, u32[]{:S(2)}, u32[]{:S(2)}) %collective-permute-start) | collective-permute-done | bytes 16416 | tf_op jit(solution)/shard_map/ppermute | solution.py:909
  10.6 2.9 %first_step.1 = (f32[56,128]{1,0:T(8,128)S(1)}, f32[32,128]{1,0:T(8,128)S(1)}, f32[8,128]{1,0:T(8,128)S(1)}, f32[32,3,4,128]{3,2,1,0:T(4,128)S(1)}) custom-call(s32[4]{0:T(128)S(1)} %pad_add_fusion.flags_ref, f32[32,128]{1,0:T(8,128)S(1)} %collective-permute-done.got_a_ref, f32[32,128]{1,0:T(8,128)S(1)} %collective-permute-done.1.got_b_ref, ...), custom_call_target="tpu_custom_call" | custom-call | tf_op jit(solution)/shard_map/first_step/pallas_call | solution.py:781
  13.5 14.8 %all_to_all.16.shares_ref = f32[32,3,4,128]{3,2,1,0:T(4,128)S(1)} all-to-all(f32[32,3,4,128]{3,2,1,0:T(4,128)S(1)} %get-tuple-element.50), channel_id=1, replica_groups=mesh['grp'=2,'dom'=16] {'grp','dom'}, dimensions={0} | all-to-all | bytes 393216 | tf_op jit(solution)/shard_map/all_to_all | solution.py:924
  28.3 4.8 %second_step.1 = (f32[56,128]{1,0:T(8,128)}, f32[32,128]{1,0:T(8,128)S(1)}, f32[32,8,128]{2,1,0:T(8,128)}) custom-call(s32[4]{0:T(128)S(1)} %pad_add_fusion.flags_ref, f32[32,128]{1,0:T(8,128)S(1)} %collective-permute-done.got_a_ref, f32[32,128]{1,0:T(8,128)S(1)} %collective-permute-done.1.got_b_ref, f32[32,3,4,128]{3,2,1,0:T(4,128)S(1)} %all_to_all.16.shares_ref, ...), custom_call_target="tpu_custom_call" | custom-call | tf_op jit(solution)/shard_map/second_step/pallas_call | solution.py:781
  33.1 2.6 %all-to-all-start.1 = ((f32[32,8,128]{2,1,0:T(8,128)}), f32[32,8,128]{2,1,0:T(8,128)S(1)}, u32[]{:S(2)}, u32[]{:S(2)}) async-start(f32[32,8,128]{2,1,0:T(8,128)} %get-tuple-element.57), calls=%async_computation.1 | async-start | bytes 262144 | tf_op jit(solution)/shard_map/all_to_all | solution.py:940
  35.7 5.7 %phases.1 = (bf16[2,512,1024]{2,1,0:T(8,128)(2,1)S(1)}, f32[32,8,128]{2,1,0:T(8,128)S(1)}, f32[32,8,128]{2,1,0:T(8,128)S(1)}, bf16[2048,1024]{1,0:T(8,128)(2,1)}) custom-call(s32[4]{0:T(128)S(1)} %pad_add_fusion.flags_ref, f32[32,128]{1,0:T(8,128)S(1)} %collective-permute-done.got_a_ref, f32[32,128]{1,0:T(8,128)S(1)} %collective-permute-done.1.got_b_ref, ...), custom_call_target="tpu_custom_call" | custom-call | tf_op jit(solution)/shard_map/phases/pallas_call | solution.py:781
  41.5 2.5 %all-to-all-done.1.share_ref = f32[32,8,128]{2,1,0:T(8,128)S(1)} async-done(((f32[32,8,128]{2,1,0:T(8,128)}), f32[32,8,128]{2,1,0:T(8,128)S(1)}, u32[]{:S(2)}, u32[]{:S(2)}) %all-to-all-start.1) | async-done | bytes 131104 | tf_op jit(solution)/shard_map/all_to_all | solution.py:940
  43.9 3.4 %far.1 = (f32[1,512]{1,0:T(1,128)S(1)}, f32[32,128]{1,0:T(8,128)}) custom-call(s32[4]{0:T(128)S(1)} %pad_add_fusion.flags_ref, f32[32,8,128]{2,1,0:T(8,128)S(1)} %get-tuple-element.52.fixed_ref, f32[32,8,128]{2,1,0:T(8,128)S(1)} %all-to-all-done.1.share_ref, f32[32,8,128]{2,1,0:T(8,128)S(1)} %get-tuple-element.58.place_ref, ...), custom_call_target="tpu_custom_call" | custom-call | tf_op jit(solution)/shard_map/far/pallas_call | solution.py:781
  47.4 9.9 %all_to_all.17 = f32[16,1,512]{2,1,0:T(1,128)S(1)} all-to-all(f32[16,1,512]{2,1,0:T(1,128)S(1)} %broadcast_in_dim.2), channel_id=1, replica_groups=mesh['grp'=2,'dom'=16] {'dom'}, dimensions={0} | all-to-all | bytes 65536 | tf_op jit(solution)/shard_map/all_to_all | solution.py:983
  57.3 0.1 reduce
  57.4 0.6 %reshape.60 = f32[4,2048]{1,0:T(4,128)} reshape(f32[16,512]{1,0:T(8,128)S(1)} %reduce) | data formatting | bytes 65536 | tf_op jit(solution)/shard_map/reshape | solution.py:985
  (1 shorter events, 0.0 us)
Async XLA Ops:
  2.3 7.5 %collective-permute-start.1 = (f32[32,128]{1,0:T(8,128)S(1)}, f32[32,128]{1,0:T(8,128)S(1)}, u32[]{:S(2)}, u32[]{:S(2)}) collective-permute-start(f32[32,128]{1,0:T(8,128)S(1)} %get-tuple-element.37), channel_id=1, source_target_pairs={{1,2},{3,4},{5,6},{7,8},{9,10},{11,12},{13,14},{15,16},{17,18},{19... | collective-permute-start | bytes 49160 | tf_op jit(solution)/shard_map/ppermute | solution.py:873
  5.4 5.2 %collective-permute-start = (f32[32,128]{1,0:T(8,128)S(1)}, f32[32,128]{1,0:T(8,128)S(1)}, u32[]{:S(2)}, u32[]{:S(2)}) collective-permute-start(f32[32,128]{1,0:T(8,128)S(1)} %get-tuple-element.36), channel_id=1, source_target_pairs={{0,1},{1,0},{2,3},{3,2},{4,5},{5,4},{6,7},{7,6},{8,9},{9,8},{10,11... | collective-permute-start | bytes 49160 | tf_op jit(solution)/shard_map/ppermute | solution.py:909
  33.1 10.8 %all-to-all-start.1 = ((f32[32,8,128]{2,1,0:T(8,128)}), f32[32,8,128]{2,1,0:T(8,128)S(1)}, u32[]{:S(2)}, u32[]{:S(2)}) async-start(f32[32,8,128]{2,1,0:T(8,128)} %get-tuple-element.57), calls=%async_computation.1 | async-start | bytes 262144 | tf_op jit(solution)/shard_map/all_to_all | solution.py:940

commit v9 on v8

--- a/solution.py
+++ b/solution.py
@@ -299,10 +299,6 @@
     eps_ref,
     lists_ref,
     geom_ref,
-    face_ref,
-    live_ref,
-    acc_ref,
-    coef_ref,
     b_out_ref,
     part_ref,
     near_ref,
@@ -310,8 +306,6 @@
     table_ref,
     left_ref,
     right_ref,
-    block_ref,
-    dom_size,
 ):
     me = flags_ref[1]
     parts = send_ref.shape[0]
@@ -335,33 +329,20 @@
     lefts = lookup(left_ref, 0, own, jnp.concatenate([prev.send_next, prev.send_prev], 0))
     rights = lookup(right_ref, 0, own, jnp.concatenate([after.send_prev, after.send_next], 0))
     near_ref[...] = jnp.concatenate([lefts[:halo], rights[:halo]], 0)
-    live = live_ref[...].astype(jnp.float32)
-    sample = lookup_row(b_out_ref, face_ref[...])
-    none = jnp.zeros((halo - 2, LANES), jnp.float32)
-    for q in range(FREQ):
-        at = slice(2 * q, 2 * q + 2)
-        known_now = (acc_ref[at, :] + coef_ref[at, :] * sample) * live
-        block_ref[q, 0] = jnp.concatenate([known_now, none], 0)
-        block_ref[q, 1] = jnp.concatenate([geom_ref[6:9, :], known_now[0:1]], 0)
-        block_ref[q, 2] = jnp.concatenate([geom_ref[0:3, :], known_now[1:2]], 0)
-    blocks = dom_size // FREQ
-
-    def freq(part):
-        return lax.rem(part, dom_size) // blocks
-
-    fill(send_ref, lambda at: block_ref[freq(at)])
+    none = jnp.zeros((1, halo, LANES), jnp.float32)
+    place = jnp.concatenate([geom_ref[6:9, :], none[0, 0 : halo - 3]], 0)
+    block = jnp.concatenate([none, place[None]], 0)
+    fill(send_ref, lambda at: block)
 
     @pl.when(me >= 1)
     def _():
         send_ref[me - 1, 0] = to_prev
         send_ref[me - 1, 1] = known[halo:]
-        send_ref[me - 1, 2] = block_ref[freq(me - 1), 0]
 
     @pl.when(me + 1 < parts)
     def _():
         send_ref[me + 1, 0] = to_next
         send_ref[me + 1, 1] = known[:halo]
-        send_ref[me + 1, 2] = block_ref[freq(me + 1), 0]
 
     @pl.when(me >= 2)
     def _():
@@ -378,11 +359,11 @@
     return jnp.where(there, ref[jnp.clip(me + by, 0, parts - 1), group], 0.0)
 
 
-def arrived(ref, me, by, first, last):
+def arrived(ref, me, by, group, row):
     parts = ref.shape[0]
     there = jnp.logical_and(me + by >= 0, me + by < parts)
     at = jnp.clip(me + by, 0, parts - 1)
-    return jnp.where(there, ref[at, first:last, :], 0.0)
+    return jnp.where(there, ref[at, group, row : row + 1, :], 0.0)
 
 
 def second_step_kernel(
@@ -447,34 +428,35 @@
     faces = face_ref[...]
     edges = edge_ref[...]
     live = live_ref[...].astype(jnp.float32)
-    b_last = lookup_row(b_out_ref, faces) * live
-    samples = (lookup_row(e_ref, edges), lookup_row(part_out_ref, edges))
+    samples = (
+        (lookup_row(b_ref, faces), lookup_row(b_out_ref, faces)),
+        (lookup_row(e_ref, edges), lookup_row(part_out_ref, edges)),
+    )
     for q in range(FREQ):
-        at = 2 * FREQ + 2 * q
-        value = acc_ref[at : at + 2, :]
-        for step in range(STEPS):
-            to = step * 2 * FREQ + 2 * q
-            value = value + coef_ref[to : to + 2, :] * samples[step]
-        block_ref[q] = jnp.concatenate(
-            [
-                b_last,
-                value * live,
-                to_left,
-                to_right,
-                geom_ref[3:6, :],
-            ],
-            0,
-        )
+        values = []
+        for kind in range(2):
+            at = 2 * FREQ * kind + 2 * q
+            value = acc_ref[at : at + 2, :]
+            for step in range(STEPS):
+                to = step * 2 * FREQ + 2 * q
+                value = value + coef_ref[to : to + 2, :] * samples[kind][step]
+            values.append(value * live)
+        block_ref[q, 0] = jnp.concatenate(values, 0)
+        block_ref[q, 1] = jnp.concatenate([to_left, to_right, geom_ref[3:5, :]], 0)
+        block_ref[q, 2] = jnp.concatenate([geom_ref[5:6, :], geom_ref[0:3, :]], 0)
     blocks = dom_size // FREQ
     fill(send_ref, lambda at: block_ref[lax.rem(at, dom_size) // blocks])
+    none = jnp.zeros((halo - 1, LANES), jnp.float32)
 
     @pl.when(me >= 1)
     def _():
-        send_ref[me - 1, 3:, :] = jnp.concatenate([to_right, to_prev], 0)
+        send_ref[me - 1, 1] = jnp.concatenate([to_right, none], 0)
+        send_ref[me - 1, 2] = to_prev
 
     @pl.when(me + 1 < parts)
     def _():
-        send_ref[me + 1, 3:, :] = jnp.concatenate([to_left, to_next], 0)
+        send_ref[me + 1, 1] = jnp.concatenate([to_left, none], 0)
+        send_ref[me + 1, 2] = to_next
 
 
 def three(value):
@@ -524,7 +506,6 @@
     dirs_ref,
     kept_ref,
     place_ref,
-    fixed_ref,
     waves_hbm,
     left_ref,
     stage,
@@ -540,18 +521,9 @@
 
     none = jnp.zeros((halo, LANES), jnp.float32)
     fill(place_ref, lambda at: jnp.concatenate([none, shares_ref[at, 1]], 0))
-    fill(
-        fixed_ref,
-        lambda at: jnp.concatenate(
-            [shares_ref[at, 2, 0:3], shares_ref[at, 1, 3:4], shares_ref[at, 2, 3:4], none[0:3]], 0
-        ),
-    )
-
     def near(part, greeted):
-        greeting = Greeting(greeted, halo)
-        place_ref[part] = jnp.concatenate([none, greeting.centres, none[0 : halo - 3]], 0)
-        fixed_ref[part] = jnp.concatenate(
-            [greeting.normals, shares_ref[part, 2, 0:2], greeting.tangents], 0
+        place_ref[part] = jnp.concatenate(
+            [none, Greeting(greeted, halo).centres, none[0 : halo - 3]], 0
         )
 
     @pl.when(me >= 1)
@@ -625,7 +597,8 @@
 
 def far_kernel(
     flags_ref,
-    fixed_ref,
+    got_a_ref,
+    got_b_ref,
     share_ref,
     place_ref,
     dirs_ref,
@@ -671,12 +644,12 @@
     lax.fori_loop(kept, blocks - late, begin, 0, unroll=4)
 
     def meet(at, none):
-        late_ref[pl.ds(at, 1), :] = arrived(share_ref, at, 1, 3, 4) + arrived(share_ref, at, -1, 4, 5)
+        late_ref[pl.ds(at, 1), :] = arrived(share_ref, at, 1, 1, 0) + arrived(share_ref, at, -1, 1, 1)
         return none
 
     lax.fori_loop(0, sources, meet, 0, unroll=8)
     back = jnp.concatenate(
-        [arrived(share_ref, me, 1, 4, 4 + halo), arrived(share_ref, me, -1, 4, 4 + halo)], 0
+        [arrived_group(share_ref, me, 1, 2), arrived_group(share_ref, me, -1, 2)], 0
     )
     delta = time_step * eps_ref[...] * spread(lists_ref[...], back, part_ref.shape[0])
     delta_ref[...] = delta
@@ -684,10 +657,14 @@
     e_copy = pltpu.make_async_copy(e_out_ref, e_hbm, sems.at[blocks - late - kept])
     e_copy.start()
 
-    late_ref[pl.ds(me + 2, 1), :] = arrived(share_ref, me, 3, 3, 4) + arrived(share_ref, me, 1, 3, 4)
+    late_ref[pl.ds(me + 2, 1), :] = arrived(share_ref, me, 3, 1, 0) + arrived(share_ref, me, 1, 1, 0)
     late_ref[pl.ds(me, 1), :] = lookup_row(delta_ref, edge_ref[...]) * live_ref[...].astype(
         jnp.float32
     )
+    from_prev, from_next = neighbours(flags_ref, got_a_ref, got_b_ref)
+    prev, after = Greeting(from_prev, halo), Greeting(from_next, halo)
+    prev_geom = jnp.concatenate([prev.tangents, prev.normals], 0)
+    next_geom = jnp.concatenate([after.tangents, after.normals], 0)
     first = 2 * FREQ * (STEPS - 1) + 2 * freq
     real = coef_ref[pl.ds(first, 1), :]
     imag = coef_ref[pl.ds(first + 1, 1), :]
@@ -696,18 +673,20 @@
         pieces = []
         for one in range(group):
             source = at * group + one
-            fixed = fixed_ref[source]
-            share = share_ref[source]
+            value = share_ref[source, 0]
             extra = late_ref[pl.ds(source, 1), :]
-            normal = fixed[0:3]
-            tangent = jnp.where(jnp.abs(source - me) == 1, fixed[5:8], share[5:8])
+            geom = jnp.concatenate([share_ref[source, 1, 2:4, :], share_ref[source, 2]], 0)
+            geom = jnp.where(source == me - 1, prev_geom, geom)
+            geom = jnp.where(source == me + 1, next_geom, geom)
+            tangent = geom[0:3]
+            normal = geom[3:6]
             pieces.append(
                 jnp.concatenate(
                     [
-                        normal * (fixed[3:4] + real * share[0:1]),
-                        normal * (fixed[4:5] + imag * share[0:1]),
-                        tangent * (share[1:2] + real * extra),
-                        tangent * (share[2:3] + imag * extra),
+                        normal * value[0:1],
+                        normal * value[1:2],
+                        tangent * (value[2:3] + real * extra),
+                        tangent * (value[3:4] + imag * extra),
                         jnp.zeros((4, LANES), jnp.float32),
                     ],
                     0,
@@ -908,17 +887,11 @@
     )
     got_a = lax.ppermute(send_a, AXES, pairs_a)
     b_table, part, near, send = call(
-        functools.partial(first_step_kernel, dom_size=dom_size),
+        first_step_kernel,
         [flags],
-        [got_a, got_b, index, signs, curl, b_table, mu_table, e_table, eps_table, lists, geom]
-        + [face_ids, live, acc, coef],
-        [f32(faces, LANES), f32(own, LANES), f32(2 * halo, LANES), f32(parts, 3, halo, LANES)],
-        [
-            scratch(rows, LANES),
-            scratch(own, LANES),
-            scratch(own, LANES),
-            scratch(FREQ, 3, halo, LANES),
-        ],
+        [got_a, got_b, index, signs, curl, b_table, mu_table, e_table, eps_table, lists, geom],
+        [f32(faces, LANES), f32(own, LANES), f32(2 * halo, LANES), f32(parts, 2, halo, LANES)],
+        [scratch(rows, LANES), scratch(own, LANES), scratch(own, LANES)],
         name="first_step",
     )
     shares = lax.all_to_all(send, AXES, 0, 0, tiled=True)
@@ -927,13 +900,13 @@
         [flags],
         [got_a, got_b, shares, part, near, eps_table, lists, index, signs, b_table, mu_table]
         + [face_ids, edge_ids, live, geom, acc, coef],
-        [f32(faces, LANES), f32(own, LANES), f32(parts, 4 + halo, LANES)],
+        [f32(faces, LANES), f32(own, LANES), f32(parts, 3, halo, LANES)],
         [
             scratch(rows, LANES),
             scratch(own, LANES),
             scratch(own, LANES),
             scratch(own, LANES),
-            scratch(FREQ, 4 + halo, LANES),
+            scratch(FREQ, 3, halo, LANES),
         ],
         name="second_step",
     )
@@ -944,14 +917,13 @@
     late = 2
     rest = parts // group - kept - late
     stages = rest if rest <= 4 else 2
-    kept_waves, places, fixed, far_waves = call(
+    kept_waves, places, far_waves = call(
         functools.partial(phases_kernel, halo=halo, rows=64, late=late),
         [flags],
         [got_a, got_b, shares, dirs],
         [
             ((kept, span, 2 * width), jnp.bfloat16),
             f32(parts, 2 * halo, LANES),
-            f32(parts, 8, LANES),
         ],
         [
             scratch(2, span, 48, kind=jnp.bfloat16),
@@ -964,7 +936,7 @@
     power, e_table = call(
         functools.partial(far_kernel, halo=halo, rows=64, scale=1.0 / (LANES * parts)),
         [flags],
-        [fixed, late_shares, places, dirs, coef, part, eps_table, lists, edge_ids, live]
+        [got_a, got_b, late_shares, places, dirs, coef, part, eps_table, lists, edge_ids, live]
         + [kept_waves],
         [f32(1, width)],
         [

time: 58.4 us -> 58.2 us (level)
  blocking collectives: 24.7 us -> 24 us
  waiting for transfers between devices: 3.32 us -> 4.01 us
    all_to_all x1, waiting for transfers between devices: 2.48 us -> 3.17 us  [per_device(): late_shares = lax.all_to_all(send, AXES, 0, 0, tiled=True)]
    all_to_all x1, blocking collectives: 14.8 us -> 14.1 us  [per_device(): shares = lax.all_to_all(send, AXES, 0, 0, tiled=True)]
where the time goes in v9:
time: 58.2 us; the launch traced here: 57.8 us
  blocking collectives  24 us (41%)
  Pallas kernels  20.6 us (35%)
  starting transfers between devices  7.63 us (13%)
  waiting for transfers between devices  4.01 us (7%)
  between operations  0.73 us (1%)
  local copies, waits for them, and re-layouts  0.66 us (1%)
    pallas_call x6, Pallas kernels, call(): pl.pallas_call(kernel, out_shape=[jax.ShapeDtypeStruct(shape, kind) for s...  20.6 us
    all_to_all x1, blocking collectives, per_device(): shares = lax.all_to_all(send, AXES, 0, 0, tiled=True)  14.1 us
    all_to_all x1, blocking collectives, per_device(): lax.all_to_all(jnp.broadcast_to(power, (dom_size, width)), 'dom', 0, 0, t...  9.91 us
    ppermute x1, starting transfers between devices, per_device(): got_a = lax.ppermute(send_a, AXES, pairs_a)  4.39 us
    all_to_all x1, waiting for transfers between devices, per_device(): late_shares = lax.all_to_all(send, AXES, 0, 0, tiled=True)  3.17 us
    all_to_all x1, starting transfers between devices, per_device(): late_shares = lax.all_to_all(send, AXES, 0, 0, tiled=True)  2.58 us
  transfers between devices with their start and end apart: 3, of which 2 were waited for; matrix products, arithmetic and copies ran while one was open for 0% of the time, Pallas kernels for 14%

profile of v9, /device:TPU:0, one launch (start us, length us, event | category | flops | bytes accessed | tf_op | source)
XLA Modules:
  0.0 57.8 jit_solution(8019342611207888608)
XLA Ops:
  0.7 0.1 pad_add_fusion.flags_ref
  0.7 1.5 %first.1 = (f32[32,128]{1,0:T(8,128)S(1)}, f32[32,128]{1,0:T(8,128)S(1)}, f32[32,128]{1,0:T(8,128)S(1)}, f32[32,128]{1,0:T(8,128)S(1)}, s32[8,128]{1,0:T(8,128)S...) custom-call(s32[4]{0:T(128)S(1)} %pad_add_fusion.flags_ref, f32[32,128]{1,0:T(8,128)} %bitcast.19, ...), custom_call_target="tpu_custom_call" | custom-call | tf_op jit(solution)/shard_map/first/pallas_call | solution.py:760
  2.3 0.7 %collective-permute-start.1 = (f32[32,128]{1,0:T(8,128)S(1)}, f32[32,128]{1,0:T(8,128)S(1)}, u32[]{:S(2)}, u32[]{:S(2)}) collective-permute-start(f32[32,128]{1,0:T(8,128)S(1)} %get-tuple-element.36), channel_id=1, source_target_pairs={{1,2},{3,4},{5,6},{7,8},{9,10},{11,12},{13,14},{15,16},{17,18},{19... | collective-permute-start | bytes 49160 | tf_op jit(solution)/shard_map/ppermute | solution.py:852
  3.0 2.5 %prepare.1 = (f32[32,128]{1,0:T(8,128)S(1)}, s32[168,128]{1,0:T(8,128)S(1)}, f32[168,128]{1,0:T(8,128)S(1)}, f32[56,128]{1,0:T(8,128)S(1)}, f32[56,128]{1,0:T(8,...) custom-call(s32[4]{0:T(128)S(1)} %pad_add_fusion.flags_ref, ...), custom_call_target="tpu_custom_call" | custom-call | tf_op jit(solution)/shard_map/prepare/pallas_call | solution.py:760
  5.4 4.4 %collective-permute-start = (f32[32,128]{1,0:T(8,128)S(1)}, f32[32,128]{1,0:T(8,128)S(1)}, u32[]{:S(2)}, u32[]{:S(2)}) collective-permute-start(f32[32,128]{1,0:T(8,128)S(1)} %get-tuple-element.35), channel_id=1, source_target_pairs={{0,1},{1,0},{2,3},{3,2},{4,5},{5,4},{6,7},{7,6},{8,9},{9,8},{10,11... | collective-permute-start | bytes 49160 | tf_op jit(solution)/shard_map/ppermute | solution.py:888
  9.8 0.0 collective-permute-done.1.got_b_ref
  9.8 0.8 %collective-permute-done.got_a_ref = f32[32,128]{1,0:T(8,128)S(1)} collective-permute-done((f32[32,128]{1,0:T(8,128)S(1)}, f32[32,128]{1,0:T(8,128)S(1)}, u32[]{:S(2)}, u32[]{:S(2)}) %collective-permute-start) | collective-permute-done | bytes 16416 | tf_op jit(solution)/shard_map/ppermute | solution.py:888
  10.6 2.7 %first_step.1 = (f32[56,128]{1,0:T(8,128)S(1)}, f32[32,128]{1,0:T(8,128)S(1)}, f32[8,128]{1,0:T(8,128)S(1)}, f32[32,2,4,128]{3,2,1,0:T(4,128)S(1)}) custom-call(s32[4]{0:T(128)S(1)} %pad_add_fusion.flags_ref, f32[32,128]{1,0:T(8,128)S(1)} %collective-permute-done.got_a_ref, f32[32,128]{1,0:T(8,128)S(1)} %collective-permute-done.1.got_b_ref, ...), custom_call_target="tpu_custom_call" | custom-call | tf_op jit(solution)/shard_map/first_step/pallas_call | solution.py:760
  13.3 14.1 %all_to_all.16.shares_ref = f32[32,2,4,128]{3,2,1,0:T(4,128)S(1)} all-to-all(f32[32,2,4,128]{3,2,1,0:T(4,128)S(1)} %get-tuple-element.45), channel_id=1, replica_groups=mesh['grp'=2,'dom'=16] {'grp','dom'}, dimensions={0} | all-to-all | bytes 262144 | tf_op jit(solution)/shard_map/all_to_all | solution.py:897
  27.5 4.8 %second_step.1 = (f32[56,128]{1,0:T(8,128)}, f32[32,128]{1,0:T(8,128)S(1)}, f32[32,3,4,128]{3,2,1,0:T(4,128)}) custom-call(s32[4]{0:T(128)S(1)} %pad_add_fusion.flags_ref, f32[32,128]{1,0:T(8,128)S(1)} %collective-permute-done.got_a_ref, f32[32,128]{1,0:T(8,128)S(1)} %collective-permute-done.1.got_b_ref, f32[32,2,4,128]{3,2,1,0:T(4,128)S(1)} %all_to_all.16.shares_ref, ...), custom_call_target="tpu_custom_call" | custom-call | tf_op jit(solution)/shard_map/second_step/pallas_call | solution.py:760
  32.3 2.6 %all-to-all-start.1 = ((f32[32,3,4,128]{3,2,1,0:T(4,128)}), f32[32,3,4,128]{3,2,1,0:T(4,128)S(1)}, u32[]{:S(2)}, u32[]{:S(2)}) async-start(f32[32,3,4,128]{3,2,1,0:T(4,128)} %get-tuple-element.54), calls=%async_computation.1 | async-start | bytes 393216 | tf_op jit(solution)/shard_map/all_to_all | solution.py:913
  34.9 5.7 %phases.1 = (bf16[2,512,1024]{2,1,0:T(8,128)(2,1)S(1)}, f32[32,8,128]{2,1,0:T(8,128)S(1)}, bf16[2048,1024]{1,0:T(8,128)(2,1)}) custom-call(s32[4]{0:T(128)S(1)} %pad_add_fusion.flags_ref, f32[32,128]{1,0:T(8,128)S(1)} %collective-permute-done.got_a_ref, f32[32,128]{1,0:T(8,128)S(1)} %collective-permute-done.1.got_b_ref, ...), custom_call_target="tpu_custom_call" | custom-call | tf_op jit(solution)/shard_map/phases/pallas_call | solution.py:760
  40.6 3.2 %all-to-all-done.1.share_ref = f32[32,3,4,128]{3,2,1,0:T(4,128)S(1)} async-done(((f32[32,3,4,128]{3,2,1,0:T(4,128)}), f32[32,3,4,128]{3,2,1,0:T(4,128)S(1)}, u32[]{:S(2)}, u32[]{:S(2)}) %all-to-all-start.1) | async-done | bytes 196640 | tf_op jit(solution)/shard_map/all_to_all | solution.py:913
  43.7 3.4 %far.1 = (f32[1,512]{1,0:T(1,128)S(1)}, f32[32,128]{1,0:T(8,128)}) custom-call(s32[4]{0:T(128)S(1)} %pad_add_fusion.flags_ref, f32[32,128]{1,0:T(8,128)S(1)} %collective-permute-done.got_a_ref, f32[32,128]{1,0:T(8,128)S(1)} %collective-permute-done.1.got_b_ref, f32[32,3,4,128]{3,2,1,0:T(4,128)S(1)} %all-to-all-done.1.share_ref, ...), custom_call_target="tpu_custom_call" | custom-call | tf_op jit(solution)/shard_map/far/pallas_call | solution.py:760
  47.2 9.9 %all_to_all.17 = f32[16,1,512]{2,1,0:T(1,128)S(1)} all-to-all(f32[16,1,512]{2,1,0:T(1,128)S(1)} %broadcast_in_dim.2), channel_id=1, replica_groups=mesh['grp'=2,'dom'=16] {'dom'}, dimensions={0} | all-to-all | bytes 65536 | tf_op jit(solution)/shard_map/all_to_all | solution.py:955
  57.1 0.1 reduce
  57.2 0.6 %reshape.60 = f32[4,2048]{1,0:T(4,128)} reshape(f32[16,512]{1,0:T(8,128)S(1)} %reduce) | data formatting | bytes 65536 | tf_op jit(solution)/shard_map/reshape | solution.py:957
  (1 shorter events, 0.0 us)
Async XLA Ops:
  2.3 7.5 %collective-permute-start.1 = (f32[32,128]{1,0:T(8,128)S(1)}, f32[32,128]{1,0:T(8,128)S(1)}, u32[]{:S(2)}, u32[]{:S(2)}) collective-permute-start(f32[32,128]{1,0:T(8,128)S(1)} %get-tuple-element.36), channel_id=1, source_target_pairs={{1,2},{3,4},{5,6},{7,8},{9,10},{11,12},{13,14},{15,16},{17,18},{19... | collective-permute-start | bytes 49160 | tf_op jit(solution)/shard_map/ppermute | solution.py:852
  5.4 5.2 %collective-permute-start = (f32[32,128]{1,0:T(8,128)S(1)}, f32[32,128]{1,0:T(8,128)S(1)}, u32[]{:S(2)}, u32[]{:S(2)}) collective-permute-start(f32[32,128]{1,0:T(8,128)S(1)} %get-tuple-element.35), channel_id=1, source_target_pairs={{0,1},{1,0},{2,3},{3,2},{4,5},{5,4},{6,7},{7,6},{8,9},{9,8},{10,11... | collective-permute-start | bytes 49160 | tf_op jit(solution)/shard_map/ppermute | solution.py:888
  32.3 11.5 %all-to-all-start.1 = ((f32[32,3,4,128]{3,2,1,0:T(4,128)}), f32[32,3,4,128]{3,2,1,0:T(4,128)S(1)}, u32[]{:S(2)}, u32[]{:S(2)}) async-start(f32[32,3,4,128]{3,2,1,0:T(4,128)} %get-tuple-element.54), calls=%async_computation.1 | async-start | bytes 393216 | tf_op jit(solution)/shard_map/all_to_all | solution.py:913
